TPU v7x, 32 devices: a whole 2x2x4 slice. The times are simulated.
32 devices in a mesh: row: 4 (over z), col: 2 (over x), sub: 4 (over y, core).
Axes of the slice: x: 2, y: 2, z: 4, core: 2. Of those that a mesh axis runs over, the one named last changes fastest.
Arguments:
- front_entries: float32 [8192, 8192], P('row', ('col', 'sub')), may hold values from -1 to 4, as said below
- child_blocks: float32 [4, 2048, 2048], P('sub', 'row', 'col'), may hold values from -1 to 2, as said below
- child_map: int32 [4, 16], P('sub'), may hold values from 0 to 63, as said below
Outputs:
- factored: float32 [8192, 8192], P('row', ('col', 'sub'))
Inputs may be any that keep to these rules, and one draw needn't show every extreme that they name: Each row of child_map lists 16 different parent blocks in increasing order and ends with block 63. In natural order front_entries is a symmetric matrix, and the assembled front is positive definite. `child_blocks`: in natural order each child's contribution block is a symmetric matrix.
All inputs are finite; a program needn't handle non-finite values.
Results may differ from a plain program's by a relative error of at most 0.00005.
Values sent between devices are 32-bit elements; how exact they have to be, the bound alone decides.
No kernel may reach another device: no remote copies, remote signals or barrier semaphores. Data moves between devices by JAX's collectives and lax.ppermute only.
A program may use at most 192 MiB of HBM per device.

v0:
```python
import jax
import jax.numpy as jnp
from jax import lax
from jax.sharding import PartitionSpec as P

BLK = 128
NPIV = 6


highest = lax.Precision.HIGHEST


def broadcast(value, axis, source):
    kept = jnp.where(lax.axis_index(axis) == source, value, 0).astype(value.dtype)
    return lax.psum(kept, axis)


def lookup(index_table, wanted):
    positions = jnp.arange(index_table.shape[0], dtype=jnp.int32)
    return jnp.sum(jnp.where(wanted[..., None] == positions, index_table, 0), axis=-1)


def body(front_entries, child_blocks, child_map):
    row_count = lax.axis_size("row")
    col_count = lax.axis_size("col")
    sub_count = lax.axis_size("sub")
    row_index = lax.axis_index("row")
    col_index = lax.axis_index("col")
    sub_index = lax.axis_index("sub")
    child_tile = child_blocks[0]
    mapping = child_map[0]
    local_rows = front_entries.shape[0]
    row_blocks = local_rows // BLK
    slot_count = front_entries.shape[1] // BLK
    col_blocks = slot_count * sub_count
    child_rows = child_tile.shape[0] // BLK
    child_cols = child_tile.shape[1] // BLK
    zero_carry = jnp.zeros((row_blocks, BLK, col_blocks, BLK), jnp.float32)
    incoming = lax.all_gather(child_tile[None], ("row", "col"), axis=0, tiled=True)
    piece_count = incoming.shape[0]
    source = jnp.arange(piece_count, dtype=jnp.int32)
    source_row = source // col_count
    source_col = source % col_count
    row_parent = lookup(
        mapping, jnp.arange(child_rows, dtype=jnp.int32)[None, :] * row_count + source_row[:, None]
    )
    col_parent = lookup(
        mapping, jnp.arange(child_cols, dtype=jnp.int32)[None, :] * col_count + source_col[:, None]
    )
    row_target = jnp.where(row_parent % row_count == row_index, row_parent // row_count, row_blocks)
    col_target = jnp.where(col_parent % col_count == col_index, col_parent // col_count, col_blocks)
    tile_stack = incoming.reshape(piece_count, child_rows, BLK, child_cols, BLK).transpose(
        0, 1, 3, 2, 4
    )
    spread_sum = zero_carry.at[row_target[:, :, None], :, col_target[:, None, :], :].add(
        tile_stack, mode="drop"
    )
    spread_sum = spread_sum.reshape(local_rows, col_blocks * BLK)
    summed = lax.psum_scatter(spread_sum, "sub", scatter_dimension=1, tiled=True)
    matrix = front_entries + summed
    row_global = jnp.repeat(jnp.arange(row_blocks, dtype=jnp.int32) * row_count + row_index, BLK)
    col_global = jnp.repeat(
        (sub_index * slot_count + jnp.arange(slot_count, dtype=jnp.int32)) * col_count + col_index,
        BLK,
    )
    col_slot = 0 // col_count % slot_count
    pivot_block = 0 // row_count
    col_source = matrix[:, col_slot * BLK : (col_slot + 1) * BLK]
    row_source = matrix[pivot_block * BLK : (pivot_block + 1) * BLK, :]
    for pivot_step in range(NPIV):
        root_group = pivot_step % col_count * sub_count + pivot_step // col_count // slot_count
        share_col_panel = broadcast(col_source, ("col", "sub"), root_group)
        share_pivot_block = pivot_step // row_count
        share_diagonal = share_col_panel[share_pivot_block * BLK : (share_pivot_block + 1) * BLK, :]
        share_pivot_row_panel, share_diagonal = (
            broadcast(row_source, "row", pivot_step % row_count),
            broadcast(share_diagonal, "row", pivot_step % row_count),
        )
        pivot_factor = jnp.linalg.cholesky(share_diagonal)
        lower_rows = jax.scipy.linalg.solve_triangular(
            pivot_factor, share_col_panel.T, lower=True
        ).T
        upper_rows = jax.scipy.linalg.solve_triangular(
            pivot_factor, share_pivot_row_panel, lower=True
        )
        left_factor = jnp.where(row_global[:, None] > pivot_step, lower_rows, 0.0)
        right_factor = jnp.where(col_global[None, :] > pivot_step, upper_rows, 0.0)
        factor_column = jnp.where(row_global[:, None] >= pivot_step, lower_rows, 0.0)
        left_factor, right_factor, column = (left_factor, right_factor, factor_column)
        if pivot_step + 1 < NPIV:
            next_slot = (pivot_step + 1) // col_count % slot_count
            next_block = (pivot_step + 1) // row_count
            col_source = matrix[:, next_slot * BLK : (next_slot + 1) * BLK] - jnp.dot(
                left_factor,
                right_factor[:, next_slot * BLK : (next_slot + 1) * BLK],
                precision=highest,
            )
            row_source = matrix[next_block * BLK : (next_block + 1) * BLK, :] - jnp.dot(
                left_factor[next_block * BLK : (next_block + 1) * BLK, :],
                right_factor,
                precision=highest,
            )
        matrix = matrix - jnp.dot(left_factor, right_factor, precision=highest)
        record_col_slot = pivot_step // col_count % slot_count
        is_owner = (col_index == pivot_step % col_count) & (
            sub_index == pivot_step // col_count // slot_count
        )
        existing = matrix[:, record_col_slot * BLK : (record_col_slot + 1) * BLK]
        matrix = matrix.at[:, record_col_slot * BLK : (record_col_slot + 1) * BLK].set(
            jnp.where(is_owner, column, existing)
        )
    upper_right = (row_global[:, None] < NPIV) & (col_global[None, :] >= NPIV)
    return jnp.where(upper_right, 0.0, matrix)


def solution(mesh):
    placed = (P("row", ("col", "sub")), P("sub", "row", "col"), P("sub", None))
    return jax.shard_map(
        body, mesh=mesh, in_specs=placed, out_specs=P("row", ("col", "sub")), check_vma=False
    )
```

profile of v0, /device:TPU:0, one launch (start us, length us, event | category | flops | bytes accessed | tf_op | source)
XLA Modules:
  0.0 1426.0 jit_solution(7147885986814681749)
XLA Ops:
  9.7 230.1 %all-gather.2.cloned.1.call-done = f32[8,512,1024]{2,1,0:T(8,128)} async-done(((f32[1,512,1024]{2,1,0:T(8,128)}), f32[8,512,1024]{2,1,0:T(8,128)}) %all-gather.2.cloned.1.call-update) | async-done | bytes 16777232 | tf_op jit(solution)/shard_map/all_gather | solution.py:39
  239.8 9.4 copy.144
  249.2 6.7 copy.90
  256.0 11.2 broadcast_in_dim.242
  267.2 50.7 %scatter_fusion = f32[16,128,32,128]{3,1,2,0:T(8,128)} fusion(f32[16,128,32,128]{3,1,2,0:T(8,128)} %broadcast_in_dim.242, s32[256]{0:T(256)S(1)} %reshape.473, f32[256,128,128]{2,1,0:T(8,128)} %bitcast.194), kind=kCustom, calls=%fused_computation | custom fusion | flops 4194304 | bytes 50333696 | tf_op jit(solution)/shard_map/scatter-add | solution.py:55
  317.9 33.4 %copy.91 = f32[16,128,32,128]{1,0,3,2:T(8,128)} copy(f32[16,128,32,128]{3,1,2,0:T(8,128)} %scatter_fusion) | data formatting | bytes 67108864 | tf_op jit(solution)/shard_map/scatter-add | solution.py:55
  351.3 29.9 %copy.147 = f32[512,8,16,128]{3,1,2,0:T(8,128)} copy(f32[512,8,16,128]{3,2,1,0:T(8,128)} %bitcast.193) | data formatting | bytes 67108864
  381.4 9.4 copy.92
  392.1 223.5 %reduce-scatter.2.cloned.1.call-done = f32[2048,1024]{0,1:T(8,128)} async-done(((f32[2048,4096]{0,1:T(8,128)}), f32[2048,1024]{0,1:T(8,128)}) %reduce-scatter.2.cloned.1.call-update) | async-done | bytes 8388624 | tf_op jit(solution)/shard_map/reduce_scatter | solution.py:59
  615.6 11.9 add.203
  627.5 2.4 slice_select_fusion
  630.0 1.9 slice_select_fusion.1
  631.9 54.7 %all-reduce.19.cloned.1.call-done = f32[2048,128]{0,1:T(8,128)} async-done(((f32[2048,128]{0,1:T(8,128)}), f32[2048,128]{0,1:T(8,128)}) %all-reduce.19.cloned.1.call-update) | async-done | bytes 1048592 | tf_op jit(solution)/shard_map/psum | solution.py:15
  690.6 37.0 %all-reduce.41.cloned.1.call-done = (f32[128,1024]{0,1:T(8,128)}, f32[128,128]{0,1:T(8,128)}) async-done(((f32[128,1024]{0,1:T(8,128)}, f32[128,128]{0,1:T(8,128)}), (f32[128,1024]{0,1:T(8,128)}, f32[128,128]{0,1:T(8,128)})) %all-reduce.41.cloned.1.call-update) | async-done | bytes 589840 | tf_op jit(solution)/shard_map/psum | solution.py:15
  729.4 11.7 cholesky.104
  742.4 9.8 custom-call.20
  753.9 2.3 fusion.26
  756.1 3.4 fusion.4
  759.7 2.4 fusion.9
  762.1 53.5 %all-reduce.21.cloned.1.call-done = f32[2048,128]{0,1:T(8,128)} async-done(((f32[2048,128]{0,1:T(8,128)}), f32[2048,128]{0,1:T(8,128)}) %all-reduce.21.cloned.1.call-update) | async-done | bytes 1048592 | tf_op jit(solution)/shard_map/psum | solution.py:15
  817.6 11.0 convolution_subtract_fusion.5
  828.5 2.9 fusion.10
  831.4 25.2 %all-reduce.39.cloned.1.call-done = (f32[128,1024]{0,1:T(8,128)}, f32[128,128]{0,1:T(8,128)}) async-done(((f32[128,1024]{0,1:T(8,128)}, f32[128,128]{0,1:T(8,128)}), (f32[128,1024]{0,1:T(8,128)}, f32[128,128]{0,1:T(8,128)})) %all-reduce.39.cloned.1.call-update) | async-done | bytes 589840 | tf_op jit(solution)/shard_map/psum | solution.py:15
  858.4 11.7 cholesky.115
  871.4 9.8 custom-call.22
  883.9 3.4 fusion.3
  887.5 2.4 fusion.8
  889.9 53.6 %all-reduce.23.cloned.1.call-done = f32[2048,128]{0,1:T(8,128)} async-done(((f32[2048,128]{0,1:T(8,128)}), f32[2048,128]{0,1:T(8,128)}) %all-reduce.23.cloned.1.call-update) | async-done | bytes 1048592 | tf_op jit(solution)/shard_map/psum | solution.py:15
  945.2 11.0 convolution_subtract_fusion.4
  956.2 2.9 fusion.11
  959.1 25.5 %all-reduce.37.cloned.1.call-done = (f32[128,1024]{0,1:T(8,128)}, f32[128,128]{0,1:T(8,128)}) async-done(((f32[128,1024]{0,1:T(8,128)}, f32[128,128]{0,1:T(8,128)}), (f32[128,1024]{0,1:T(8,128)}, f32[128,128]{0,1:T(8,128)})) %all-reduce.37.cloned.1.call-update) | async-done | bytes 589840 | tf_op jit(solution)/shard_map/psum | solution.py:15
  986.3 11.7 cholesky.126
  999.4 9.8 custom-call.24
  1009.2 1.6 convolution_select_fusion.3
  1011.9 3.4 fusion.2
  1015.7 2.4 fusion.7
  1018.1 53.3 %all-reduce.25.cloned.1.call-done = f32[2048,128]{0,1:T(8,128)} async-done(((f32[2048,128]{0,1:T(8,128)}), f32[2048,128]{0,1:T(8,128)}) %all-reduce.25.cloned.1.call-update) | async-done | bytes 1048592 | tf_op jit(solution)/shard_map/psum | solution.py:15
  1072.9 11.0 convolution_subtract_fusion.3
  1084.0 3.0 fusion.12
  1086.9 25.4 %all-reduce.35.cloned.1.call-done = (f32[128,1024]{0,1:T(8,128)}, f32[128,128]{0,1:T(8,128)}) async-done(((f32[128,1024]{0,1:T(8,128)}, f32[128,128]{0,1:T(8,128)}), (f32[128,1024]{0,1:T(8,128)}, f32[128,128]{0,1:T(8,128)})) %all-reduce.35.cloned.1.call-update) | async-done | bytes 589840 | tf_op jit(solution)/shard_map/psum | solution.py:15
  1114.1 11.7 cholesky.137
  1127.1 9.8 custom-call.26
  1136.9 1.6 convolution_select_fusion.2
  1139.6 3.4 fusion.1
  1143.6 2.4 fusion.6
  1146.0 53.2 %all-reduce.27.cloned.1.call-done = f32[2048,128]{0,1:T(8,128)} async-done(((f32[2048,128]{0,1:T(8,128)}), f32[2048,128]{0,1:T(8,128)}) %all-reduce.27.cloned.1.call-update) | async-done | bytes 1048592 | tf_op jit(solution)/shard_map/psum | solution.py:15
  1200.7 11.0 convolution_subtract_fusion.2
  1211.8 3.0 fusion.13
  1214.7 25.4 %all-reduce.33.cloned.1.call-done = (f32[128,1024]{0,1:T(8,128)}, f32[128,128]{0,1:T(8,128)}) async-done(((f32[128,1024]{0,1:T(8,128)}, f32[128,128]{0,1:T(8,128)}), (f32[128,1024]{0,1:T(8,128)}, f32[128,128]{0,1:T(8,128)})) %all-reduce.33.cloned.1.call-update) | async-done | bytes 589840 | tf_op jit(solution)/shard_map/psum | solution.py:15
  1242.0 11.7 cholesky.148
  1255.0 9.8 custom-call.28
  1264.8 1.6 convolution_select_fusion.1
  1267.5 3.4 fusion
  1271.2 2.4 fusion.5
  1273.6 53.3 %all-reduce.29.cloned.1.call-done = f32[2048,128]{0,1:T(8,128)} async-done(((f32[2048,128]{0,1:T(8,128)}), f32[2048,128]{0,1:T(8,128)}) %all-reduce.29.cloned.1.call-update) | async-done | bytes 1048592 | tf_op jit(solution)/shard_map/psum | solution.py:15
  1328.5 11.0 convolution_subtract_fusion.1
  1339.5 2.9 fusion.14
  1342.5 25.5 %all-reduce.31.cloned.1.call-done = (f32[128,1024]{0,1:T(8,128)}, f32[128,128]{0,1:T(8,128)}) async-done(((f32[128,1024]{0,1:T(8,128)}, f32[128,128]{0,1:T(8,128)}), (f32[128,1024]{0,1:T(8,128)}, f32[128,128]{0,1:T(8,128)})) %all-reduce.31.cloned.1.call-update) | async-done | bytes 589840 | tf_op jit(solution)/shard_map/psum | solution.py:15
  1369.8 11.7 cholesky.159
  1382.8 9.8 custom-call.30
  1392.6 1.6 convolution_select_fusion
  1395.3 9.7 convolution_subtract_fusion
  1405.8 4.1 and_select_fusion
  1410.0 9.2 copy.121
  (139 shorter events, 46.1 us)
Async XLA Ops:
  6.5 233.3 %all-gather.2.cloned.1.call-start = ((), (), s32[]{:S(2)}) async-start(), calls=%async_computation.1 | async-start | bytes 18874368 | tf_op jit(solution)/shard_map/all_gather | solution.py:39
  7.3 608.3 %reduce-scatter.2.cloned.1.call-start = ((), (), s32[]{:S(2)}) async-start(), calls=%async_computation.2 | async-start | bytes 41943040 | tf_op jit(solution)/shard_map/reduce_scatter | solution.py:59
  381.3 305.3 %all-reduce.19.cloned.1.call-start = ((), (), s32[]{:S(2)}) async-start(), calls=%async_computation.3 | async-start | bytes 2097152 | tf_op jit(solution)/shard_map/psum | solution.py:15
  629.8 97.7 %all-reduce.41.cloned.1.call-start = ((), (), s32[]{:S(2)}) async-start(), calls=%async_computation.14 | async-start | bytes 1179648 | tf_op jit(solution)/shard_map/psum | solution.py:15
  688.1 127.5 %all-reduce.21.cloned.1.call-start = ((), (), s32[]{:S(2)}) async-start(), calls=%async_computation.4 | async-start | bytes 2097152 | tf_op jit(solution)/shard_map/psum | solution.py:15
  759.5 97.1 %all-reduce.39.cloned.1.call-start = ((), (), s32[]{:S(2)}) async-start(), calls=%async_computation.13 | async-start | bytes 1179648 | tf_op jit(solution)/shard_map/psum | solution.py:15
  817.1 65.8 %copy-start.3 = (f32[2048,128]{0,1:T(8,128)S(1)}, f32[2048,128]{0,1:T(8,128)}, u32[]{:S(2)}) copy-start(f32[2048,128]{0,1:T(8,128)} %all-reduce.21.cloned.1.call-done) | copy-start | bytes 3145732
  817.1 126.3 %all-reduce.23.cloned.1.call-start = ((), (), s32[]{:S(2)}) async-start(), calls=%async_computation.5 | async-start | bytes 2097152 | tf_op jit(solution)/shard_map/psum | solution.py:15
  887.3 97.2 %all-reduce.37.cloned.1.call-start = ((), (), s32[]{:S(2)}) async-start(), calls=%async_computation.12 | async-start | bytes 1179648 | tf_op jit(solution)/shard_map/psum | solution.py:15
  944.9 65.9 %copy-start = (f32[2048,128]{0,1:T(8,128)S(1)}, f32[2048,128]{0,1:T(8,128)}, u32[]{:S(2)}) copy-start(f32[2048,128]{0,1:T(8,128)} %all-reduce.23.cloned.1.call-done) | copy-start | bytes 3145732
  945.0 126.4 %all-reduce.25.cloned.1.call-start = ((), (), s32[]{:S(2)}) async-start(), calls=%async_computation.6 | async-start | bytes 2097152 | tf_op jit(solution)/shard_map/psum | solution.py:15
  1015.3 97.0 %all-reduce.35.cloned.1.call-start = ((), (), s32[]{:S(2)}) async-start(), calls=%async_computation.11 | async-start | bytes 1179648 | tf_op jit(solution)/shard_map/psum | solution.py:15
  1072.9 65.7 %copy-start.2 = (f32[2048,128]{0,1:T(8,128)S(1)}, f32[2048,128]{0,1:T(8,128)}, u32[]{:S(2)}) copy-start(f32[2048,128]{0,1:T(8,128)} %all-reduce.25.cloned.1.call-done) | copy-start | bytes 3145732
  1072.9 126.3 %all-reduce.27.cloned.1.call-start = ((), (), s32[]{:S(2)}) async-start(), calls=%async_computation.7 | async-start | bytes 2097152 | tf_op jit(solution)/shard_map/psum | solution.py:15
  1143.0 97.1 %all-reduce.33.cloned.1.call-start = ((), (), s32[]{:S(2)}) async-start(), calls=%async_computation.10 | async-start | bytes 1179648 | tf_op jit(solution)/shard_map/psum | solution.py:15
  1200.7 65.8 %copy-start.1 = (f32[2048,128]{0,1:T(8,128)S(1)}, f32[2048,128]{0,1:T(8,128)}, u32[]{:S(2)}) copy-start(f32[2048,128]{0,1:T(8,128)} %all-reduce.27.cloned.1.call-done) | copy-start | bytes 3145732
  1200.7 126.3 %all-reduce.29.cloned.1.call-start = ((), (), s32[]{:S(2)}) async-start(), calls=%async_computation.8 | async-start | bytes 2097152 | tf_op jit(solution)/shard_map/psum | solution.py:15
  1270.9 97.1 %all-reduce.31.cloned.1.call-start = ((), (), s32[]{:S(2)}) async-start(), calls=%async_computation.9 | async-start | bytes 1179648 | tf_op jit(solution)/shard_map/psum | solution.py:15
  1328.5 65.8 %copy-start.4 = (f32[2048,128]{0,1:T(8,128)S(1)}, f32[2048,128]{0,1:T(8,128)}, u32[]{:S(2)}) copy-start(f32[2048,128]{0,1:T(8,128)} %all-reduce.29.cloned.1.call-done) | copy-start | bytes 3145732
Sparse Core Ops, SparseCore 0:
  9.5 230.3 all-gather.1
  381.4 234.1 reduce-scatter.1
  630.0 56.5 all-reduce.18
  688.9 38.6 all-reduce.40
  759.7 55.9 all-reduce.20
  817.9 38.6 all-reduce.38
  887.5 55.9 all-reduce.22
  945.9 38.6 all-reduce.36
  1015.4 55.9 all-reduce.24
  1073.6 38.6 all-reduce.34
  1143.2 55.9 all-reduce.26
  1201.4 38.6 all-reduce.32
  1271.0 55.9 all-reduce.28
  1329.3 38.6 all-reduce.30
where the time goes:
time: 1440 us; the launch traced here: 1430 us
  waiting for transfers between devices  940 us (65%)
  other arithmetic  242 us (17%)
  local copies, waits for them, and re-layouts  117 us (8%)
  matrix products  111 us (8%)
    psum x12, waiting for transfers between devices, broadcast(): return lax.psum(kept, axis)  486 us
    all_gather x1, waiting for transfers between devices, body(): lax.all_gather(child_tile[None], ('row', 'col'), axis=0, tiled=True)  230 us
    reduce_scatter x1, waiting for transfers between devices, body(): lax.psum_scatter(spread_sum, 'sub', scatter_dimension=1, tiled=True)  224 us
    another operation x18, other arithmetic, body(): pivot_factor = jnp.linalg.cholesky(share_diagonal)  74.5 us
    dot_general x6, matrix products, body(): matrix = matrix - jnp.dot(left_factor, right_factor, precision=highest)  64.8 us
    another operation x12, other arithmetic, body(): jax.scipy.linalg.solve_triangular(pivot_factor, share_col_panel.T, lower=...  62.5 us
    scatter-add x1, other arithmetic, body(): zero_carry.at[row_target[:, :, None], :, col_target[:, None, :], :]  50.7 us
    unnamed x13, local copies, waits for them, and re-layouts  48.8 us
  transfers between devices with their start and end apart: 14, of which 14 were waited for; matrix products, arithmetic and copies ran while one was open for 7% of the time, Pallas kernels for 0%

commit v1 on v0

v1 whole, which is shorter than its diff:
```python
import functools

import jax
import jax.numpy as jnp
from jax import lax
from jax.experimental import pallas as pl
from jax.experimental.pallas import tpu as pltpu
from jax.sharding import PartitionSpec as P

BLK = 128
NPIV = 6
PLANE = ("col", "sub")
VMEM_BYTES = 60 * 1024 * 1024

highest = lax.Precision.HIGHEST


def quot(value, number):
    if number & (number - 1) == 0:
        return lax.shift_right_logical(value, jnp.int32(number.bit_length() - 1))
    return lax.div(value, jnp.int32(number))


def rem(value, number):
    if number & (number - 1) == 0:
        return value & (number - 1)
    return lax.rem(value, jnp.int32(number))


def whole(memory):
    return pl.BlockSpec(memory_space=memory)


def params(**more):
    return pltpu.CompilerParams(vmem_limit_bytes=VMEM_BYTES, **more)


class Plan:
    def __init__(self, front_shape, child_shape):
        self.rows = lax.axis_size("row")
        self.cols = lax.axis_size("col")
        self.subs = lax.axis_size("sub")
        self.plane = self.cols * self.subs
        self.part = BLK // self.plane
        self.row_blocks = front_shape[0] // BLK
        self.slots = front_shape[1] // BLK
        self.child_rows = child_shape[1] // BLK
        self.child_cols = child_shape[2] // BLK
        self.order = self.child_rows * self.rows
        self.lead_cols = -(-NPIV // self.cols)
        self.lead_rows = -(-NPIV // self.rows)
        reach = [
            min((self.rows * t + self.rows - 1) // self.cols + 1, self.child_cols)
            for t in range(self.child_rows)
        ]
        first = [(t, u) for t in range(self.child_rows) for u in range(min(reach[t], self.lead_cols))]
        second = [(t, u) for t in range(self.child_rows) for u in range(self.lead_cols, reach[t])]
        self.first = len(first)
        self.second = len(second)
        self.blocks = first + second
        self.first_start = [first.index((t, 0)) for t in range(self.child_rows)]
        self.second_start = [
            sum(1 for b in second if b[0] < t) for t in range(self.child_rows)
        ]

    def dest(self, block):
        high = quot(block, self.cols)
        return rem(block, self.cols), quot(high, self.slots), rem(high, self.slots)

    def offset(self, starts, t):
        out = jnp.int32(starts[0])
        for step in range(1, len(starts)):
            out = jnp.where(t == step, jnp.int32(starts[step]), out)
        return out


def take_rows(ref, lead, base, index, part, lanes):
    if part % 8 == 0:
        return ref[(*lead, pl.ds(pl.multiple_of(base + index * part, part), part), lanes)]
    share = 8 // part
    group = ref[(*lead, pl.ds(pl.multiple_of(base + quot(index, share) * 8, 8), 8), lanes)]
    out = group[:part]
    for step in range(1, share):
        out = jnp.where(rem(index, share) == step, group[step * part : (step + 1) * part], out)
    return out


def put_rows(ref, base, index, lanes, value):
    part = value.shape[0]
    if part % 8 == 0:
        ref[pl.ds(pl.multiple_of(base + index * part, part), part), lanes] = value
        return
    share = 8 // part
    rows = pl.ds(pl.multiple_of(base + quot(index, share) * 8, 8), 8)
    spot = lax.broadcasted_iota(jnp.int32, (8, value.shape[1]), 0)
    mine = quot(spot, part) == rem(index, share)
    ref[rows, lanes] = jnp.where(mine, jnp.concatenate([value] * share, axis=0), ref[rows, lanes])


def block_lanes(number):
    return slice(number * BLK, (number + 1) * BLK)


def cut_child_kernel(plan, place_ref, tile_ref, *out_refs):
    me = place_ref[0]
    for m, out_ref in enumerate(out_refs):
        for b, (t, u) in enumerate(plan.blocks):
            out_ref[b] = take_rows(tile_ref, (0,), t * BLK, me ^ m, plan.part, block_lanes(u))


def cut_front_kernel(plan, place_ref, front_ref, *out_refs):
    me = place_ref[0]

    @pl.loop(0, plan.row_blocks)
    def _(t):
        for m, out_ref in enumerate(out_refs):
            for u in range(plan.lead_cols):
                out_ref[t, u] = take_rows(front_ref, (), t * BLK, me ^ m, plan.part, block_lanes(u))


def front_panel_kernel(plan, place_ref, *refs):
    pieces = refs[: plan.plane]
    panel_ref, lead_ref = refs[plan.plane :]
    col, sub = place_ref[2], place_ref[3]
    panel_ref[...] = jnp.zeros_like(panel_ref)
    for mc in range(plan.cols):
        for u in range(plan.lead_cols):
            pivot = plan.cols * u + (col ^ mc)

            @pl.when(pivot < NPIV)
            def _():
                @pl.loop(0, plan.row_blocks)
                def _(t):
                    total = jnp.zeros((plan.part, BLK), jnp.float32)
                    for ms in range(plan.subs):
                        piece = pieces[mc * plan.subs + ms][t, u]
                        if mc == 0 and ms == 0:
                            piece = jnp.where(sub == 0, piece, 0.0)
                        total = total + piece
                    panel_ref[t, pivot] = total

    lead_ref[...] = panel_ref[: plan.lead_rows]


def panel_kernel(plan, place_ref, maps_ref, *refs):
    rows = plan.rows
    ring = refs[:rows]
    leads = refs[rows : 2 * rows]
    front_ref = refs[2 * rows]
    panel_ref, corner_ref = refs[2 * rows + 1 : 2 * rows + 3]
    outs = refs[2 * rows + 3 : 2 * rows + 3 + plan.plane]
    held, across, sems = refs[2 * rows + 3 + plan.plane :]
    row, col, sub = place_ref[1], place_ref[2], place_ref[3]
    copies = [
        pltpu.make_async_copy(ring[h], held.at[h], sems.at[h]) for h in range(rows)
    ]
    for copy in copies:
        copy.start()
    panel_ref[...] = front_ref[...]
    corner_ref[...] = jnp.zeros_like(corner_ref)
    for h in range(rows):
        for q in range(plan.lead_rows):
            block = rows * q + rem(row - h + rows, rows)

            @pl.when(block < NPIV)
            def _():
                corner_ref[block] = leads[h][q]

    across[...] = jnp.zeros_like(across)
    for copy in copies:
        copy.wait()

    def place(block):
        block_col, block_sub, slot = plan.dest(block)
        return (block_col ^ col) * plan.subs + (block_sub ^ sub), slot

    @pl.loop(0, plan.subs)
    def _(ms):
        @pl.loop(0, min(NPIV, plan.order))
        def _(j):
            pivot = maps_ref[ms, j]

            @pl.when(pivot < NPIV)
            def _():
                u = quot(j, plan.cols)
                m = (rem(j, plan.cols) ^ col) * plan.subs + ms

                @pl.loop(j, plan.order)
                def _(i):
                    block = maps_ref[ms, i]
                    h = rem(row - rem(i, rows) + rows, rows)
                    b = plan.offset(plan.first_start, quot(i, rows)) + u

                    @pl.when(rem(block, rows) == row)
                    def _():
                        panel_ref[quot(block, rows), pivot] += held[h, m, b]

                    @pl.when(block < NPIV)
                    def _():
                        corner_ref[block, pivot] += held[h, m, b]

                    @pl.when(rem(pivot, rows) == row)
                    def _():
                        target, slot = place(block)
                        across[target, quot(pivot, rows), slot] += held[h, m, b]

                    @pl.when((block < NPIV) & (block != pivot) & (rem(block, rows) == row))
                    def _():
                        target, slot = place(pivot)
                        across[target, quot(block, rows), slot] += held[h, m, b]

    for m in range(plan.plane):
        outs[m][...] = across[m]


def spread_kernel(plan, place_ref, maps_ref, *refs):
    rows = plan.rows
    ring_first = refs[:rows]
    ring_second = refs[rows : 2 * rows]
    outs = refs[2 * rows : 2 * rows + plan.plane]
    held, total, sems, out_sems = refs[2 * rows + plan.plane :]
    row, col, sub = place_ref[1], place_ref[2], place_ref[3]
    copies = []
    for h in range(rows):
        copies.append(
            pltpu.make_async_copy(
                ring_first[h], held.at[h, :, pl.ds(0, plan.first)], sems.at[h]
            )
        )
        copies.append(
            pltpu.make_async_copy(
                ring_second[h], held.at[h, :, pl.ds(plan.first, plan.second)], sems.at[rows + h]
            )
        )
    for copy in copies:
        copy.start()

    @pl.loop(0, plan.row_blocks)
    def _(t):
        for m in range(plan.plane):
            total[m, t] = jnp.zeros((plan.slots, plan.part, BLK), jnp.float32)

    for copy in copies:
        copy.wait()

    @pl.loop(0, plan.subs)
    def _(ms):
        @pl.loop(0, plan.order)
        def _(i):
            block_row = maps_ref[ms, i]

            @pl.when((rem(block_row, rows) == row) & (block_row >= NPIV))
            def _():
                @pl.loop(0, plan.order)
                def _(j):
                    block_col, block_sub, slot = plan.dest(maps_ref[ms, j])
                    high = jnp.maximum(i, j)
                    low = jnp.minimum(i, j)
                    h = rem(row - rem(high, rows) + rows, rows)
                    t = quot(high, rows)
                    u = quot(low, plan.cols)
                    m = (rem(low, plan.cols) ^ col) * plan.subs + ms
                    b = jnp.where(
                        u < plan.lead_cols,
                        plan.offset(plan.first_start, t) + u,
                        plan.first + plan.offset(plan.second_start, t) + u - plan.lead_cols,
                    )
                    target = (block_col ^ col) * plan.subs + (block_sub ^ sub)
                    total[target, quot(block_row, rows), slot] += held[h, m, b]

    out_copies = [
        pltpu.make_async_copy(total.at[m], outs[m], out_sems.at[m]) for m in range(plan.plane)
    ]
    for copy in out_copies:
        copy.start()
    for copy in out_copies:
        copy.wait()


def join_parts(plan, me, parts, block, column, scratch):
    for m, part in enumerate(parts):
        put_rows(scratch, 0, me ^ m, slice(None), part)
    joined = scratch[...]
    return jnp.where(column > block, joined.T, joined)


def lead_rows_kernel(plan, place_ref, front_ref, *refs):
    parts = refs[: plan.plane]
    out_ref, scratch = refs[plan.plane :]
    me, row, col, sub = place_ref[0], place_ref[1], place_ref[2], place_ref[3]
    for q in range(plan.lead_rows):
        block = plan.rows * q + row
        for slot in range(plan.slots):
            column = (sub * plan.slots + slot) * plan.cols + col
            joined = join_parts(
                plan, me, [part[q, slot] for part in parts], block, column, scratch
            )
            out_ref[q, :, slot * BLK : (slot + 1) * BLK] = (
                front_ref[q * BLK : (q + 1) * BLK, slot * BLK : (slot + 1) * BLK] + joined
            )


def corner_kernel(plan, place_ref, *refs):
    parts = refs[: plan.plane]
    out_ref = refs[plan.plane]
    me = place_ref[0]
    for m, part in enumerate(parts):
        for block in range(NPIV):
            for pivot in range(NPIV):
                put_rows(out_ref, block * BLK, me ^ m, block_lanes(pivot), part[block, pivot])


def halves(value):
    high = value.astype(jnp.bfloat16)
    return high, (value - high.astype(jnp.float32)).astype(jnp.bfloat16)


def right_kernel(plan, place_ref, inverse_ref, *refs):
    leads = refs[: plan.rows]
    high_ref, low_ref, stack = refs[plan.rows :]
    row = place_ref[1]
    for h in range(plan.rows):
        for q in range(plan.lead_rows):
            block = plan.rows * q + rem(row - h + plan.rows, plan.rows)

            @pl.when(block < NPIV)
            def _():
                stack[pl.ds(pl.multiple_of(block * BLK, BLK), BLK), :] = leads[h][q]

    for pivot in range(NPIV):
        depth = (pivot + 1) * BLK
        value = jnp.dot(
            inverse_ref[pivot * BLK : depth, :depth], stack[:depth, :],
            precision=highest, preferred_element_type=jnp.float32,
        )
        high, low = halves(value)
        high_ref[pivot * BLK : depth, :] = high
        low_ref[pivot * BLK : depth, :] = low


def left_kernel(plan, tile_blocks, half_steps, place_ref, inverse_ref, factor_ref, *refs):
    count = plan.plane
    first, second = refs[:count], refs[count : 2 * count]
    high_ref, low_ref, own_ref, panel, value_ref = refs[2 * count :]
    me, row, col = place_ref[0], place_ref[1], place_ref[2]
    step = pl.program_id(0)

    def load(parts):
        for t in range(tile_blocks):
            for m in range(count):
                for pivot in range(NPIV):
                    put_rows(panel, t * BLK, me ^ m, block_lanes(pivot), parts[m][t, pivot])

    @pl.when(step < half_steps)
    def _():
        load(first)

    @pl.when(step >= half_steps)
    def _():
        load(second)

    for pivot in range(NPIV):
        depth = (pivot + 1) * BLK
        value_ref[:, pivot * BLK : depth] = lax.dot_general(
            panel[:, :depth], inverse_ref[pivot * BLK : depth, :depth],
            (((1,), (1,)), ((), ())),
            precision=highest, preferred_element_type=jnp.float32,
        )
    high, low = halves(value_ref[...])
    high_ref[...] = high
    low_ref[...] = low
    for t in range(tile_blocks):
        block = plan.rows * (step * tile_blocks + t) + row
        for u in range(plan.lead_cols):
            pivot = jnp.minimum(plan.cols * u + col, NPIV - 1)
            lanes = pl.ds(pl.multiple_of(pivot * BLK, BLK), BLK)
            here = (slice(t * BLK, (t + 1) * BLK), slice(u * BLK, (u + 1) * BLK))
            own_ref[here] = value_ref[t * BLK : (t + 1) * BLK, lanes]

            @pl.when(block < NPIV)
            def _():
                own_ref[here] = factor_ref[
                    pl.ds(pl.multiple_of(block * BLK, BLK), BLK), lanes
                ]


def schur_kernel(plan, tile_blocks, place_ref, front_ref, high_ref, low_ref, own_ref,
                 right_high_ref, right_low_ref, *refs):
    parts = refs[: plan.plane]
    out_ref, scratch = refs[plan.plane :]
    me, row, col, sub = place_ref[0], place_ref[1], place_ref[2], place_ref[3]
    step = pl.program_id(0)
    update = jnp.dot(high_ref[...], right_high_ref[...], preferred_element_type=jnp.float32)
    update += jnp.dot(high_ref[...], right_low_ref[...], preferred_element_type=jnp.float32)
    update += jnp.dot(low_ref[...], right_high_ref[...], preferred_element_type=jnp.float32)
    out_ref[...] = front_ref[...] - update
    for t in range(tile_blocks):
        block = plan.rows * (step * tile_blocks + t) + row
        for slot in range(plan.slots):
            column = (sub * plan.slots + slot) * plan.cols + col
            here = (slice(t * BLK, (t + 1) * BLK), slice(slot * BLK, (slot + 1) * BLK))
            joined = join_parts(
                plan, me, [part[t, slot] for part in parts], block, column,
                scratch.at[t, slot],
            )
            value = out_ref[here] + joined
            value = jnp.where((block < NPIV) & (column >= NPIV), 0.0, value)
            if slot < plan.lead_cols:
                value = jnp.where(column < NPIV, own_ref[here], value)
            out_ref[here] = value


def swap(value, plan, bit):
    return lax.ppermute(value, PLANE, [(k, k ^ bit) for k in range(plan.plane)])


def gather_plane(value, plan, bits):
    held = {0: value}
    for bit in bits:
        for m in sorted(held):
            held[m ^ bit] = swap(held[m], plan, bit)
    return [held[m] for m in range(plan.plane)]


def ring_gather(value, plan):
    held = [value]
    for _ in range(1, plan.rows):
        held.append(
            lax.ppermute(held[-1], "row", [(r, (r + 1) % plan.rows) for r in range(plan.rows)])
        )
    return held


def body(front_entries, child_blocks, child_map):
    plan = Plan(front_entries.shape, child_blocks.shape)
    f32 = jnp.float32
    row = lax.axis_index("row").astype(jnp.int32)
    col = lax.axis_index("col").astype(jnp.int32)
    sub = lax.axis_index("sub").astype(jnp.int32)
    place = jnp.stack([col * plan.subs + sub, row, col, sub])
    vmem, smem, hbm = whole(pltpu.VMEM), whole(pltpu.SMEM), whole(pl.ANY)
    part, plane, rows = plan.part, plan.plane, plan.rows
    every = [(0, m) for m in range(1, plane)]

    maps = [child_map[0]]
    for m in range(1, plan.subs):
        maps.append(lax.ppermute(child_map[0], "sub", [(s, s ^ m) for s in range(plan.subs)]))
    maps = jnp.stack(maps)

    cut = pl.pallas_call(
        functools.partial(cut_child_kernel, plan),
        out_shape=[jax.ShapeDtypeStruct((plan.first + plan.second, part, BLK), f32)] * plane,
        in_specs=[smem, vmem],
        out_specs=[vmem] * plane,
        compiler_params=params(),
        name="cut_child",
    )(place, child_blocks)
    got = [cut[0]] + [swap(cut[m], plan, m) for m in range(1, plane)]
    ring_first = ring_gather(jnp.stack([g[: plan.first] for g in got]), plan)
    ring_second = ring_gather(jnp.stack([g[plan.first :] for g in got]), plan)

    lead_width = plan.lead_cols * BLK
    local_rows = front_entries.shape[0]
    front_cut = pl.pallas_call(
        functools.partial(cut_front_kernel, plan),
        grid=(1,),
        out_shape=[jax.ShapeDtypeStruct((plan.row_blocks, plan.lead_cols, part, BLK), f32)] * plane,
        in_specs=[smem, pl.BlockSpec((local_rows, lead_width), lambda g: (0, 0))],
        out_specs=[vmem] * plane,
        compiler_params=params(),
        name="cut_front",
    )(place, front_entries)
    owners = [k for k in range(plane) if k % plan.subs == 0]
    front_got = [front_cut[0]] + [
        lax.ppermute(front_cut[m], PLANE, [(k, k ^ m) for k in owners]) for m in range(1, plane)
    ]
    front_panel, front_lead = pl.pallas_call(
        functools.partial(front_panel_kernel, plan),
        out_shape=[
            jax.ShapeDtypeStruct((plan.row_blocks, NPIV, part, BLK), f32),
            jax.ShapeDtypeStruct((plan.lead_rows, NPIV, part, BLK), f32),
        ],
        in_specs=[smem] + [vmem] * plane,
        out_specs=[vmem] * 2,
        compiler_params=params(),
        name="front_panel",
    )(place, *front_got)
    leads = ring_gather(front_lead, plan)

    results = pl.pallas_call(
        functools.partial(panel_kernel, plan),
        out_shape=[
            jax.ShapeDtypeStruct((plan.row_blocks, NPIV, part, BLK), f32),
            jax.ShapeDtypeStruct((NPIV, NPIV, part, BLK), f32),
        ]
        + [jax.ShapeDtypeStruct((plan.lead_rows, plan.slots, part, BLK), f32)] * plane,
        in_specs=[smem, smem] + [hbm] * rows + [vmem] * (rows + 1),
        out_specs=[vmem] * (2 + plane),
        scratch_shapes=[
            pltpu.VMEM((rows, plane, plan.first, part, BLK), f32),
            pltpu.VMEM((plane, plan.lead_rows, plan.slots, part, BLK), f32),
            pltpu.SemaphoreType.DMA((rows,)),
        ],
        compiler_params=params(),
        name="panel",
    )(place, maps, *ring_first, *leads, front_panel)
    panel, corner_part, lead_parts = results[0], results[1], results[2:]

    bits = [1 << b for b in range(plane.bit_length() - 1)][::-1]
    other = bits[1:2] + bits[:1] + bits[2:]
    corner = pl.pallas_call(
        functools.partial(corner_kernel, plan),
        out_shape=jax.ShapeDtypeStruct((NPIV * BLK, NPIV * BLK), f32),
        in_specs=[smem] + [vmem] * plane,
        out_specs=vmem,
        compiler_params=params(),
        name="corner",
    )(place, *gather_plane(corner_part, plan, bits))
    factor = jnp.tril(lax.linalg.cholesky(corner, symmetrize_input=False))
    inverse = lax.linalg.triangular_solve(
        factor, jnp.eye(NPIV * BLK, dtype=f32), left_side=True, lower=True
    )

    lead_got = [lead_parts[0]] + [swap(lead_parts[m], plan, m) for m in range(1, plane)]
    lead_rows = pl.pallas_call(
        functools.partial(lead_rows_kernel, plan),
        grid=(1,),
        out_shape=jax.ShapeDtypeStruct((plan.lead_rows, BLK, plan.slots * BLK), f32),
        in_specs=[smem, pl.BlockSpec((plan.lead_rows * BLK, plan.slots * BLK), lambda g: (0, 0))]
        + [vmem] * plane,
        out_specs=vmem,
        scratch_shapes=[pltpu.VMEM((BLK, BLK), f32)],
        compiler_params=params(),
        name="lead_rows",
    )(place, front_entries, *lead_got)
    lead_ring = ring_gather(lead_rows, plan)
    right_high, right_low = pl.pallas_call(
        functools.partial(right_kernel, plan),
        out_shape=[jax.ShapeDtypeStruct((NPIV * BLK, plan.slots * BLK), jnp.bfloat16)] * 2,
        in_specs=[smem, vmem] + [vmem] * rows,
        out_specs=[vmem] * 2,
        scratch_shapes=[pltpu.VMEM((NPIV * BLK, plan.slots * BLK), f32)],
        compiler_params=params(),
        name="right_factor",
    )(place, inverse, *lead_ring)

    half = plan.row_blocks // 2
    panel_first = gather_plane(panel[:half], plan, bits)
    panel_second = gather_plane(panel[half:], plan, other)
    tile = 2
    half_steps = half // tile
    left_high, left_low, own = pl.pallas_call(
        functools.partial(left_kernel, plan, tile, half_steps),
        grid=(2 * half_steps,),
        out_shape=[
            jax.ShapeDtypeStruct((local_rows, NPIV * BLK), jnp.bfloat16),
            jax.ShapeDtypeStruct((local_rows, NPIV * BLK), jnp.bfloat16),
            jax.ShapeDtypeStruct((local_rows, lead_width), f32),
        ],
        in_specs=[smem, vmem, vmem]
        + [
            pl.BlockSpec(
                (tile, NPIV, part, BLK), lambda g: (jnp.minimum(g, half_steps - 1), 0, 0, 0)
            )
        ]
        * plane
        + [
            pl.BlockSpec(
                (tile, NPIV, part, BLK), lambda g: (jnp.maximum(g - half_steps, 0), 0, 0, 0)
            )
        ]
        * plane,
        out_specs=[
            pl.BlockSpec((tile * BLK, NPIV * BLK), lambda g: (g, 0)),
            pl.BlockSpec((tile * BLK, NPIV * BLK), lambda g: (g, 0)),
            pl.BlockSpec((tile * BLK, lead_width), lambda g: (g, 0)),
        ],
        scratch_shapes=[
            pltpu.VMEM((tile * BLK, NPIV * BLK), f32),
            pltpu.VMEM((tile * BLK, NPIV * BLK), f32),
        ],
        compiler_params=params(),
        name="left_factor",
    )(place, inverse, factor, *panel_first, *panel_second)

    spread = pl.pallas_call(
        functools.partial(spread_kernel, plan),
        out_shape=[jax.ShapeDtypeStruct((plan.row_blocks, plan.slots, part, BLK), f32)] * plane,
        in_specs=[smem, smem] + [hbm] * (2 * rows),
        out_specs=[hbm] * plane,
        scratch_shapes=[
            pltpu.VMEM((rows, plane, plan.first + plan.second, part, BLK), f32),
            pltpu.VMEM((plane, plan.row_blocks, plan.slots, part, BLK), f32),
            pltpu.SemaphoreType.DMA((2 * rows,)),
            pltpu.SemaphoreType.DMA((plane,)),
        ],
        compiler_params=params(),
        name="spread",
    )(place, maps, *ring_first, *ring_second)
    spread_got = [spread[0]] + [swap(spread[m], plan, m) for m in range(1, plane)]

    full = lambda g: (0, 0)
    by_row = lambda g: (g, 0)
    width = plan.slots * BLK
    return pl.pallas_call(
        functools.partial(schur_kernel, plan, tile),
        grid=(plan.row_blocks // tile,),
        out_shape=jax.ShapeDtypeStruct(front_entries.shape, f32),
        in_specs=[
            smem,
            pl.BlockSpec((tile * BLK, width), by_row),
            pl.BlockSpec((tile * BLK, NPIV * BLK), by_row),
            pl.BlockSpec((tile * BLK, NPIV * BLK), by_row),
            pl.BlockSpec((tile * BLK, lead_width), by_row),
            pl.BlockSpec((NPIV * BLK, width), full),
            pl.BlockSpec((NPIV * BLK, width), full),
        ]
        + [pl.BlockSpec((tile, plan.slots, part, BLK), lambda g: (g, 0, 0, 0))] * plane,
        out_specs=pl.BlockSpec((tile * BLK, width), by_row),
        scratch_shapes=[pltpu.VMEM((tile, plan.slots, BLK, BLK), f32)],
        compiler_params=params(),
        name="schur",
    )(place, front_entries, left_high, left_low, own, right_high, right_low, *spread_got)


def solution(mesh):
    placed = (P("row", ("col", "sub")), P("sub", "row", "col"), P("sub", None))
    return jax.shard_map(
        body, mesh=mesh, in_specs=placed, out_specs=P("row", ("col", "sub")), check_vma=False
    )
```

time: 1440 us -> 572 us (0.40)
  waiting for transfers between devices: 940 us -> 152 us
  Pallas kernels: 0 us -> 89.9 us
  matrix products: 111 us -> 23.3 us
  local copies, waits for them, and re-layouts: 117 us -> 29.6 us
  starting transfers between devices: 2.12 us -> 68.4 us
  other arithmetic: 242 us -> 192 us
    psum x12 -> x0, waiting for transfers between devices: 486 us -> none  [broadcast(): return lax.psum(kept, axis)]
    all_gather x1 -> x0, waiting for transfers between devices: 230 us -> none  [body(): lax.all_gather(child_tile[None], ('row', 'col'), axis=0, tiled=True)]
    reduce_scatter x1 -> x0, waiting for transfers between devices: 224 us -> none  [body(): lax.psum_scatter(spread_sum, 'sub', scatter_dimension=1, tiled=True)]
    ppermute x0 -> x64, waiting for transfers between devices: none -> 152 us  [the longest x42 84.7 us: swap(): return lax.ppermute(value, PLANE, [(k, k ^ bit) for k in range(plan.plane)])]
    dot_general x16 -> x0, matrix products: 93.8 us -> none  [the longest x6 64.8 us: body(): matrix = matrix - jnp.dot(left_factor, right_factor, precision=highest)]
    pallas_call x0 -> x10, Pallas kernels: none -> 89.9 us  [the longest x1 24.6 us: body(): pl.pallas_call(functools.partial(left_kernel, plan, tile, half_steps), gr...]
    ppermute x0 -> x64, starting transfers between devices: none -> 68.4 us  [the longest x42 33.1 us: swap(): return lax.ppermute(value, PLANE, [(k, k ^ bit) for k in range(plan.plane)])]
    another operation x33 -> x27, other arithmetic: 139 us -> 190 us  [the longest x22 126 us: body(): factor = jnp.tril(lax.linalg.cholesky(corner, symmetrize_input=False))]
  transfers between devices with their start and end apart: 14 -> 64, of which waited for: 14 -> 21; matrix products, arithmetic and copies ran while one was open for 7% -> 43% of each run, Pallas kernels for 0% -> 12%
where the time goes in v1:
time: 572 us; the launch traced here: 561 us
  other arithmetic  192 us (34%)
  waiting for transfers between devices  152 us (27%)
  Pallas kernels  89.9 us (16%)
  starting transfers between devices  68.4 us (12%)
  local copies, waits for them, and re-layouts  29.6 us (5%)
  matrix products  23.3 us (4%)
    another operation x22, other arithmetic, body(): factor = jnp.tril(lax.linalg.cholesky(corner, symmetrize_input=False))  126 us
    ppermute x42, waiting for transfers between devices, swap(): return lax.ppermute(value, PLANE, [(k, k ^ bit) for k in range(plan.plane)])  84.7 us
    another operation x3, other arithmetic, body(): lax.linalg.triangular_solve(factor, jnp.eye(NPIV * BLK, dtype=f32), left_...  62.9 us
    ppermute x12, waiting for transfers between devices, ring_gather(): lax.ppermute(held[-1], 'row', [(r, (r + 1) % plan.rows) for r in range(pl...  59.6 us
    ppermute x42, starting transfers between devices, swap(): return lax.ppermute(value, PLANE, [(k, k ^ bit) for k in range(plan.plane)])  33.1 us
    pallas_call x1, Pallas kernels, body(): pl.pallas_call(functools.partial(left_kernel, plan, tile, half_steps), gr...  24.6 us
    another operation x18, local copies, waits for them, and re-layouts  21.1 us
    ppermute x7, starting transfers between devices, body(): lax.ppermute(front_cut[m], PLANE, [(k, k ^ m) for k in owners])  20.8 us
  transfers between devices with their start and end apart: 64, of which 21 were waited for; matrix products, arithmetic and copies ran while one was open for 43% of the time, Pallas kernels for 12%

profile of v1, /device:TPU:0, one launch (start us, length us, event | category | flops | bytes accessed | tf_op | source)
XLA Modules:
  0.0 561.3 jit_solution(4196455511427180611)
XLA Ops:
  0.7 2.8 cut_child.1
  3.9 2.5 collective-permute-start.4
  9.2 3.9 cut_front.1
  14.2 2.7 collective-permute-start.8
  17.1 2.2 collective-permute-start.13
  19.4 2.7 collective-permute-done.8
  22.1 2.6 collective-permute-done.9
  28.4 17.2 %collective-permute-done.10.refs_1_ = f32[8,11,16,128]{3,2,1,0:T(8,128)S(1)} collective-permute-done((f32[8,11,16,128]{3,2,1,0:T(8,128)S(1)}, f32[8,11,16,128]{3,2,1,0:T(8,128)S(1)}, u32[]{:S(2)}, u32[]{:S(2)}) %collective-permute-start.10) | collective-permute-done | bytes 720928 | tf_op jit(solution)/shard_map/ppermute | solution.py:429
  45.6 4.4 collective-permute-start.14
  50.0 2.0 collective-permute-start.15
  52.1 3.4 collective-permute-start.16
  55.4 2.8 collective-permute-done.54.refs_5_
  58.3 15.4 %collective-permute-done.11.refs_2_ = f32[8,11,16,128]{3,2,1,0:T(8,128)S(1)} collective-permute-done((f32[8,11,16,128]{3,2,1,0:T(8,128)S(1)}, f32[8,11,16,128]{3,2,1,0:T(8,128)S(1)}, u32[]{:S(2)}, u32[]{:S(2)}) %collective-permute-start.11) | collective-permute-done | bytes 720928 | tf_op jit(solution)/shard_map/ppermute | solution.py:429
  73.7 2.8 collective-permute-start.17
  76.5 3.9 collective-permute-start.18
  80.5 2.0 collective-permute-start.19
  82.5 2.8 collective-permute-done.18.refs_6_
  85.3 4.2 collective-permute-done.19.refs_7_
  89.5 3.6 front_panel.1
  95.7 8.2 %collective-permute-done.20.refs_5_ = f32[2,6,16,128]{3,2,1,0:T(8,128)S(1)} collective-permute-done((f32[2,6,16,128]{3,2,1,0:T(8,128)}, f32[2,6,16,128]{3,2,1,0:T(8,128)S(1)}, u32[]{:S(2)}, u32[]{:S(2)}) %collective-permute-start.20) | collective-permute-done | bytes 98336 | tf_op jit(solution)/shard_map/ppermute | solution.py:429
  108.0 10.2 %collective-permute-done.21.refs_6_ = f32[2,6,16,128]{3,2,1,0:T(8,128)S(1)} collective-permute-done((f32[2,6,16,128]{3,2,1,0:T(8,128)S(1)}, f32[2,6,16,128]{3,2,1,0:T(8,128)S(1)}, u32[]{:S(2)}, u32[]{:S(2)}) %collective-permute-start.21) | collective-permute-done | bytes 98336 | tf_op jit(solution)/shard_map/ppermute | solution.py:429
  118.8 5.8 %collective-permute-done.22.refs_7_ = f32[2,6,16,128]{3,2,1,0:T(8,128)S(1)} collective-permute-done((f32[2,6,16,128]{3,2,1,0:T(8,128)S(1)}, f32[2,6,16,128]{3,2,1,0:T(8,128)S(1)}, u32[]{:S(2)}, u32[]{:S(2)}) %collective-permute-start.22) | collective-permute-done | bytes 98336 | tf_op jit(solution)/shard_map/ppermute | solution.py:429
  126.2 8.5 %panel.1 = (f32[16,6,16,128]{3,2,1,0:T(8,128)}, f32[6,6,16,128]{3,2,1,0:T(8,128)}, f32[2,8,16,128]{3,2,1,0:T(8,128)}, f32[2,8,16,128]{3,2,1,0:T(8,128)}, f32[2,8...) custom-call(s32[4]{0:T(128)} %pad_add_fusion.1.place_ref, ...), custom_call_target="tpu_custom_call" | custom-call | tf_op jit(solution)/shard_map/panel/pallas_call | solution.py:490
  140.0 2.8 collective-permute-done.45.refs_2_
  146.7 4.5 collective-permute-done.46.refs_3_
  154.6 6.1 %collective-permute-done.28.refs_6_ = f32[6,6,16,128]{3,2,1,0:T(8,128)S(1)} collective-permute-done((f32[6,6,16,128]{3,2,1,0:T(8,128)S(1)}, f32[6,6,16,128]{3,2,1,0:T(8,128)S(1)}, u32[]{:S(2)}, u32[]{:S(2)}) %collective-permute-start.28) | collective-permute-done | bytes 294944 | tf_op jit(solution)/shard_map/ppermute | solution.py:414
  160.7 10.9 %spread.1 = (f32[16,8,16,128]{3,2,1,0:T(8,128)}, f32[16,8,16,128]{3,2,1,0:T(8,128)}, f32[16,8,16,128]{3,2,1,0:T(8,128)}, f32[16,8,16,128]{3,2,1,0:T(8,128)}, f32...) custom-call(s32[4]{0:T(128)} %pad_add_fusion.1.place_ref, ...), custom_call_target="tpu_custom_call" | custom-call | tf_op jit(solution)/shard_map/spread/pallas_call | solution.py:586
  173.5 4.2 collective-permute-done.50.refs_7_
  178.3 3.0 lead_rows.1.refs_0_
  181.3 2.1 collective-permute-start.31
  184.7 3.2 corner.1
  188.7 11.7 %cholesky.165 = f32[128,128]{1,0:T(8,128)S(1)} custom-call(f32[128,128]{1,0:T(8,128)S(1)} %cholesky.424), custom_call_target="Cholesky" | custom-call | tf_op jit(solution)/shard_map/cholesky | solution.py:519
  200.6 9.8 %custom-call.35 = f32[1,128,128]{1,2,0:T(8,128)S(1)} custom-call(f32[1,128,128]{2,1,0:T(8,128)S(1)} %get-tuple-element.134), custom_call_target="InvertDiagBlocksLowerTriangular" | custom-call | tf_op jit(solution)/shard_map/cholesky | solution.py:519
  213.8 12.5 %cholesky.188 = f32[128,128]{1,0:T(8,128)S(1)} custom-call(f32[128,128]{1,0:T(8,128)} %cholesky.428), custom_call_target="Cholesky" | custom-call | tf_op jit(solution)/shard_map/cholesky | solution.py:519
  227.0 11.0 %custom-call.36 = f32[1,128,128]{1,2,0:T(8,128)S(1)} custom-call(f32[1,128,128]{2,1,0:T(8,128)} %get-tuple-element.131), custom_call_target="InvertDiagBlocksLowerTriangular" | custom-call | tf_op jit(solution)/shard_map/cholesky | solution.py:519
  240.0 11.7 %cholesky.354 = f32[128,128]{1,0:T(8,128)S(1)} custom-call(f32[128,128]{1,0:T(8,128)S(1)} %cholesky.433), custom_call_target="Cholesky" | custom-call | tf_op jit(solution)/shard_map/cholesky | solution.py:519
  251.7 9.8 %custom-call.37 = f32[1,128,128]{1,2,0:T(8,128)S(1)} custom-call(f32[1,128,128]{2,1,0:T(8,128)S(1)} %get-tuple-element.128), custom_call_target="InvertDiagBlocksLowerTriangular" | custom-call | tf_op jit(solution)/shard_map/cholesky | solution.py:519
  263.4 11.9 %cholesky.373 = f32[128,128]{1,0:T(8,128)S(1)} custom-call(f32[128,128]{1,0:T(8,128)S(1)} %cholesky.438), custom_call_target="Cholesky" | custom-call | tf_op jit(solution)/shard_map/cholesky | solution.py:519
  275.3 9.8 %custom-call.38 = f32[1,128,128]{1,2,0:T(8,128)S(1)} custom-call(f32[1,128,128]{2,1,0:T(8,128)S(1)} %get-tuple-element.125), custom_call_target="InvertDiagBlocksLowerTriangular" | custom-call | tf_op jit(solution)/shard_map/cholesky | solution.py:519
  286.9 11.7 %cholesky.392 = f32[128,128]{1,0:T(8,128)S(1)} custom-call(f32[128,128]{1,0:T(8,128)S(1)} %cholesky.443), custom_call_target="Cholesky" | custom-call | tf_op jit(solution)/shard_map/cholesky | solution.py:519
  298.7 9.8 %custom-call.39 = f32[1,128,128]{1,2,0:T(8,128)S(1)} custom-call(f32[1,128,128]{2,1,0:T(8,128)S(1)} %get-tuple-element.122), custom_call_target="InvertDiagBlocksLowerTriangular" | custom-call | tf_op jit(solution)/shard_map/cholesky | solution.py:519
  310.0 11.9 %cholesky.410 = f32[128,128]{1,0:T(8,128)S(1)} custom-call(f32[128,128]{1,0:T(8,128)S(1)} %slice_subtract_fusion.4), custom_call_target="Cholesky" | custom-call | tf_op jit(solution)/shard_map/cholesky | solution.py:519
  329.1 2.5 fusion
  334.8 21.1 %while.1 = (s32[]{:T(128)}, f32[768,768]{1,0:T(8,128)}, s32[6,2]{0,1:T(2,128)S(1)}, f32[6,128,128]{2,1,0:T(8,128)}, s32[]{:T(128)}) while((s32[]{:T(128)}, f32[768,768]{1,0:T(8,128)}, s32[6,2]{0,1:T(2,128)S(1)}, f32[6,128,128]{2,1,0:T(8,128)}, s32[]{:T(128)}) %tuple.42), condition=%wide.while_cond, body=%wide.while_body.sunk | while | flops 2 | bytes 132205 | solution.py:520
  335.4 2.9 bitcast_dynamic-update-slice_fusion.4
  339.0 2.9 bitcast_dynamic-update-slice_fusion.4
  342.5 2.9 bitcast_dynamic-update-slice_fusion.4
  346.0 2.9 bitcast_dynamic-update-slice_fusion.4
  349.5 2.9 bitcast_dynamic-update-slice_fusion.4
  353.1 2.8 bitcast_dynamic-update-slice_fusion.4
  355.9 60.4 %custom-call.40 = f32[6,128,128]{1,2,0:T(8,128)} custom-call(f32[6,128,128]{2,1,0:T(8,128)} %get-tuple-element.94), custom_call_target="InvertDiagBlocksLowerTriangular" | custom-call | tf_op jit(solution)/shard_map/triangular_solve | solution.py:520
  422.2 4.0 collective-permute-start.53
  426.8 3.5 collective-permute-done.35.refs_6_
  433.7 6.1 %collective-permute-done.42.refs_14_ = f32[8,6,16,128]{3,2,1,0:T(8,128)S(1)} collective-permute-done((f32[8,6,16,128]{3,2,1,0:T(8,128)S(1)}, f32[8,6,16,128]{3,2,1,0:T(8,128)S(1)}, u32[]{:S(2)}, u32[]{:S(2)}) %collective-permute-start.42) | collective-permute-done | bytes 393248 | tf_op jit(solution)/shard_map/ppermute | solution.py:414
  439.8 2.0 convolution_subtract_fusion.1
  443.4 9.5 %collective-permute-done.58.refs_2_ = f32[16,8,16,128]{3,2,1,0:T(8,128)} collective-permute-done((f32[16,8,16,128]{3,2,1,0:T(8,128)}, f32[16,8,16,128]{3,2,1,0:T(8,128)}, u32[]{:S(2)}, u32[]{:S(2)}) %collective-permute-start.58) | collective-permute-done | bytes 1048608 | tf_op jit(solution)/shard_map/ppermute | solution.py:414
  453.5 2.0 collective-permute-start.62
  457.3 2.0 fusion.9
  459.8 2.3 convolution_subtract_fusion
  464.1 24.6 %left_factor.1 = (bf16[2048,768]{1,0:T(8,128)(2,1)}, bf16[2048,768]{1,0:T(8,128)(2,1)}, f32[2048,384]{1,0:T(8,128)}) custom-call(s32[4]{0:T(128)} %pad_add_fusion.1.place_ref, f32[768,768]{1,0:T(8,128)} %copy-done, f32[768,768]{1,0:T(8,128)} %get-tuple-element.104.factor_ref, f32[8,6,16,128]{3,2,1,0:T(8,128)} %copy-done.7, ...), custom_call_target="tpu_custom_call" | custom-call | tf_op jit(solution)/shard_map/left_factor/pallas_call | solution.py:552
  488.7 10.6 %right_factor.1 = (bf16[768,1024]{1,0:T(8,128)(2,1)}, bf16[768,1024]{1,0:T(8,128)(2,1)}) custom-call(s32[4]{0:T(128)} %pad_add_fusion.1.place_ref, f32[768,768]{1,0:T(8,128)} %copy-done, f32[2,128,1024]{2,1,0:T(8,128)} %lead_rows.1.refs_0_, f32[2,128,1024]{2,1,0:T(8,128)} %collective-permute-done.51.refs_1_, ...), custom_call_target="tpu_custom_call" | custom-call | tf_op jit(solution)/shard_map/right_factor/pallas_call | solution.py:537
  499.8 24.9 %collective-permute-done.62.refs_6_ = f32[16,8,16,128]{3,2,1,0:T(8,128)} collective-permute-done((f32[16,8,16,128]{3,2,1,0:T(8,128)}, f32[16,8,16,128]{3,2,1,0:T(8,128)}, u32[]{:S(2)}, u32[]{:S(2)}) %collective-permute-start.62) | collective-permute-done | bytes 1048608 | tf_op jit(solution)/shard_map/ppermute | solution.py:414
  524.7 17.4 %collective-permute-done.63.refs_7_ = f32[16,8,16,128]{3,2,1,0:T(8,128)} collective-permute-done((f32[16,8,16,128]{3,2,1,0:T(8,128)}, f32[16,8,16,128]{3,2,1,0:T(8,128)}, u32[]{:S(2)}, u32[]{:S(2)}) %collective-permute-start.63) | collective-permute-done | bytes 1048608 | tf_op jit(solution)/shard_map/ppermute | solution.py:414
  542.1 18.8 %schur.1 = f32[2048,1024]{1,0:T(8,128)} custom-call(s32[4]{0:T(128)} %pad_add_fusion.1.place_ref, f32[2048,1024]{1,0:T(8,128)} %front_ref.5, bf16[2048,768]{1,0:T(8,128)(2,1)} %get-tuple-element.66.high_ref, bf16[2048,768]{1,0:T(8,128)(2,1)} %get-tuple-element.67.low_ref, f32[2048,384]{1,0:T(8,128)} %get-tuple-element.68.own_ref, ...), custom_call_target="tpu_custom_call" | custom-call | tf_op jit(solution)/shard_map/schur/pallas_call | solution.py:605
  (266 shorter events, 73.2 us)
Async XLA Ops:
  3.5 10.7 %collective-permute-start.3 = (f32[20,16,128]{2,1,0:T(8,128)}, f32[20,16,128]{2,1,0:T(8,128)S(1)}, u32[]{:S(2)}, u32[]{:S(2)}) collective-permute-start(f32[20,16,128]{2,1,0:T(8,128)} %get-tuple-element.47), channel_id=1, source_target_pairs={{0,1},{1,0},{2,3},{3,2},{4,5},{5,4},{6,7},{7,6},{8,9},{9,8},{10,11... | collective-permute-start | bytes 491528 | tf_op jit(solution)/shard_map/ppermute | solution.py:414
  3.9 12.9 %collective-permute-start.4 = (f32[20,16,128]{2,1,0:T(8,128)}, f32[20,16,128]{2,1,0:T(8,128)S(1)}, u32[]{:S(2)}, u32[]{:S(2)}) collective-permute-start(f32[20,16,128]{2,1,0:T(8,128)} %get-tuple-element.48), channel_id=1, source_target_pairs={{0,2},{1,3},{2,0},{3,1},{4,6},{5,7},{6,4},{7,5},{8,10},{9,11},{10,... | collective-permute-start | bytes 491528 | tf_op jit(solution)/shard_map/ppermute | solution.py:414
  6.4 10.6 %collective-permute-start.5 = (f32[20,16,128]{2,1,0:T(8,128)}, f32[20,16,128]{2,1,0:T(8,128)S(1)}, u32[]{:S(2)}, u32[]{:S(2)}) collective-permute-start(f32[20,16,128]{2,1,0:T(8,128)} %get-tuple-element.49), channel_id=1, source_target_pairs={{0,3},{1,2},{2,1},{3,0},{4,7},{5,6},{6,5},{7,4},{8,11},{9,10},{10,... | collective-permute-start | bytes 491528 | tf_op jit(solution)/shard_map/ppermute | solution.py:414
  6.6 12.8 %collective-permute-start.6 = (f32[20,16,128]{2,1,0:T(8,128)}, f32[20,16,128]{2,1,0:T(8,128)S(1)}, u32[]{:S(2)}, u32[]{:S(2)}) collective-permute-start(f32[20,16,128]{2,1,0:T(8,128)} %get-tuple-element.50), channel_id=1, source_target_pairs={{0,4},{1,5},{2,6},{3,7},{4,0},{5,1},{6,2},{7,3},{8,12},{9,13},{10,... | collective-permute-start | bytes 491528 | tf_op jit(solution)/shard_map/ppermute | solution.py:414
  8.3 11.1 %collective-permute-start.7 = (f32[20,16,128]{2,1,0:T(8,128)}, f32[20,16,128]{2,1,0:T(8,128)S(1)}, u32[]{:S(2)}, u32[]{:S(2)}) collective-permute-start(f32[20,16,128]{2,1,0:T(8,128)} %get-tuple-element.51), channel_id=1, source_target_pairs={{0,5},{1,4},{2,7},{3,6},{4,1},{5,0},{6,3},{7,2},{8,13},{9,12},{10,... | collective-permute-start | bytes 491528 | tf_op jit(solution)/shard_map/ppermute | solution.py:414
  14.2 8.0 %collective-permute-start.8 = (f32[20,16,128]{2,1,0:T(8,128)S(1)}, f32[20,16,128]{2,1,0:T(8,128)S(1)}, u32[]{:S(2)}, u32[]{:S(2)}) collective-permute-start(f32[20,16,128]{2,1,0:T(8,128)S(1)} %copy-done.46), channel_id=1, source_target_pairs={{0,6},{1,7},{2,4},{3,5},{4,2},{5,3},{6,0},{7,1},{8,14},{9,15},{10,... | collective-permute-start | bytes 491528 | tf_op jit(solution)/shard_map/ppermute | solution.py:414
  16.9 7.9 %collective-permute-start.9 = (f32[20,16,128]{2,1,0:T(8,128)S(1)}, f32[20,16,128]{2,1,0:T(8,128)S(1)}, u32[]{:S(2)}, u32[]{:S(2)}) collective-permute-start(f32[20,16,128]{2,1,0:T(8,128)S(1)} %copy-done.45), channel_id=1, source_target_pairs={{0,7},{1,6},{2,5},{3,4},{4,3},{5,2},{6,1},{7,0},{8,15},{9,14},{10,... | collective-permute-start | bytes 491528 | tf_op jit(solution)/shard_map/ppermute | solution.py:414
  17.1 35.0 %collective-permute-start.13 = (f32[16,3,16,128]{3,2,1,0:T(8,128)}, f32[16,3,16,128]{3,2,1,0:T(8,128)S(1)}, u32[]{:S(2)}, u32[]{:S(2)}) collective-permute-start(f32[16,3,16,128]{3,2,1,0:T(8,128)} %get-tuple-element.55), channel_id=1, source_target_pairs={{0,1},{4,5},{8,9},{12,13},{16,17},{20,21},{24,25},{28,29}} | collective-permute-start | bytes 1179656 | tf_op jit(solution)/shard_map/ppermute | solution.py:475
  24.8 20.8 %collective-permute-start.10 = (f32[8,11,16,128]{3,2,1,0:T(8,128)S(1)}, f32[8,11,16,128]{3,2,1,0:T(8,128)S(1)}, u32[]{:S(2)}, u32[]{:S(2)}) collective-permute-start(f32[8,11,16,128]{3,2,1,0:T(8,128)S(1)} %fusion.47.refs_0_), channel_id=1, source_target_pairs={{0,8},{8,16},{16,24},{24,0},{1,9},{9,17},{17,25},{25,1},{2,10},{10... | collective-permute-start | bytes 2162696 | tf_op jit(solution)/shard_map/ppermute | solution.py:429
  26.7 31.5 %collective-permute-start.54 = (f32[8,9,16,128]{3,2,1,0:T(8,128)S(1)}, f32[8,9,16,128]{3,2,1,0:T(8,128)S(1)}, u32[]{:S(2)}, u32[]{:S(2)}) collective-permute-start(f32[8,9,16,128]{3,2,1,0:T(8,128)S(1)} %fusion.54.refs_4_), channel_id=1, source_target_pairs={{0,8},{8,16},{16,24},{24,0},{1,9},{9,17},{17,25},{25,1},{2,10},{10... | collective-permute-start | bytes 1769480 | tf_op jit(solution)/shard_map/ppermute | solution.py:429
  45.6 28.1 %collective-permute-start.11 = (f32[8,11,16,128]{3,2,1,0:T(8,128)S(1)}, f32[8,11,16,128]{3,2,1,0:T(8,128)S(1)}, u32[]{:S(2)}, u32[]{:S(2)}) collective-permute-start(f32[8,11,16,128]{3,2,1,0:T(8,128)S(1)} %collective-permute-done.10.refs_1_), channel_id=1, source_target_pairs={{0,8},{8,16},{16,24},{24,0},{1,9},{9,17},{17,25},{25,1},{2,10},{10... | collective-permute-start | bytes 2162696 | tf_op jit(solution)/shard_map/ppermute | solution.py:429
  45.6 28.1 %collective-permute-start.14 = (f32[16,3,16,128]{3,2,1,0:T(8,128)S(1)}, f32[16,3,16,128]{3,2,1,0:T(8,128)}, u32[]{:S(2)}, u32[]{:S(2)}) collective-permute-start(f32[16,3,16,128]{3,2,1,0:T(8,128)S(1)} %copy-done.44), channel_id=1, source_target_pairs={{0,2},{4,6},{8,10},{12,14},{16,18},{20,22},{24,26},{28,30}} | collective-permute-start | bytes 1179656 | tf_op jit(solution)/shard_map/ppermute | solution.py:475
  50.0 26.5 %collective-permute-start.15 = (f32[16,3,16,128]{3,2,1,0:T(8,128)S(1)}, f32[16,3,16,128]{3,2,1,0:T(8,128)}, u32[]{:S(2)}, u32[]{:S(2)}) collective-permute-start(f32[16,3,16,128]{3,2,1,0:T(8,128)S(1)} %copy-done.43), channel_id=1, source_target_pairs={{0,3},{4,7},{8,11},{12,15},{16,19},{20,23},{24,27},{28,31}} | collective-permute-start | bytes 1179656 | tf_op jit(solution)/shard_map/ppermute | solution.py:475
  52.1 28.4 %collective-permute-start.16 = (f32[16,3,16,128]{3,2,1,0:T(8,128)S(1)}, f32[16,3,16,128]{3,2,1,0:T(8,128)}, u32[]{:S(2)}, u32[]{:S(2)}) collective-permute-start(f32[16,3,16,128]{3,2,1,0:T(8,128)S(1)} %copy-done.42), channel_id=1, source_target_pairs={{0,4},{4,0},{8,12},{12,8},{16,20},{20,16},{24,28},{28,24}} | collective-permute-start | bytes 1179656 | tf_op jit(solution)/shard_map/ppermute | solution.py:475
  58.2 35.9 %collective-permute-start.55 = (f32[8,9,16,128]{3,2,1,0:T(8,128)S(1)}, f32[8,9,16,128]{3,2,1,0:T(8,128)}, u32[]{:S(2)}, u32[]{:S(2)}) collective-permute-start(f32[8,9,16,128]{3,2,1,0:T(8,128)S(1)} %collective-permute-done.54.refs_5_), channel_id=1, source_target_pairs={{0,8},{8,16},{16,24},{24,0},{1,9},{9,17},{17,25},{25,1},{2,10},{10... | collective-permute-start | bytes 1769480 | tf_op jit(solution)/shard_map/ppermute | solution.py:429
  73.7 51.0 %collective-permute-start.12 = (f32[8,11,16,128]{3,2,1,0:T(8,128)S(1)}, f32[8,11,16,128]{3,2,1,0:T(8,128)S(1)}, u32[]{:S(2)}, u32[]{:S(2)}) collective-permute-start(f32[8,11,16,128]{3,2,1,0:T(8,128)S(1)} %collective-permute-done.11.refs_2_), channel_id=1, source_target_pairs={{0,8},{8,16},{16,24},{24,0},{1,9},{9,17},{17,25},{25,1},{2,10},{10... | collective-permute-start | bytes 2162696 | tf_op jit(solution)/shard_map/ppermute | solution.py:429
  73.7 8.8 %collective-permute-start.17 = (f32[16,3,16,128]{3,2,1,0:T(8,128)S(1)}, f32[16,3,16,128]{3,2,1,0:T(8,128)}, u32[]{:S(2)}, u32[]{:S(2)}) collective-permute-start(f32[16,3,16,128]{3,2,1,0:T(8,128)S(1)} %copy-done.41), channel_id=1, source_target_pairs={{0,5},{4,1},{8,13},{12,9},{16,21},{20,17},{24,29},{28,25}} | collective-permute-start | bytes 1179656 | tf_op jit(solution)/shard_map/ppermute | solution.py:475
  76.5 8.7 %collective-permute-start.18 = (f32[16,3,16,128]{3,2,1,0:T(8,128)S(1)}, f32[16,3,16,128]{3,2,1,0:T(8,128)}, u32[]{:S(2)}, u32[]{:S(2)}) collective-permute-start(f32[16,3,16,128]{3,2,1,0:T(8,128)S(1)} %copy-done.40), channel_id=1, source_target_pairs={{0,6},{4,2},{8,14},{12,10},{16,22},{20,18},{24,30},{28,26}} | collective-permute-start | bytes 1179656 | tf_op jit(solution)/shard_map/ppermute | solution.py:475
  80.5 9.0 %collective-permute-start.19 = (f32[16,3,16,128]{3,2,1,0:T(8,128)S(1)}, f32[16,3,16,128]{3,2,1,0:T(8,128)}, u32[]{:S(2)}, u32[]{:S(2)}) collective-permute-start(f32[16,3,16,128]{3,2,1,0:T(8,128)S(1)} %copy-done.39), channel_id=1, source_target_pairs={{0,7},{4,3},{8,15},{12,11},{16,23},{20,19},{24,31},{28,27}} | collective-permute-start | bytes 1179656 | tf_op jit(solution)/shard_map/ppermute | solution.py:475
  93.1 10.8 %collective-permute-start.20 = (f32[2,6,16,128]{3,2,1,0:T(8,128)}, f32[2,6,16,128]{3,2,1,0:T(8,128)S(1)}, u32[]{:S(2)}, u32[]{:S(2)}) collective-permute-start(f32[2,6,16,128]{3,2,1,0:T(8,128)} %get-tuple-element.62.refs_4_), channel_id=1, source_target_pairs={{0,8},{8,16},{16,24},{24,0},{1,9},{9,17},{17,25},{25,1},{2,10},{10... | collective-permute-start | bytes 294920 | tf_op jit(solution)/shard_map/ppermute | solution.py:429
  94.1 44.2 %collective-permute-start.56 = (f32[8,9,16,128]{3,2,1,0:T(8,128)}, f32[8,9,16,128]{3,2,1,0:T(8,128)}, u32[]{:S(2)}, u32[]{:S(2)}) collective-permute-start(f32[8,9,16,128]{3,2,1,0:T(8,128)} %collective-permute-done.55.refs_6_), channel_id=1, source_target_pairs={{0,8},{8,16},{16,24},{24,0},{1,9},{9,17},{17,25},{25,1},{2,10},{10... | collective-permute-start | bytes 1769480 | tf_op jit(solution)/shard_map/ppermute | solution.py:429
  104.5 13.7 %collective-permute-start.21 = (f32[2,6,16,128]{3,2,1,0:T(8,128)S(1)}, f32[2,6,16,128]{3,2,1,0:T(8,128)S(1)}, u32[]{:S(2)}, u32[]{:S(2)}) collective-permute-start(f32[2,6,16,128]{3,2,1,0:T(8,128)S(1)} %collective-permute-done.20.refs_5_), channel_id=1, source_target_pairs={{0,8},{8,16},{16,24},{24,0},{1,9},{9,17},{17,25},{25,1},{2,10},{10... | collective-permute-start | bytes 294920 | tf_op jit(solution)/shard_map/ppermute | solution.py:429
  104.5 3.0 collective-permute-start.2
  104.7 13.5 %collective-permute-start.1 = (s32[16]{0:T(128)S(1)}, s32[16]{0:T(128)S(1)}, u32[]{:S(2)}, u32[]{:S(2)}) collective-permute-start(s32[16]{0:T(128)S(1)} %bitcast.142), channel_id=1, source_target_pairs={{0,2},{1,3},{2,0},{3,1},{4,6},{5,7},{6,4},{7,5},{8,10},{9,11},{10,... | collective-permute-start | bytes 200 | tf_op jit(solution)/shard_map/ppermute | solution.py:447
  107.5 10.7 %collective-permute-start = (s32[16]{0:T(128)S(1)}, s32[16]{0:T(128)S(1)}, u32[]{:S(2)}, u32[]{:S(2)}) collective-permute-start(s32[16]{0:T(128)S(1)} %bitcast.143), channel_id=1, source_target_pairs={{0,1},{1,0},{2,3},{3,2},{4,5},{5,4},{6,7},{7,6},{8,9},{9,8},{10,11... | collective-permute-start | bytes 200 | tf_op jit(solution)/shard_map/ppermute | solution.py:447
  118.2 6.4 %collective-permute-start.22 = (f32[2,6,16,128]{3,2,1,0:T(8,128)S(1)}, f32[2,6,16,128]{3,2,1,0:T(8,128)S(1)}, u32[]{:S(2)}, u32[]{:S(2)}) collective-permute-start(f32[2,6,16,128]{3,2,1,0:T(8,128)S(1)} %collective-permute-done.21.refs_6_), channel_id=1, source_target_pairs={{0,8},{8,16},{16,24},{24,0},{1,9},{9,17},{17,25},{25,1},{2,10},{10... | collective-permute-start | bytes 294920 | tf_op jit(solution)/shard_map/ppermute | solution.py:429
  134.7 8.7 %collective-permute-start.26 = (f32[6,6,16,128]{3,2,1,0:T(8,128)}, f32[6,6,16,128]{3,2,1,0:T(8,128)S(1)}, u32[]{:S(2)}, u32[]{:S(2)}) collective-permute-start(f32[6,6,16,128]{3,2,1,0:T(8,128)} %get-tuple-element.64.refs_0_), channel_id=1, source_target_pairs={{0,4},{1,5},{2,6},{3,7},{4,0},{5,1},{6,2},{7,3},{8,12},{9,13},{10,... | collective-permute-start | bytes 884744 | tf_op jit(solution)/shard_map/ppermute | solution.py:414
  136.3 3.2 collective-permute-start.44
  136.3 6.5 %collective-permute-start.45 = (f32[2,8,16,128]{3,2,1,0:T(8,128)}, f32[2,8,16,128]{3,2,1,0:T(8,128)S(1)}, u32[]{:S(2)}, u32[]{:S(2)}) collective-permute-start(f32[2,8,16,128]{3,2,1,0:T(8,128)} %get-tuple-element.71), channel_id=1, source_target_pairs={{0,2},{1,3},{2,0},{3,1},{4,6},{5,7},{6,4},{7,5},{8,10},{9,11},{10,... | collective-permute-start | bytes 393224 | tf_op jit(solution)/shard_map/ppermute | solution.py:414
  137.8 16.4 %collective-permute-start.24 = (f32[6,6,16,128]{3,2,1,0:T(8,128)}, f32[6,6,16,128]{3,2,1,0:T(8,128)S(1)}, u32[]{:S(2)}, u32[]{:S(2)}) collective-permute-start(f32[6,6,16,128]{3,2,1,0:T(8,128)} %get-tuple-element.64.refs_0_), channel_id=1, source_target_pairs={{0,2},{1,3},{2,0},{3,1},{4,6},{5,7},{6,4},{7,5},{8,10},{9,11},{10,... | collective-permute-start | bytes 884744 | tf_op jit(solution)/shard_map/ppermute | solution.py:414
  138.3 12.8 %collective-permute-start.46 = (f32[2,8,16,128]{3,2,1,0:T(8,128)}, f32[2,8,16,128]{3,2,1,0:T(8,128)S(1)}, u32[]{:S(2)}, u32[]{:S(2)}) collective-permute-start(f32[2,8,16,128]{3,2,1,0:T(8,128)} %get-tuple-element.72), channel_id=1, source_target_pairs={{0,3},{1,2},{2,1},{3,0},{4,7},{5,6},{6,5},{7,4},{8,11},{9,10},{10,... | collective-permute-start | bytes 393224 | tf_op jit(solution)/shard_map/ppermute | solution.py:414
  139.4 14.2 %collective-permute-start.47 = (f32[2,8,16,128]{3,2,1,0:T(8,128)}, f32[2,8,16,128]{3,2,1,0:T(8,128)}, u32[]{:S(2)}, u32[]{:S(2)}) collective-permute-start(f32[2,8,16,128]{3,2,1,0:T(8,128)} %get-tuple-element.73), channel_id=1, source_target_pairs={{0,4},{1,5},{2,6},{3,7},{4,0},{5,1},{6,2},{7,3},{8,12},{9,13},{10,... | collective-permute-start | bytes 393224 | tf_op jit(solution)/shard_map/ppermute | solution.py:414
  142.8 11.3 %collective-permute-start.48 = (f32[2,8,16,128]{3,2,1,0:T(8,128)}, f32[2,8,16,128]{3,2,1,0:T(8,128)}, u32[]{:S(2)}, u32[]{:S(2)}) collective-permute-start(f32[2,8,16,128]{3,2,1,0:T(8,128)} %get-tuple-element.74), channel_id=1, source_target_pairs={{0,5},{1,4},{2,7},{3,6},{4,1},{5,0},{6,3},{7,2},{8,13},{9,12},{10,... | collective-permute-start | bytes 393224 | tf_op jit(solution)/shard_map/ppermute | solution.py:414
  143.4 17.2 %collective-permute-start.28 = (f32[6,6,16,128]{3,2,1,0:T(8,128)S(1)}, f32[6,6,16,128]{3,2,1,0:T(8,128)S(1)}, u32[]{:S(2)}, u32[]{:S(2)}) collective-permute-start(f32[6,6,16,128]{3,2,1,0:T(8,128)S(1)} %collective-permute-done.26.refs_4_), channel_id=1, source_target_pairs={{0,2},{1,3},{2,0},{3,1},{4,6},{5,7},{6,4},{7,5},{8,10},{9,11},{10,... | collective-permute-start | bytes 884744 | tf_op jit(solution)/shard_map/ppermute | solution.py:414
  151.1 20.5 %collective-permute-start.49 = (f32[2,8,16,128]{3,2,1,0:T(8,128)S(1)}, f32[2,8,16,128]{3,2,1,0:T(8,128)S(1)}, u32[]{:S(2)}, u32[]{:S(2)}) collective-permute-start(f32[2,8,16,128]{3,2,1,0:T(8,128)S(1)} %copy-done.48), channel_id=1, source_target_pairs={{0,6},{1,7},{2,4},{3,5},{4,2},{5,3},{6,0},{7,1},{8,14},{9,15},{10,... | collective-permute-start | bytes 393224 | tf_op jit(solution)/shard_map/ppermute | solution.py:414
  153.7 27.6 %collective-permute-start.23 = (f32[6,6,16,128]{3,2,1,0:T(8,128)S(1)}, f32[6,6,16,128]{3,2,1,0:T(8,128)S(1)}, u32[]{:S(2)}, u32[]{:S(2)}) collective-permute-start(f32[6,6,16,128]{3,2,1,0:T(8,128)S(1)} %copy-done.24), channel_id=1, source_target_pairs={{0,1},{1,0},{2,3},{3,2},{4,5},{5,4},{6,7},{7,6},{8,9},{9,8},{10,11... | collective-permute-start | bytes 884744 | tf_op jit(solution)/shard_map/ppermute | solution.py:414
  154.1 29.9 %collective-permute-start.27 = (f32[6,6,16,128]{3,2,1,0:T(8,128)S(1)}, f32[6,6,16,128]{3,2,1,0:T(8,128)S(1)}, u32[]{:S(2)}, u32[]{:S(2)}) collective-permute-start(f32[6,6,16,128]{3,2,1,0:T(8,128)S(1)} %collective-permute-done.26.refs_4_), channel_id=1, source_target_pairs={{0,1},{1,0},{2,3},{3,2},{4,5},{5,4},{6,7},{7,6},{8,9},{9,8},{10,11... | collective-permute-start | bytes 884744 | tf_op jit(solution)/shard_map/ppermute | solution.py:414
  154.3 29.1 %collective-permute-start.25 = (f32[6,6,16,128]{3,2,1,0:T(8,128)S(1)}, f32[6,6,16,128]{3,2,1,0:T(8,128)}, u32[]{:S(2)}, u32[]{:S(2)}) collective-permute-start(f32[6,6,16,128]{3,2,1,0:T(8,128)S(1)} %collective-permute-done.24.refs_2_), channel_id=1, source_target_pairs={{0,1},{1,0},{2,3},{3,2},{4,5},{5,4},{6,7},{7,6},{8,9},{9,8},{10,11... | collective-permute-start | bytes 884744 | tf_op jit(solution)/shard_map/ppermute | solution.py:414
  160.7 23.3 %collective-permute-start.29 = (f32[6,6,16,128]{3,2,1,0:T(8,128)S(1)}, f32[6,6,16,128]{3,2,1,0:T(8,128)}, u32[]{:S(2)}, u32[]{:S(2)}) collective-permute-start(f32[6,6,16,128]{3,2,1,0:T(8,128)S(1)} %collective-permute-done.28.refs_6_), channel_id=1, source_target_pairs={{0,1},{1,0},{2,3},{3,2},{4,5},{5,4},{6,7},{7,6},{8,9},{9,8},{10,11... | collective-permute-start | bytes 884744 | tf_op jit(solution)/shard_map/ppermute | solution.py:414
  171.7 6.0 %collective-permute-start.50 = (f32[2,8,16,128]{3,2,1,0:T(8,128)S(1)}, f32[2,8,16,128]{3,2,1,0:T(8,128)S(1)}, u32[]{:S(2)}, u32[]{:S(2)}) collective-permute-start(f32[2,8,16,128]{3,2,1,0:T(8,128)S(1)} %copy-done.47), channel_id=1, source_target_pairs={{0,7},{1,6},{2,5},{3,4},{4,3},{5,2},{6,1},{7,0},{8,15},{9,14},{10,... | collective-permute-start | bytes 393224 | tf_op jit(solution)/shard_map/ppermute | solution.py:414
  177.7 153.9 %collective-permute-start.30 = (f32[8,6,16,128]{3,2,1,0:T(8,128)S(1)}, f32[8,6,16,128]{3,2,1,0:T(8,128)}, u32[]{:S(2)}, u32[]{:S(2)}) collective-permute-start(f32[8,6,16,128]{3,2,1,0:T(8,128)S(1)} %get-tuple-element.108.refs_0_), channel_id=1, source_target_pairs={{0,1},{1,0},{2,3},{3,2},{4,5},{5,4},{6,7},{7,6},{8,9},{9,8},{10,11... | collective-permute-start | bytes 1179656 | tf_op jit(solution)/shard_map/ppermute | solution.py:414
  181.3 150.4 %collective-permute-start.31 = (f32[8,6,16,128]{3,2,1,0:T(8,128)S(1)}, f32[8,6,16,128]{3,2,1,0:T(8,128)}, u32[]{:S(2)}, u32[]{:S(2)}) collective-permute-start(f32[8,6,16,128]{3,2,1,0:T(8,128)S(1)} %get-tuple-element.108.refs_0_), channel_id=1, source_target_pairs={{0,2},{1,3},{2,0},{3,1},{4,6},{5,7},{6,4},{7,5},{8,10},{9,11},{10,... | collective-permute-start | bytes 1179656 | tf_op jit(solution)/shard_map/ppermute | solution.py:414
  183.4 232.9 %collective-permute-start.33 = (f32[8,6,16,128]{3,2,1,0:T(8,128)S(1)}, f32[8,6,16,128]{3,2,1,0:T(8,128)}, u32[]{:S(2)}, u32[]{:S(2)}) collective-permute-start(f32[8,6,16,128]{3,2,1,0:T(8,128)S(1)} %get-tuple-element.108.refs_0_), channel_id=1, source_target_pairs={{0,4},{1,5},{2,6},{3,7},{4,0},{5,1},{6,2},{7,3},{8,12},{9,13},{10,... | collective-permute-start | bytes 1179656 | tf_op jit(solution)/shard_map/ppermute | solution.py:414
  184.0 232.3 %collective-permute-start.37 = (f32[8,6,16,128]{3,2,1,0:T(8,128)S(1)}, f32[8,6,16,128]{3,2,1,0:T(8,128)}, u32[]{:S(2)}, u32[]{:S(2)}) collective-permute-start(f32[8,6,16,128]{3,2,1,0:T(8,128)S(1)} %get-tuple-element.107.refs_8_), channel_id=1, source_target_pairs={{0,1},{1,0},{2,3},{3,2},{4,5},{5,4},{6,7},{7,6},{8,9},{9,8},{10,11... | collective-permute-start | bytes 1179656 | tf_op jit(solution)/shard_map/ppermute | solution.py:414
  184.0 149.2 %collective-permute-start.51 = (f32[2,128,1024]{2,1,0:T(8,128)}, f32[2,128,1024]{2,1,0:T(8,128)}, u32[]{:S(2)}, u32[]{:S(2)}) collective-permute-start(f32[2,128,1024]{2,1,0:T(8,128)} %lead_rows.1.refs_0_), channel_id=1, source_target_pairs={{0,8},{8,16},{16,24},{24,0},{1,9},{9,17},{17,25},{25,1},{2,10},{10... | collective-permute-start | bytes 3145736 | tf_op jit(solution)/shard_map/ppermute | solution.py:429
  331.6 86.4 %collective-permute-start.38 = (f32[8,6,16,128]{3,2,1,0:T(8,128)S(1)}, f32[8,6,16,128]{3,2,1,0:T(8,128)S(1)}, u32[]{:S(2)}, u32[]{:S(2)}) collective-permute-start(f32[8,6,16,128]{3,2,1,0:T(8,128)S(1)} %get-tuple-element.107.refs_8_), channel_id=1, source_target_pairs={{0,2},{1,3},{2,0},{3,1},{4,6},{5,7},{6,4},{7,5},{8,10},{9,11},{10,... | collective-permute-start | bytes 1179656 | tf_op jit(solution)/shard_map/ppermute | solution.py:414
  331.7 87.5 %collective-permute-start.40 = (f32[8,6,16,128]{3,2,1,0:T(8,128)S(1)}, f32[8,6,16,128]{3,2,1,0:T(8,128)S(1)}, u32[]{:S(2)}, u32[]{:S(2)}) collective-permute-start(f32[8,6,16,128]{3,2,1,0:T(8,128)S(1)} %get-tuple-element.107.refs_8_), channel_id=1, source_target_pairs={{0,4},{1,5},{2,6},{3,7},{4,0},{5,1},{6,2},{7,3},{8,12},{9,13},{10,... | collective-permute-start | bytes 1179656 | tf_op jit(solution)/shard_map/ppermute | solution.py:414
  333.2 89.1 %collective-permute-start.52 = (f32[2,128,1024]{2,1,0:T(8,128)}, f32[2,128,1024]{2,1,0:T(8,128)}, u32[]{:S(2)}, u32[]{:S(2)}) collective-permute-start(f32[2,128,1024]{2,1,0:T(8,128)} %collective-permute-done.51.refs_1_), channel_id=1, source_target_pairs={{0,8},{8,16},{16,24},{24,0},{1,9},{9,17},{17,25},{25,1},{2,10},{10... | collective-permute-start | bytes 3145736 | tf_op jit(solution)/shard_map/ppermute | solution.py:429
  416.3 4.5 collective-permute-start.32
  416.3 5.0 collective-permute-start.34
  418.0 12.2 %collective-permute-start.35 = (f32[8,6,16,128]{3,2,1,0:T(8,128)}, f32[8,6,16,128]{3,2,1,0:T(8,128)S(1)}, u32[]{:S(2)}, u32[]{:S(2)}) collective-permute-start(f32[8,6,16,128]{3,2,1,0:T(8,128)} %collective-permute-done.33.refs_4_), channel_id=1, source_target_pairs={{0,2},{1,3},{2,0},{3,1},{4,6},{5,7},{6,4},{7,5},{8,10},{9,11},{10,... | collective-permute-start | bytes 1179656 | tf_op jit(solution)/shard_map/ppermute | solution.py:414
  419.1 11.7 %collective-permute-start.39 = (f32[8,6,16,128]{3,2,1,0:T(8,128)S(1)}, f32[8,6,16,128]{3,2,1,0:T(8,128)S(1)}, u32[]{:S(2)}, u32[]{:S(2)}) collective-permute-start(f32[8,6,16,128]{3,2,1,0:T(8,128)S(1)} %collective-permute-done.38.refs_10_), channel_id=1, source_target_pairs={{0,1},{1,0},{2,3},{3,2},{4,5},{5,4},{6,7},{7,6},{8,9},{9,8},{10,11... | collective-permute-start | bytes 1179656 | tf_op jit(solution)/shard_map/ppermute | solution.py:414
  420.8 21.5 %collective-permute-start.57 = (f32[16,8,16,128]{3,2,1,0:T(8,128)}, f32[16,8,16,128]{3,2,1,0:T(8,128)S(1)}, u32[]{:S(2)}, u32[]{:S(2)}) collective-permute-start(f32[16,8,16,128]{3,2,1,0:T(8,128)} %get-tuple-element.80), channel_id=1, source_target_pairs={{0,1},{1,0},{2,3},{3,2},{4,5},{5,4},{6,7},{7,6},{8,9},{9,8},{10,11... | collective-permute-start | bytes 3145736 | tf_op jit(solution)/shard_map/ppermute | solution.py:414
  421.3 31.6 %collective-permute-start.58 = (f32[16,8,16,128]{3,2,1,0:T(8,128)}, f32[16,8,16,128]{3,2,1,0:T(8,128)}, u32[]{:S(2)}, u32[]{:S(2)}) collective-permute-start(f32[16,8,16,128]{3,2,1,0:T(8,128)} %get-tuple-element.81), channel_id=1, source_target_pairs={{0,2},{1,3},{2,0},{3,1},{4,6},{5,7},{6,4},{7,5},{8,10},{9,11},{10,... | collective-permute-start | bytes 3145736 | tf_op jit(solution)/shard_map/ppermute | solution.py:414
  422.2 33.3 %collective-permute-start.53 = (f32[2,128,1024]{2,1,0:T(8,128)}, f32[2,128,1024]{2,1,0:T(8,128)}, u32[]{:S(2)}, u32[]{:S(2)}) collective-permute-start(f32[2,128,1024]{2,1,0:T(8,128)} %collective-permute-done.52.refs_2_), channel_id=1, source_target_pairs={{0,8},{8,16},{16,24},{24,0},{1,9},{9,17},{17,25},{25,1},{2,10},{10... | collective-permute-start | bytes 3145736 | tf_op jit(solution)/shard_map/ppermute | solution.py:429
  430.3 9.5 %collective-permute-start.42 = (f32[8,6,16,128]{3,2,1,0:T(8,128)S(1)}, f32[8,6,16,128]{3,2,1,0:T(8,128)S(1)}, u32[]{:S(2)}, u32[]{:S(2)}) collective-permute-start(f32[8,6,16,128]{3,2,1,0:T(8,128)S(1)} %collective-permute-done.38.refs_10_), channel_id=1, source_target_pairs={{0,4},{1,5},{2,6},{3,7},{4,0},{5,1},{6,2},{7,3},{8,12},{9,13},{10,... | collective-permute-start | bytes 1179656 | tf_op jit(solution)/shard_map/ppermute | solution.py:414
  430.8 2.4 collective-permute-start.41
  433.2 20.2 %collective-permute-start.36 = (f32[8,6,16,128]{3,2,1,0:T(8,128)S(1)}, f32[8,6,16,128]{3,2,1,0:T(8,128)S(1)}, u32[]{:S(2)}, u32[]{:S(2)}) collective-permute-start(f32[8,6,16,128]{3,2,1,0:T(8,128)S(1)} %collective-permute-done.35.refs_6_), channel_id=1, source_target_pairs={{0,1},{1,0},{2,3},{3,2},{4,5},{5,4},{6,7},{7,6},{8,9},{9,8},{10,11... | collective-permute-start | bytes 1179656 | tf_op jit(solution)/shard_map/ppermute | solution.py:414
  439.8 13.7 %collective-permute-start.43 = (f32[8,6,16,128]{3,2,1,0:T(8,128)S(1)}, f32[8,6,16,128]{3,2,1,0:T(8,128)S(1)}, u32[]{:S(2)}, u32[]{:S(2)}) collective-permute-start(f32[8,6,16,128]{3,2,1,0:T(8,128)S(1)} %collective-permute-done.42.refs_14_), channel_id=1, source_target_pairs={{0,1},{1,0},{2,3},{3,2},{4,5},{5,4},{6,7},{7,6},{8,9},{9,8},{10,11... | collective-permute-start | bytes 1179656 | tf_op jit(solution)/shard_map/ppermute | solution.py:414
  442.3 57.0 %collective-permute-start.59 = (f32[16,8,16,128]{3,2,1,0:T(8,128)}, f32[16,8,16,128]{3,2,1,0:T(8,128)}, u32[]{:S(2)}, u32[]{:S(2)}) collective-permute-start(f32[16,8,16,128]{3,2,1,0:T(8,128)} %get-tuple-element.82), channel_id=1, source_target_pairs={{0,3},{1,2},{2,1},{3,0},{4,7},{5,6},{6,5},{7,4},{8,11},{9,10},{10,... | collective-permute-start | bytes 3145736 | tf_op jit(solution)/shard_map/ppermute | solution.py:414
  452.9 46.5 %collective-permute-start.60 = (f32[16,8,16,128]{3,2,1,0:T(8,128)}, f32[16,8,16,128]{3,2,1,0:T(8,128)}, u32[]{:S(2)}, u32[]{:S(2)}) collective-permute-start(f32[16,8,16,128]{3,2,1,0:T(8,128)} %get-tuple-element.83), channel_id=1, source_target_pairs={{0,4},{1,5},{2,6},{3,7},{4,0},{5,1},{6,2},{7,3},{8,12},{9,13},{10,... | collective-permute-start | bytes 3145736 | tf_op jit(solution)/shard_map/ppermute | solution.py:414
  453.4 46.4 %collective-permute-start.61 = (f32[16,8,16,128]{3,2,1,0:T(8,128)}, f32[16,8,16,128]{3,2,1,0:T(8,128)}, u32[]{:S(2)}, u32[]{:S(2)}) collective-permute-start(f32[16,8,16,128]{3,2,1,0:T(8,128)} %get-tuple-element.84), channel_id=1, source_target_pairs={{0,5},{1,4},{2,7},{3,6},{4,1},{5,0},{6,3},{7,2},{8,13},{9,12},{10,... | collective-permute-start | bytes 3145736 | tf_op jit(solution)/shard_map/ppermute | solution.py:414
  453.5 71.2 %collective-permute-start.62 = (f32[16,8,16,128]{3,2,1,0:T(8,128)}, f32[16,8,16,128]{3,2,1,0:T(8,128)}, u32[]{:S(2)}, u32[]{:S(2)}) collective-permute-start(f32[16,8,16,128]{3,2,1,0:T(8,128)} %get-tuple-element.85), channel_id=1, source_target_pairs={{0,6},{1,7},{2,4},{3,5},{4,2},{5,3},{6,0},{7,1},{8,14},{9,15},{10,... | collective-permute-start | bytes 3145736 | tf_op jit(solution)/shard_map/ppermute | solution.py:414
  455.5 86.5 %collective-permute-start.63 = (f32[16,8,16,128]{3,2,1,0:T(8,128)}, f32[16,8,16,128]{3,2,1,0:T(8,128)}, u32[]{:S(2)}, u32[]{:S(2)}) collective-permute-start(f32[16,8,16,128]{3,2,1,0:T(8,128)} %get-tuple-element.86), channel_id=1, source_target_pairs={{0,7},{1,6},{2,5},{3,4},{4,3},{5,2},{6,1},{7,0},{8,15},{9,14},{10,... | collective-permute-start | bytes 3145736 | tf_op jit(solution)/shard_map/ppermute | solution.py:414
  (49 other events, 1312.2 us)

commit v2 on v1

--- a/solution.py
+++ b/solution.py
@@ -300,14 +300,84 @@
             )
 
 
+def spread_lane(value, lane):
+    return jnp.broadcast_to(value[:, lane : lane + 1], value.shape)
+
+
+def spread_row(value, row):
+    return jnp.broadcast_to(value[row : row + 1, :], value.shape)
+
+
+def factor_block(matrix):
+    group = 8
+    count = BLK // group
+    shape = (group, BLK)
+    at_row = lax.broadcasted_iota(jnp.int32, shape, 0)
+    at_lane = lax.broadcasted_iota(jnp.int32, shape, 1)
+    left = [matrix[group * s : group * (s + 1), :] for s in range(count)]
+    right = [jnp.where(at_lane == at_row + group * s, 1.0, 0.0) for s in range(count)]
+    for s in range(count):
+        cols = {
+            t: [spread_lane(left[t], group * s + q) for q in range(group)] for t in range(s, count)
+        }
+        for o in range(group):
+            inverse = 1.0 / spread_row(cols[s][o], o)
+            scale = [spread_row(cols[s][q], o) * inverse for q in range(o + 1, group)]
+            row_left = spread_row(left[s], o) * inverse
+            row_right = spread_row(right[s], o) * inverse
+            for t in range(s, count):
+                col = cols[t][o]
+                if t == s:
+                    col = jnp.where(at_row > o, col, 0.0)
+                for q in range(o + 1, group):
+                    cols[t][q] = cols[t][q] - col * scale[q - o - 1]
+                left[t] = left[t] - col * row_left
+                right[t] = right[t] - col * row_right
+    for s in range(count):
+        pivots = jnp.sum(
+            jnp.where(at_lane == at_row + group * s, left[s], 0.0), axis=1, keepdims=True
+        )
+        root = lax.rsqrt(pivots)
+        root = root * (1.5 - 0.5 * pivots * root * root)
+        left[s] = jnp.where(at_lane >= at_row + group * s, left[s] * root, 0.0)
+        right[s] = right[s] * root
+    return jnp.concatenate(left, axis=0), jnp.concatenate(right, axis=0)
+
+
 def corner_kernel(plan, place_ref, *refs):
     parts = refs[: plan.plane]
-    out_ref = refs[plan.plane]
+    factor_ref, work = refs[plan.plane :]
     me = place_ref[0]
     for m, part in enumerate(parts):
         for block in range(NPIV):
-            for pivot in range(NPIV):
-                put_rows(out_ref, block * BLK, me ^ m, block_lanes(pivot), part[block, pivot])
+            for pivot in range(block + 1):
+                put_rows(work, block * BLK, me ^ m, block_lanes(pivot), part[block, pivot])
+    for block in range(NPIV):
+        for pivot in range(block):
+            work[block_lanes(pivot), block_lanes(block)] = work[
+                block_lanes(block), block_lanes(pivot)
+            ].T
+
+    exact = functools.partial(
+        lax.dot_general, precision=highest, preferred_element_type=jnp.float32
+    )
+    factor_ref[...] = jnp.zeros_like(factor_ref)
+
+    @pl.loop(0, NPIV)
+    def _(pivot):
+        here = pl.ds(pl.multiple_of(pivot * BLK, BLK), BLK)
+        upper, inverse = factor_block(work[here, here])
+        factor_ref[here, here] = upper.T
+        work[here, :] = exact(inverse, work[here, :], (((1,), (0,)), ((), ())))
+        work[here, here] = inverse
+
+        @pl.loop(pivot + 1, NPIV)
+        def _(block):
+            there = pl.ds(pl.multiple_of(block * BLK, BLK), BLK)
+            lower = work[here, there].T
+            factor_ref[there, here] = lower
+            work[there, here] = jnp.zeros((BLK, BLK), jnp.float32)
+            work[there, :] -= exact(lower, work[here, :], (((1,), (0,)), ((), ())))
 
 
 def halves(value):
@@ -508,18 +578,14 @@
 
     bits = [1 << b for b in range(plane.bit_length() - 1)][::-1]
     other = bits[1:2] + bits[:1] + bits[2:]
-    corner = pl.pallas_call(
+    factor, inverse = pl.pallas_call(
         functools.partial(corner_kernel, plan),
-        out_shape=jax.ShapeDtypeStruct((NPIV * BLK, NPIV * BLK), f32),
+        out_shape=[jax.ShapeDtypeStruct((NPIV * BLK, NPIV * BLK), f32)] * 2,
         in_specs=[smem] + [vmem] * plane,
-        out_specs=vmem,
+        out_specs=[vmem] * 2,
         compiler_params=params(),
         name="corner",
     )(place, *gather_plane(corner_part, plan, bits))
-    factor = jnp.tril(lax.linalg.cholesky(corner, symmetrize_input=False))
-    inverse = lax.linalg.triangular_solve(
-        factor, jnp.eye(NPIV * BLK, dtype=f32), left_side=True, lower=True
-    )
 
     lead_got = [lead_parts[0]] + [swap(lead_parts[m], plan, m) for m in range(1, plane)]
     lead_rows = pl.pallas_call(

time: 572 us -> 361 us (0.63); the launches traced: 561 us -> 362 us
  other arithmetic: 192 us -> 1.2 us
  Pallas kernels: 89.9 us -> 131 us
  local copies, waits for them, and re-layouts: 29.6 us -> 6.18 us
  matrix products: 23.3 us -> 0 us
  waiting for transfers between devices: 152 us -> 169 us
  starting transfers between devices: 68.4 us -> 54.4 us
    another operation x25 -> x0, other arithmetic: 189 us -> none  [the longest x22 126 us: body(): factor = jnp.tril(lax.linalg.cholesky(corner, symmetrize_input=False))]
    pallas_call x1, Pallas kernels: 3.17 us -> 39.9 us  [body(): pl.pallas_call(functools.partial(corner_kernel, plan), out_shape=[jax.Sha...]
    ppermute x12, waiting for transfers between devices: 59.6 us -> 92.1 us  [ring_gather(): lax.ppermute(held[-1], 'row', [(r, (r + 1) % plan.rows) for r in range(pl...]
    another operation x21 -> x0, matrix products: 23.3 us -> none  [the longest x11 13.5 us: body(): lax.linalg.triangular_solve(factor, jnp.eye(NPIV * BLK, dtype=f32), left_...]
    another operation x25 -> x0, local copies, waits for them, and re-layouts: 22.7 us -> none
    ppermute x42, waiting for transfers between devices: 84.7 us -> 74.8 us  [swap(): return lax.ppermute(value, PLANE, [(k, k ^ bit) for k in range(plan.plane)])]
    ppermute x12, starting transfers between devices: 12.1 us -> 2.57 us  [ring_gather(): lax.ppermute(held[-1], 'row', [(r, (r + 1) % plan.rows) for r in range(pl...]
    ppermute x7, waiting for transfers between devices: 6.99 us -> 0.02 us  [body(): lax.ppermute(front_cut[m], PLANE, [(k, k ^ m) for k in owners])]
  transfers between devices with their start and end apart: 64 -> 64, of which waited for: 21 -> 23; matrix products, arithmetic and copies ran while one was open for 43% -> 1% of each run, Pallas kernels for 12% -> 30%
where the time goes in v2:
time: 361 us; the launch traced here: 362 us
  waiting for transfers between devices  169 us (47%)
  Pallas kernels  131 us (36%)
  starting transfers between devices  54.4 us (15%)
  local copies, waits for them, and re-layouts  6.18 us (2%)
    ppermute x12, waiting for transfers between devices, ring_gather(): lax.ppermute(held[-1], 'row', [(r, (r + 1) % plan.rows) for r in range(pl...  92.1 us
    ppermute x42, waiting for transfers between devices, swap(): return lax.ppermute(value, PLANE, [(k, k ^ bit) for k in range(plan.plane)])  74.8 us
    pallas_call x1, Pallas kernels, body(): pl.pallas_call(functools.partial(corner_kernel, plan), out_shape=[jax.Sha...  39.9 us
    ppermute x42, starting transfers between devices, swap(): return lax.ppermute(value, PLANE, [(k, k ^ bit) for k in range(plan.plane)])  35.1 us
    pallas_call x1, Pallas kernels, body(): pl.pallas_call(functools.partial(left_kernel, plan, tile, half_steps), gr...  24.6 us
    pallas_call x1, Pallas kernels, body(): pl.pallas_call(functools.partial(schur_kernel, plan, tile), grid=(plan.ro...  18.8 us
    ppermute x7, starting transfers between devices, body(): lax.ppermute(front_cut[m], PLANE, [(k, k ^ m) for k in owners])  15.9 us
    pallas_call x1, Pallas kernels, body(): pl.pallas_call(functools.partial(spread_kernel, plan), out_shape=[jax.Sha...  14.1 us
  transfers between devices with their start and end apart: 64, of which 23 were waited for; matrix products, arithmetic and copies ran while one was open for 1% of the time, Pallas kernels for 30%

profile of v2, /device:TPU:0, one launch (start us, length us, event | category | flops | bytes accessed | tf_op | source)
XLA Modules:
  0.0 362.3 jit_solution(1608979043120222534)
XLA Ops:
  0.6 2.7 cut_child.1
  3.8 2.5 collective-permute-start.4
  6.4 1.7 collective-permute-start.6
  8.1 0.9 bitcast_dynamic-update-slice_fusion
  9.0 2.7 collective-permute-start.8
  11.7 1.6 collective-permute-start.9
  13.4 1.3 collective-permute-done.5
  14.7 1.8 collective-permute-done.7
  16.5 5.4 %collective-permute-done.8 = f32[20,16,128]{2,1,0:T(8,128)S(1)} collective-permute-done((f32[20,16,128]{2,1,0:T(8,128)}, f32[20,16,128]{2,1,0:T(8,128)S(1)}, u32[]{:S(2)}, u32[]{:S(2)}) %collective-permute-start.8) | collective-permute-done | bytes 163872 | tf_op jit(solution)/shard_map/ppermute | solution.py:484
  21.9 2.2 collective-permute-done.9
  24.1 1.6 collective-permute-start.10
  25.8 3.9 %cut_front.1 = (f32[16,3,16,128]{3,2,1,0:T(8,128)}, f32[16,3,16,128]{3,2,1,0:T(8,128)}, f32[16,3,16,128]{3,2,1,0:T(8,128)}, f32[16,3,16,128]{3,2,1,0:T(8,128)}, ...) custom-call(s32[4]{0:T(128)} %pad_add_fusion.1.place_ref, ...), custom_call_target="tpu_custom_call" | custom-call | tf_op jit(solution)/shard_map/cut_front/pallas_call | solution.py:534
  29.6 2.2 collective-permute-start.13
  31.9 1.3 collective-permute-start.14
  33.2 1.3 collective-permute-start.15
  34.5 3.4 collective-permute-start.16
  37.9 0.9 bitcast_dynamic-update-slice_fusion.1
  38.8 0.9 fusion.12
  39.7 4.8 %collective-permute-done.10.refs_1_ = f32[8,11,16,128]{3,2,1,0:T(8,128)S(1)} collective-permute-done((f32[8,11,16,128]{3,2,1,0:T(8,128)S(1)}, f32[8,11,16,128]{3,2,1,0:T(8,128)S(1)}, u32[]{:S(2)}, u32[]{:S(2)}) %collective-permute-start.10) | collective-permute-done | bytes 720928 | tf_op jit(solution)/shard_map/ppermute | solution.py:499
  44.6 1.0 fusion.8
  45.6 3.5 collective-permute-start.17
  49.1 2.1 collective-permute-start.18
  51.2 2.1 collective-permute-start.19
  53.2 10.9 %collective-permute-done.11.refs_2_ = f32[8,11,16,128]{3,2,1,0:T(8,128)S(1)} collective-permute-done((f32[8,11,16,128]{3,2,1,0:T(8,128)S(1)}, f32[8,11,16,128]{3,2,1,0:T(8,128)S(1)}, u32[]{:S(2)}, u32[]{:S(2)}) %collective-permute-start.11) | collective-permute-done | bytes 720928 | tf_op jit(solution)/shard_map/ppermute | solution.py:499
  64.3 3.9 %front_panel.1 = (f32[16,6,16,128]{3,2,1,0:T(8,128)}, f32[2,6,16,128]{3,2,1,0:T(8,128)}) custom-call(s32[4]{0:T(128)} %pad_add_fusion.1.place_ref, f32[16,3,16,128]{3,2,1,0:T(8,128)} %get-tuple-element.56.refs_0_, f32[16,3,16,128]{3,2,1,0:T(8,128)} %copy-done.19, f32[16,3,16,128]{3,2,1,0:T(8,128)} %copy-done.20, f32[16,3,16,128]{3,2,1,0:T(8,128)} %copy-done.21, ...), custom_call_target="tpu_custom_call" | custom-call | tf_op jit(solution)/shard_map/front_panel/pallas_call | solution.py:547
  68.9 28.7 %collective-permute-done.20.refs_5_ = f32[2,6,16,128]{3,2,1,0:T(8,128)S(1)} collective-permute-done((f32[2,6,16,128]{3,2,1,0:T(8,128)}, f32[2,6,16,128]{3,2,1,0:T(8,128)S(1)}, u32[]{:S(2)}, u32[]{:S(2)}) %collective-permute-start.20) | collective-permute-done | bytes 98336 | tf_op jit(solution)/shard_map/ppermute | solution.py:499
  98.5 2.2 collective-permute-done.2
  100.7 3.4 collective-permute-done.21.refs_6_
  104.7 6.8 %collective-permute-done.22.refs_7_ = f32[2,6,16,128]{3,2,1,0:T(8,128)S(1)} collective-permute-done((f32[2,6,16,128]{3,2,1,0:T(8,128)S(1)}, f32[2,6,16,128]{3,2,1,0:T(8,128)S(1)}, u32[]{:S(2)}, u32[]{:S(2)}) %collective-permute-start.22) | collective-permute-done | bytes 98336 | tf_op jit(solution)/shard_map/ppermute | solution.py:499
  112.5 9.3 %panel.1 = (f32[16,6,16,128]{3,2,1,0:T(8,128)}, f32[6,6,16,128]{3,2,1,0:T(8,128)}, f32[2,8,16,128]{3,2,1,0:T(8,128)}, f32[2,8,16,128]{3,2,1,0:T(8,128)}, f32[2,8...) custom-call(s32[4]{0:T(128)} %pad_add_fusion.1.place_ref, ...), custom_call_target="tpu_custom_call" | custom-call | tf_op jit(solution)/shard_map/panel/pallas_call | solution.py:560
  121.8 1.0 collective-permute-start.45
  122.9 0.8 collective-permute-start.46
  123.7 1.4 collective-permute-start.47
  125.4 3.0 collective-permute-done.45.refs_2_
  128.4 1.7 collective-permute-start.49
  130.3 1.8 collective-permute-start.50
  132.2 4.1 %collective-permute-done.49.refs_6_ = f32[2,8,16,128]{3,2,1,0:T(8,128)S(1)} collective-permute-done((f32[2,8,16,128]{3,2,1,0:T(8,128)}, f32[2,8,16,128]{3,2,1,0:T(8,128)S(1)}, u32[]{:S(2)}, u32[]{:S(2)}) %collective-permute-start.49) | collective-permute-done | bytes 131104 | tf_op jit(solution)/shard_map/ppermute | solution.py:484
  136.3 1.7 collective-permute-done.50.refs_7_
  138.6 3.1 lead_rows.1.refs_0_
  141.7 1.3 collective-permute-start.26
  143.1 1.3 collective-permute-start.24
  144.4 37.4 %collective-permute-done.56.refs_7_ = f32[8,9,16,128]{3,2,1,0:T(8,128)S(1)} collective-permute-done((f32[8,9,16,128]{3,2,1,0:T(8,128)}, f32[8,9,16,128]{3,2,1,0:T(8,128)S(1)}, u32[]{:S(2)}, u32[]{:S(2)}) %collective-permute-start.56) | collective-permute-done | bytes 589856 | tf_op jit(solution)/shard_map/ppermute | solution.py:499
  181.8 1.3 collective-permute-start.40
  183.1 1.3 collective-permute-start.38
  185.0 8.8 %collective-permute-done.40.refs_12_ = f32[8,6,16,128]{3,2,1,0:T(8,128)S(1)} collective-permute-done((f32[8,6,16,128]{3,2,1,0:T(8,128)S(1)}, f32[8,6,16,128]{3,2,1,0:T(8,128)S(1)}, u32[]{:S(2)}, u32[]{:S(2)}) %collective-permute-start.40) | collective-permute-done | bytes 393248 | tf_op jit(solution)/shard_map/ppermute | solution.py:484
  193.8 1.1 collective-permute-start.31
  194.9 1.0 collective-permute-start.28
  195.9 5.0 %collective-permute-done.33.refs_4_ = f32[8,6,16,128]{3,2,1,0:T(8,128)} collective-permute-done((f32[8,6,16,128]{3,2,1,0:T(8,128)S(1)}, f32[8,6,16,128]{3,2,1,0:T(8,128)}, u32[]{:S(2)}, u32[]{:S(2)}) %collective-permute-start.33) | collective-permute-done | bytes 393248 | tf_op jit(solution)/shard_map/ppermute | solution.py:484
  201.0 4.5 %collective-permute-done.31.refs_2_ = f32[8,6,16,128]{3,2,1,0:T(8,128)S(1)} collective-permute-done((f32[8,6,16,128]{3,2,1,0:T(8,128)S(1)}, f32[8,6,16,128]{3,2,1,0:T(8,128)S(1)}, u32[]{:S(2)}, u32[]{:S(2)}) %collective-permute-start.31) | collective-permute-done | bytes 393248 | tf_op jit(solution)/shard_map/ppermute | solution.py:484
  206.0 2.7 collective-permute-done.28.refs_6_
  208.7 1.3 collective-permute-start.42
  210.0 1.3 collective-permute-start.35
  212.3 14.1 %spread.1 = (f32[16,8,16,128]{3,2,1,0:T(8,128)}, f32[16,8,16,128]{3,2,1,0:T(8,128)}, f32[16,8,16,128]{3,2,1,0:T(8,128)}, f32[16,8,16,128]{3,2,1,0:T(8,128)}, f32...) custom-call(s32[4]{0:T(128)} %pad_add_fusion.1.place_ref, ...), custom_call_target="tpu_custom_call" | custom-call | tf_op jit(solution)/shard_map/spread/pallas_call | solution.py:652
  226.9 0.8 collective-permute-start.58
  228.3 1.7 collective-permute-done.32.refs_3_
  230.7 0.9 collective-permute-start.59
  231.6 21.6 %collective-permute-done.58.refs_2_ = f32[16,8,16,128]{3,2,1,0:T(8,128)S(1)} collective-permute-done((f32[16,8,16,128]{3,2,1,0:T(8,128)}, f32[16,8,16,128]{3,2,1,0:T(8,128)S(1)}, u32[]{:S(2)}, u32[]{:S(2)}) %collective-permute-start.58) | collective-permute-done | bytes 1048608 | tf_op jit(solution)/shard_map/ppermute | solution.py:484
  253.8 1.7 collective-permute-start.62
  255.5 2.2 collective-permute-start.63
  257.6 39.9 %corner.1 = (f32[768,768]{1,0:T(8,128)}, f32[768,768]{1,0:T(8,128)}) custom-call(s32[4]{0:T(128)} %pad_add_fusion.1.place_ref, f32[6,6,16,128]{3,2,1,0:T(8,128)} %get-tuple-element.66.refs_0_, f32[6,6,16,128]{3,2,1,0:T(8,128)} %copy-done.25, f32[6,6,16,128]{3,2,1,0:T(8,128)} %copy-done.24, f32[6,6,16,128]{3,2,1,0:T(8,128)} %copy-done.27, ...), custom_call_target="tpu_custom_call" | custom-call | tf_op jit(solution)/shard_map/corner/pallas_call | solution.py:581
  297.6 24.6 %left_factor.1 = (bf16[2048,768]{1,0:T(8,128)(2,1)}, bf16[2048,768]{1,0:T(8,128)(2,1)}, f32[2048,384]{1,0:T(8,128)}) custom-call(s32[4]{0:T(128)} %pad_add_fusion.1.place_ref, f32[768,768]{1,0:T(8,128)} %get-tuple-element.67.inverse_ref, f32[768,768]{1,0:T(8,128)} %get-tuple-element.68.factor_ref, f32[8,6,16,128]{3,2,1,0:T(8,128)} %copy-done.5, ...), custom_call_target="tpu_custom_call" | custom-call | tf_op jit(solution)/shard_map/left_factor/pallas_call | solution.py:618
  322.2 10.5 %right_factor.1 = (bf16[768,1024]{1,0:T(8,128)(2,1)}, bf16[768,1024]{1,0:T(8,128)(2,1)}) custom-call(s32[4]{0:T(128)} %pad_add_fusion.1.place_ref, f32[768,768]{1,0:T(8,128)} %get-tuple-element.67.inverse_ref, f32[2,128,1024]{2,1,0:T(8,128)} %lead_rows.1.refs_0_, f32[2,128,1024]{2,1,0:T(8,128)} %copy-done.9, ...), custom_call_target="tpu_custom_call" | custom-call | tf_op jit(solution)/shard_map/right_factor/pallas_call | solution.py:603
  332.7 10.6 %collective-permute-done.63.refs_7_ = f32[16,8,16,128]{3,2,1,0:T(8,128)} collective-permute-done((f32[16,8,16,128]{3,2,1,0:T(8,128)}, f32[16,8,16,128]{3,2,1,0:T(8,128)}, u32[]{:S(2)}, u32[]{:S(2)}) %collective-permute-start.63) | collective-permute-done | bytes 1048608 | tf_op jit(solution)/shard_map/ppermute | solution.py:484
  343.3 18.8 %schur.1 = f32[2048,1024]{1,0:T(8,128)} custom-call(s32[4]{0:T(128)} %pad_add_fusion.1.place_ref, f32[2048,1024]{1,0:T(8,128)} %front_ref.5, bf16[2048,768]{1,0:T(8,128)(2,1)} %get-tuple-element.70.high_ref, bf16[2048,768]{1,0:T(8,128)(2,1)} %get-tuple-element.71.low_ref, f32[2048,384]{1,0:T(8,128)} %get-tuple-element.72.own_ref, ...), custom_call_target="tpu_custom_call" | custom-call | tf_op jit(solution)/shard_map/schur/pallas_call | solution.py:671
  (177 shorter events, 10.4 us)
Async XLA Ops:
  3.3 5.7 %collective-permute-start.3 = (f32[20,16,128]{2,1,0:T(8,128)}, f32[20,16,128]{2,1,0:T(8,128)S(1)}, u32[]{:S(2)}, u32[]{:S(2)}) collective-permute-start(f32[20,16,128]{2,1,0:T(8,128)} %get-tuple-element.49), channel_id=1, source_target_pairs={{0,1},{1,0},{2,3},{3,2},{4,5},{5,4},{6,7},{7,6},{8,9},{9,8},{10,11... | collective-permute-start | bytes 491528 | tf_op jit(solution)/shard_map/ppermute | solution.py:484
  3.8 7.9 %collective-permute-start.4 = (f32[20,16,128]{2,1,0:T(8,128)}, f32[20,16,128]{2,1,0:T(8,128)S(1)}, u32[]{:S(2)}, u32[]{:S(2)}) collective-permute-start(f32[20,16,128]{2,1,0:T(8,128)} %get-tuple-element.50), channel_id=1, source_target_pairs={{0,2},{1,3},{2,0},{3,1},{4,6},{5,7},{6,4},{7,5},{8,10},{9,11},{10,... | collective-permute-start | bytes 491528 | tf_op jit(solution)/shard_map/ppermute | solution.py:484
  6.3 8.4 %collective-permute-start.5 = (f32[20,16,128]{2,1,0:T(8,128)}, f32[20,16,128]{2,1,0:T(8,128)S(1)}, u32[]{:S(2)}, u32[]{:S(2)}) collective-permute-start(f32[20,16,128]{2,1,0:T(8,128)} %get-tuple-element.51), channel_id=1, source_target_pairs={{0,3},{1,2},{2,1},{3,0},{4,7},{5,6},{6,5},{7,4},{8,11},{9,10},{10,... | collective-permute-start | bytes 491528 | tf_op jit(solution)/shard_map/ppermute | solution.py:484
  6.4 8.3 %collective-permute-start.6 = (f32[20,16,128]{2,1,0:T(8,128)}, f32[20,16,128]{2,1,0:T(8,128)S(1)}, u32[]{:S(2)}, u32[]{:S(2)}) collective-permute-start(f32[20,16,128]{2,1,0:T(8,128)} %get-tuple-element.52), channel_id=1, source_target_pairs={{0,4},{1,5},{2,6},{3,7},{4,0},{5,1},{6,2},{7,3},{8,12},{9,13},{10,... | collective-permute-start | bytes 491528 | tf_op jit(solution)/shard_map/ppermute | solution.py:484
  8.1 8.4 %collective-permute-start.7 = (f32[20,16,128]{2,1,0:T(8,128)}, f32[20,16,128]{2,1,0:T(8,128)S(1)}, u32[]{:S(2)}, u32[]{:S(2)}) collective-permute-start(f32[20,16,128]{2,1,0:T(8,128)} %get-tuple-element.53), channel_id=1, source_target_pairs={{0,5},{1,4},{2,7},{3,6},{4,1},{5,0},{6,3},{7,2},{8,13},{9,12},{10,... | collective-permute-start | bytes 491528 | tf_op jit(solution)/shard_map/ppermute | solution.py:484
  9.0 12.8 %collective-permute-start.8 = (f32[20,16,128]{2,1,0:T(8,128)}, f32[20,16,128]{2,1,0:T(8,128)S(1)}, u32[]{:S(2)}, u32[]{:S(2)}) collective-permute-start(f32[20,16,128]{2,1,0:T(8,128)} %get-tuple-element.54), channel_id=1, source_target_pairs={{0,6},{1,7},{2,4},{3,5},{4,2},{5,3},{6,0},{7,1},{8,14},{9,15},{10,... | collective-permute-start | bytes 491528 | tf_op jit(solution)/shard_map/ppermute | solution.py:484
  11.7 12.4 %collective-permute-start.9 = (f32[20,16,128]{2,1,0:T(8,128)}, f32[20,16,128]{2,1,0:T(8,128)S(1)}, u32[]{:S(2)}, u32[]{:S(2)}) collective-permute-start(f32[20,16,128]{2,1,0:T(8,128)} %get-tuple-element.55), channel_id=1, source_target_pairs={{0,7},{1,6},{2,5},{3,4},{4,3},{5,2},{6,1},{7,0},{8,15},{9,14},{10,... | collective-permute-start | bytes 491528 | tf_op jit(solution)/shard_map/ppermute | solution.py:484
  24.1 20.4 %collective-permute-start.10 = (f32[8,11,16,128]{3,2,1,0:T(8,128)S(1)}, f32[8,11,16,128]{3,2,1,0:T(8,128)S(1)}, u32[]{:S(2)}, u32[]{:S(2)}) collective-permute-start(f32[8,11,16,128]{3,2,1,0:T(8,128)S(1)} %fusion.refs_0_), channel_id=1, source_target_pairs={{0,8},{8,16},{16,24},{24,0},{1,9},{9,17},{17,25},{25,1},{2,10},{10... | collective-permute-start | bytes 2162696 | tf_op jit(solution)/shard_map/ppermute | solution.py:499
  29.6 15.9 %collective-permute-start.13 = (f32[16,3,16,128]{3,2,1,0:T(8,128)}, f32[16,3,16,128]{3,2,1,0:T(8,128)S(1)}, u32[]{:S(2)}, u32[]{:S(2)}) collective-permute-start(f32[16,3,16,128]{3,2,1,0:T(8,128)} %get-tuple-element.57), channel_id=1, source_target_pairs={{0,1},{4,5},{8,9},{12,13},{16,17},{20,21},{24,25},{28,29}} | collective-permute-start | bytes 1179656 | tf_op jit(solution)/shard_map/ppermute | solution.py:545
  31.9 17.2 %collective-permute-start.14 = (f32[16,3,16,128]{3,2,1,0:T(8,128)}, f32[16,3,16,128]{3,2,1,0:T(8,128)S(1)}, u32[]{:S(2)}, u32[]{:S(2)}) collective-permute-start(f32[16,3,16,128]{3,2,1,0:T(8,128)} %get-tuple-element.58), channel_id=1, source_target_pairs={{0,2},{4,6},{8,10},{12,14},{16,18},{20,22},{24,26},{28,30}} | collective-permute-start | bytes 1179656 | tf_op jit(solution)/shard_map/ppermute | solution.py:545
  33.2 18.0 %collective-permute-start.15 = (f32[16,3,16,128]{3,2,1,0:T(8,128)}, f32[16,3,16,128]{3,2,1,0:T(8,128)S(1)}, u32[]{:S(2)}, u32[]{:S(2)}) collective-permute-start(f32[16,3,16,128]{3,2,1,0:T(8,128)} %get-tuple-element.59), channel_id=1, source_target_pairs={{0,3},{4,7},{8,11},{12,15},{16,19},{20,23},{24,27},{28,31}} | collective-permute-start | bytes 1179656 | tf_op jit(solution)/shard_map/ppermute | solution.py:545
  34.5 29.7 %collective-permute-start.16 = (f32[16,3,16,128]{3,2,1,0:T(8,128)}, f32[16,3,16,128]{3,2,1,0:T(8,128)}, u32[]{:S(2)}, u32[]{:S(2)}) collective-permute-start(f32[16,3,16,128]{3,2,1,0:T(8,128)} %get-tuple-element.60), channel_id=1, source_target_pairs={{0,4},{4,0},{8,12},{12,8},{16,20},{20,16},{24,28},{28,24}} | collective-permute-start | bytes 1179656 | tf_op jit(solution)/shard_map/ppermute | solution.py:545
  44.5 19.6 %collective-permute-start.11 = (f32[8,11,16,128]{3,2,1,0:T(8,128)S(1)}, f32[8,11,16,128]{3,2,1,0:T(8,128)S(1)}, u32[]{:S(2)}, u32[]{:S(2)}) collective-permute-start(f32[8,11,16,128]{3,2,1,0:T(8,128)S(1)} %collective-permute-done.10.refs_1_), channel_id=1, source_target_pairs={{0,8},{8,16},{16,24},{24,0},{1,9},{9,17},{17,25},{25,1},{2,10},{10... | collective-permute-start | bytes 2162696 | tf_op jit(solution)/shard_map/ppermute | solution.py:499
  45.6 18.7 %collective-permute-start.17 = (f32[16,3,16,128]{3,2,1,0:T(8,128)}, f32[16,3,16,128]{3,2,1,0:T(8,128)}, u32[]{:S(2)}, u32[]{:S(2)}) collective-permute-start(f32[16,3,16,128]{3,2,1,0:T(8,128)} %get-tuple-element.61), channel_id=1, source_target_pairs={{0,5},{4,1},{8,13},{12,9},{16,21},{20,17},{24,29},{28,25}} | collective-permute-start | bytes 1179656 | tf_op jit(solution)/shard_map/ppermute | solution.py:545
  49.1 15.2 %collective-permute-start.18 = (f32[16,3,16,128]{3,2,1,0:T(8,128)}, f32[16,3,16,128]{3,2,1,0:T(8,128)}, u32[]{:S(2)}, u32[]{:S(2)}) collective-permute-start(f32[16,3,16,128]{3,2,1,0:T(8,128)} %get-tuple-element.62), channel_id=1, source_target_pairs={{0,6},{4,2},{8,14},{12,10},{16,22},{20,18},{24,30},{28,26}} | collective-permute-start | bytes 1179656 | tf_op jit(solution)/shard_map/ppermute | solution.py:545
  51.2 13.1 %collective-permute-start.19 = (f32[16,3,16,128]{3,2,1,0:T(8,128)}, f32[16,3,16,128]{3,2,1,0:T(8,128)}, u32[]{:S(2)}, u32[]{:S(2)}) collective-permute-start(f32[16,3,16,128]{3,2,1,0:T(8,128)} %get-tuple-element.63), channel_id=1, source_target_pairs={{0,7},{4,3},{8,15},{12,11},{16,23},{20,19},{24,31},{28,27}} | collective-permute-start | bytes 1179656 | tf_op jit(solution)/shard_map/ppermute | solution.py:545
  64.1 47.4 %collective-permute-start.12 = (f32[8,11,16,128]{3,2,1,0:T(8,128)S(1)}, f32[8,11,16,128]{3,2,1,0:T(8,128)S(1)}, u32[]{:S(2)}, u32[]{:S(2)}) collective-permute-start(f32[8,11,16,128]{3,2,1,0:T(8,128)S(1)} %collective-permute-done.11.refs_2_), channel_id=1, source_target_pairs={{0,8},{8,16},{16,24},{24,0},{1,9},{9,17},{17,25},{25,1},{2,10},{10... | collective-permute-start | bytes 2162696 | tf_op jit(solution)/shard_map/ppermute | solution.py:499
  64.2 39.9 %collective-permute-start.54 = (f32[8,9,16,128]{3,2,1,0:T(8,128)S(1)}, f32[8,9,16,128]{3,2,1,0:T(8,128)}, u32[]{:S(2)}, u32[]{:S(2)}) collective-permute-start(f32[8,9,16,128]{3,2,1,0:T(8,128)S(1)} %fusion.7.refs_4_), channel_id=1, source_target_pairs={{0,8},{8,16},{16,24},{24,0},{1,9},{9,17},{17,25},{25,1},{2,10},{10... | collective-permute-start | bytes 1769480 | tf_op jit(solution)/shard_map/ppermute | solution.py:499
  68.2 29.4 %collective-permute-start.20 = (f32[2,6,16,128]{3,2,1,0:T(8,128)}, f32[2,6,16,128]{3,2,1,0:T(8,128)S(1)}, u32[]{:S(2)}, u32[]{:S(2)}) collective-permute-start(f32[2,6,16,128]{3,2,1,0:T(8,128)} %get-tuple-element.64.refs_4_), channel_id=1, source_target_pairs={{0,8},{8,16},{16,24},{24,0},{1,9},{9,17},{17,25},{25,1},{2,10},{10... | collective-permute-start | bytes 294920 | tf_op jit(solution)/shard_map/ppermute | solution.py:499
  97.6 6.4 %collective-permute-start.21 = (f32[2,6,16,128]{3,2,1,0:T(8,128)S(1)}, f32[2,6,16,128]{3,2,1,0:T(8,128)S(1)}, u32[]{:S(2)}, u32[]{:S(2)}) collective-permute-start(f32[2,6,16,128]{3,2,1,0:T(8,128)S(1)} %collective-permute-done.20.refs_5_), channel_id=1, source_target_pairs={{0,8},{8,16},{16,24},{24,0},{1,9},{9,17},{17,25},{25,1},{2,10},{10... | collective-permute-start | bytes 294920 | tf_op jit(solution)/shard_map/ppermute | solution.py:499
  97.6 3.0 collective-permute-start.2
  97.7 6.4 %collective-permute-start.1 = (s32[16]{0:T(128)S(1)}, s32[16]{0:T(128)S(1)}, u32[]{:S(2)}, u32[]{:S(2)}) collective-permute-start(s32[16]{0:T(128)S(1)} %bitcast.69), channel_id=1, source_target_pairs={{0,2},{1,3},{2,0},{3,1},{4,6},{5,7},{6,4},{7,5},{8,10},{9,11},{10,... | collective-permute-start | bytes 200 | tf_op jit(solution)/shard_map/ppermute | solution.py:517
  100.6 3.5 collective-permute-start
  104.0 7.5 %collective-permute-start.22 = (f32[2,6,16,128]{3,2,1,0:T(8,128)S(1)}, f32[2,6,16,128]{3,2,1,0:T(8,128)S(1)}, u32[]{:S(2)}, u32[]{:S(2)}) collective-permute-start(f32[2,6,16,128]{3,2,1,0:T(8,128)S(1)} %collective-permute-done.21.refs_6_), channel_id=1, source_target_pairs={{0,8},{8,16},{16,24},{24,0},{1,9},{9,17},{17,25},{25,1},{2,10},{10... | collective-permute-start | bytes 294920 | tf_op jit(solution)/shard_map/ppermute | solution.py:499
  104.0 37.6 %collective-permute-start.55 = (f32[8,9,16,128]{3,2,1,0:T(8,128)}, f32[8,9,16,128]{3,2,1,0:T(8,128)}, u32[]{:S(2)}, u32[]{:S(2)}) collective-permute-start(f32[8,9,16,128]{3,2,1,0:T(8,128)} %collective-permute-done.54.refs_5_), channel_id=1, source_target_pairs={{0,8},{8,16},{16,24},{24,0},{1,9},{9,17},{17,25},{25,1},{2,10},{10... | collective-permute-start | bytes 1769480 | tf_op jit(solution)/shard_map/ppermute | solution.py:499
  121.8 3.4 collective-permute-start.44
  121.8 6.6 %collective-permute-start.45 = (f32[2,8,16,128]{3,2,1,0:T(8,128)}, f32[2,8,16,128]{3,2,1,0:T(8,128)S(1)}, u32[]{:S(2)}, u32[]{:S(2)}) collective-permute-start(f32[2,8,16,128]{3,2,1,0:T(8,128)} %get-tuple-element.75), channel_id=1, source_target_pairs={{0,2},{1,3},{2,0},{3,1},{4,6},{5,7},{6,4},{7,5},{8,10},{9,11},{10,... | collective-permute-start | bytes 393224 | tf_op jit(solution)/shard_map/ppermute | solution.py:484
  122.9 7.4 %collective-permute-start.46 = (f32[2,8,16,128]{3,2,1,0:T(8,128)}, f32[2,8,16,128]{3,2,1,0:T(8,128)S(1)}, u32[]{:S(2)}, u32[]{:S(2)}) collective-permute-start(f32[2,8,16,128]{3,2,1,0:T(8,128)} %get-tuple-element.76), channel_id=1, source_target_pairs={{0,3},{1,2},{2,1},{3,0},{4,7},{5,6},{6,5},{7,4},{8,11},{9,10},{10,... | collective-permute-start | bytes 393224 | tf_op jit(solution)/shard_map/ppermute | solution.py:484
  123.7 8.5 %collective-permute-start.47 = (f32[2,8,16,128]{3,2,1,0:T(8,128)}, f32[2,8,16,128]{3,2,1,0:T(8,128)S(1)}, u32[]{:S(2)}, u32[]{:S(2)}) collective-permute-start(f32[2,8,16,128]{3,2,1,0:T(8,128)} %get-tuple-element.77), channel_id=1, source_target_pairs={{0,4},{1,5},{2,6},{3,7},{4,0},{5,1},{6,2},{7,3},{8,12},{9,13},{10,... | collective-permute-start | bytes 393224 | tf_op jit(solution)/shard_map/ppermute | solution.py:484
  125.2 7.0 %collective-permute-start.48 = (f32[2,8,16,128]{3,2,1,0:T(8,128)}, f32[2,8,16,128]{3,2,1,0:T(8,128)S(1)}, u32[]{:S(2)}, u32[]{:S(2)}) collective-permute-start(f32[2,8,16,128]{3,2,1,0:T(8,128)} %get-tuple-element.78), channel_id=1, source_target_pairs={{0,5},{1,4},{2,7},{3,6},{4,1},{5,0},{6,3},{7,2},{8,13},{9,12},{10,... | collective-permute-start | bytes 393224 | tf_op jit(solution)/shard_map/ppermute | solution.py:484
  128.4 7.8 %collective-permute-start.49 = (f32[2,8,16,128]{3,2,1,0:T(8,128)}, f32[2,8,16,128]{3,2,1,0:T(8,128)S(1)}, u32[]{:S(2)}, u32[]{:S(2)}) collective-permute-start(f32[2,8,16,128]{3,2,1,0:T(8,128)} %get-tuple-element.79), channel_id=1, source_target_pairs={{0,6},{1,7},{2,4},{3,5},{4,2},{5,3},{6,0},{7,1},{8,14},{9,15},{10,... | collective-permute-start | bytes 393224 | tf_op jit(solution)/shard_map/ppermute | solution.py:484
  130.3 7.6 %collective-permute-start.50 = (f32[2,8,16,128]{3,2,1,0:T(8,128)}, f32[2,8,16,128]{3,2,1,0:T(8,128)S(1)}, u32[]{:S(2)}, u32[]{:S(2)}) collective-permute-start(f32[2,8,16,128]{3,2,1,0:T(8,128)} %get-tuple-element.80), channel_id=1, source_target_pairs={{0,7},{1,6},{2,5},{3,4},{4,3},{5,2},{6,1},{7,0},{8,15},{9,14},{10,... | collective-permute-start | bytes 393224 | tf_op jit(solution)/shard_map/ppermute | solution.py:484
  141.7 43.3 %collective-permute-start.51 = (f32[2,128,1024]{2,1,0:T(8,128)}, f32[2,128,1024]{2,1,0:T(8,128)S(1)}, u32[]{:S(2)}, u32[]{:S(2)}) collective-permute-start(f32[2,128,1024]{2,1,0:T(8,128)} %lead_rows.1.refs_0_), channel_id=1, source_target_pairs={{0,8},{8,16},{16,24},{24,0},{1,9},{9,17},{17,25},{25,1},{2,10},{10... | collective-permute-start | bytes 3145736 | tf_op jit(solution)/shard_map/ppermute | solution.py:499
  141.7 40.1 %collective-permute-start.56 = (f32[8,9,16,128]{3,2,1,0:T(8,128)}, f32[8,9,16,128]{3,2,1,0:T(8,128)S(1)}, u32[]{:S(2)}, u32[]{:S(2)}) collective-permute-start(f32[8,9,16,128]{3,2,1,0:T(8,128)} %collective-permute-done.55.refs_6_), channel_id=1, source_target_pairs={{0,8},{8,16},{16,24},{24,0},{1,9},{9,17},{17,25},{25,1},{2,10},{10... | collective-permute-start | bytes 1769480 | tf_op jit(solution)/shard_map/ppermute | solution.py:499
  141.7 41.3 %collective-permute-start.26 = (f32[6,6,16,128]{3,2,1,0:T(8,128)S(1)}, f32[6,6,16,128]{3,2,1,0:T(8,128)S(1)}, u32[]{:S(2)}, u32[]{:S(2)}) collective-permute-start(f32[6,6,16,128]{3,2,1,0:T(8,128)S(1)} %copy-done.22), channel_id=1, source_target_pairs={{0,4},{1,5},{2,6},{3,7},{4,0},{5,1},{6,2},{7,3},{8,12},{9,13},{10,... | collective-permute-start | bytes 884744 | tf_op jit(solution)/shard_map/ppermute | solution.py:484
  143.1 41.3 %collective-permute-start.24 = (f32[6,6,16,128]{3,2,1,0:T(8,128)S(1)}, f32[6,6,16,128]{3,2,1,0:T(8,128)S(1)}, u32[]{:S(2)}, u32[]{:S(2)}) collective-permute-start(f32[6,6,16,128]{3,2,1,0:T(8,128)S(1)} %copy-done.22), channel_id=1, source_target_pairs={{0,2},{1,3},{2,0},{3,1},{4,6},{5,7},{6,4},{7,5},{8,10},{9,11},{10,... | collective-permute-start | bytes 884744 | tf_op jit(solution)/shard_map/ppermute | solution.py:484
  144.3 40.0 %collective-permute-start.23 = (f32[6,6,16,128]{3,2,1,0:T(8,128)S(1)}, f32[6,6,16,128]{3,2,1,0:T(8,128)S(1)}, u32[]{:S(2)}, u32[]{:S(2)}) collective-permute-start(f32[6,6,16,128]{3,2,1,0:T(8,128)S(1)} %copy-done.22), channel_id=1, source_target_pairs={{0,1},{1,0},{2,3},{3,2},{4,5},{5,4},{6,7},{7,6},{8,9},{9,8},{10,11... | collective-permute-start | bytes 884744 | tf_op jit(solution)/shard_map/ppermute | solution.py:484
  181.8 12.0 %collective-permute-start.40 = (f32[8,6,16,128]{3,2,1,0:T(8,128)S(1)}, f32[8,6,16,128]{3,2,1,0:T(8,128)S(1)}, u32[]{:S(2)}, u32[]{:S(2)}) collective-permute-start(f32[8,6,16,128]{3,2,1,0:T(8,128)S(1)} %get-tuple-element.91.refs_8_), channel_id=1, source_target_pairs={{0,4},{1,5},{2,6},{3,7},{4,0},{5,1},{6,2},{7,3},{8,12},{9,13},{10,... | collective-permute-start | bytes 1179656 | tf_op jit(solution)/shard_map/ppermute | solution.py:484
  183.1 11.8 %collective-permute-start.38 = (f32[8,6,16,128]{3,2,1,0:T(8,128)S(1)}, f32[8,6,16,128]{3,2,1,0:T(8,128)}, u32[]{:S(2)}, u32[]{:S(2)}) collective-permute-start(f32[8,6,16,128]{3,2,1,0:T(8,128)S(1)} %get-tuple-element.91.refs_8_), channel_id=1, source_target_pairs={{0,2},{1,3},{2,0},{3,1},{4,6},{5,7},{6,4},{7,5},{8,10},{9,11},{10,... | collective-permute-start | bytes 1179656 | tf_op jit(solution)/shard_map/ppermute | solution.py:484
  184.3 10.6 %collective-permute-start.37 = (f32[8,6,16,128]{3,2,1,0:T(8,128)S(1)}, f32[8,6,16,128]{3,2,1,0:T(8,128)S(1)}, u32[]{:S(2)}, u32[]{:S(2)}) collective-permute-start(f32[8,6,16,128]{3,2,1,0:T(8,128)S(1)} %get-tuple-element.91.refs_8_), channel_id=1, source_target_pairs={{0,1},{1,0},{2,3},{3,2},{4,5},{5,4},{6,7},{7,6},{8,9},{9,8},{10,11... | collective-permute-start | bytes 1179656 | tf_op jit(solution)/shard_map/ppermute | solution.py:484
  184.3 16.6 %collective-permute-start.33 = (f32[8,6,16,128]{3,2,1,0:T(8,128)S(1)}, f32[8,6,16,128]{3,2,1,0:T(8,128)}, u32[]{:S(2)}, u32[]{:S(2)}) collective-permute-start(f32[8,6,16,128]{3,2,1,0:T(8,128)S(1)} %get-tuple-element.92.refs_0_), channel_id=1, source_target_pairs={{0,4},{1,5},{2,6},{3,7},{4,0},{5,1},{6,2},{7,3},{8,12},{9,13},{10,... | collective-permute-start | bytes 1179656 | tf_op jit(solution)/shard_map/ppermute | solution.py:484
  185.0 42.7 %collective-permute-start.52 = (f32[2,128,1024]{2,1,0:T(8,128)S(1)}, f32[2,128,1024]{2,1,0:T(8,128)}, u32[]{:S(2)}, u32[]{:S(2)}) collective-permute-start(f32[2,128,1024]{2,1,0:T(8,128)S(1)} %collective-permute-done.51.refs_1_), channel_id=1, source_target_pairs={{0,8},{8,16},{16,24},{24,0},{1,9},{9,17},{17,25},{25,1},{2,10},{10... | collective-permute-start | bytes 3145736 | tf_op jit(solution)/shard_map/ppermute | solution.py:499
  193.8 11.7 %collective-permute-start.31 = (f32[8,6,16,128]{3,2,1,0:T(8,128)S(1)}, f32[8,6,16,128]{3,2,1,0:T(8,128)S(1)}, u32[]{:S(2)}, u32[]{:S(2)}) collective-permute-start(f32[8,6,16,128]{3,2,1,0:T(8,128)S(1)} %get-tuple-element.92.refs_0_), channel_id=1, source_target_pairs={{0,2},{1,3},{2,0},{3,1},{4,6},{5,7},{6,4},{7,5},{8,10},{9,11},{10,... | collective-permute-start | bytes 1179656 | tf_op jit(solution)/shard_map/ppermute | solution.py:484
  194.9 10.6 %collective-permute-start.30 = (f32[8,6,16,128]{3,2,1,0:T(8,128)S(1)}, f32[8,6,16,128]{3,2,1,0:T(8,128)S(1)}, u32[]{:S(2)}, u32[]{:S(2)}) collective-permute-start(f32[8,6,16,128]{3,2,1,0:T(8,128)S(1)} %get-tuple-element.92.refs_0_), channel_id=1, source_target_pairs={{0,1},{1,0},{2,3},{3,2},{4,5},{5,4},{6,7},{7,6},{8,9},{9,8},{10,11... | collective-permute-start | bytes 1179656 | tf_op jit(solution)/shard_map/ppermute | solution.py:484
  194.9 13.8 %collective-permute-start.28 = (f32[6,6,16,128]{3,2,1,0:T(8,128)S(1)}, f32[6,6,16,128]{3,2,1,0:T(8,128)}, u32[]{:S(2)}, u32[]{:S(2)}) collective-permute-start(f32[6,6,16,128]{3,2,1,0:T(8,128)S(1)} %collective-permute-done.26.refs_4_), channel_id=1, source_target_pairs={{0,2},{1,3},{2,0},{3,1},{4,6},{5,7},{6,4},{7,5},{8,10},{9,11},{10,... | collective-permute-start | bytes 884744 | tf_op jit(solution)/shard_map/ppermute | solution.py:484
  201.0 9.0 %collective-permute-start.27 = (f32[6,6,16,128]{3,2,1,0:T(8,128)S(1)}, f32[6,6,16,128]{3,2,1,0:T(8,128)S(1)}, u32[]{:S(2)}, u32[]{:S(2)}) collective-permute-start(f32[6,6,16,128]{3,2,1,0:T(8,128)S(1)} %collective-permute-done.26.refs_4_), channel_id=1, source_target_pairs={{0,1},{1,0},{2,3},{3,2},{4,5},{5,4},{6,7},{7,6},{8,9},{9,8},{10,11... | collective-permute-start | bytes 884744 | tf_op jit(solution)/shard_map/ppermute | solution.py:484
  205.5 4.5 %collective-permute-start.25 = (f32[6,6,16,128]{3,2,1,0:T(8,128)S(1)}, f32[6,6,16,128]{3,2,1,0:T(8,128)S(1)}, u32[]{:S(2)}, u32[]{:S(2)}) collective-permute-start(f32[6,6,16,128]{3,2,1,0:T(8,128)S(1)} %collective-permute-done.24.refs_2_), channel_id=1, source_target_pairs={{0,1},{1,0},{2,3},{3,2},{4,5},{5,4},{6,7},{7,6},{8,9},{9,8},{10,11... | collective-permute-start | bytes 884744 | tf_op jit(solution)/shard_map/ppermute | solution.py:484
  205.5 5.9 %collective-permute-start.41 = (f32[8,6,16,128]{3,2,1,0:T(8,128)S(1)}, f32[8,6,16,128]{3,2,1,0:T(8,128)S(1)}, u32[]{:S(2)}, u32[]{:S(2)}) collective-permute-start(f32[8,6,16,128]{3,2,1,0:T(8,128)S(1)} %collective-permute-done.40.refs_12_), channel_id=1, source_target_pairs={{0,1},{1,0},{2,3},{3,2},{4,5},{5,4},{6,7},{7,6},{8,9},{9,8},{10,11... | collective-permute-start | bytes 1179656 | tf_op jit(solution)/shard_map/ppermute | solution.py:484
  208.7 17.7 %collective-permute-start.42 = (f32[8,6,16,128]{3,2,1,0:T(8,128)}, f32[8,6,16,128]{3,2,1,0:T(8,128)}, u32[]{:S(2)}, u32[]{:S(2)}) collective-permute-start(f32[8,6,16,128]{3,2,1,0:T(8,128)} %collective-permute-done.38.refs_10_), channel_id=1, source_target_pairs={{0,4},{1,5},{2,6},{3,7},{4,0},{5,1},{6,2},{7,3},{8,12},{9,13},{10,... | collective-permute-start | bytes 1179656 | tf_op jit(solution)/shard_map/ppermute | solution.py:484
  210.0 16.8 %collective-permute-start.39 = (f32[8,6,16,128]{3,2,1,0:T(8,128)}, f32[8,6,16,128]{3,2,1,0:T(8,128)}, u32[]{:S(2)}, u32[]{:S(2)}) collective-permute-start(f32[8,6,16,128]{3,2,1,0:T(8,128)} %collective-permute-done.38.refs_10_), channel_id=1, source_target_pairs={{0,1},{1,0},{2,3},{3,2},{4,5},{5,4},{6,7},{7,6},{8,9},{9,8},{10,11... | collective-permute-start | bytes 1179656 | tf_op jit(solution)/shard_map/ppermute | solution.py:484
  210.0 17.6 %collective-permute-start.35 = (f32[8,6,16,128]{3,2,1,0:T(8,128)}, f32[8,6,16,128]{3,2,1,0:T(8,128)}, u32[]{:S(2)}, u32[]{:S(2)}) collective-permute-start(f32[8,6,16,128]{3,2,1,0:T(8,128)} %collective-permute-done.33.refs_4_), channel_id=1, source_target_pairs={{0,2},{1,3},{2,0},{3,1},{4,6},{5,7},{6,4},{7,5},{8,10},{9,11},{10,... | collective-permute-start | bytes 1179656 | tf_op jit(solution)/shard_map/ppermute | solution.py:484
  212.2 15.7 %collective-permute-start.34 = (f32[8,6,16,128]{3,2,1,0:T(8,128)}, f32[8,6,16,128]{3,2,1,0:T(8,128)}, u32[]{:S(2)}, u32[]{:S(2)}) collective-permute-start(f32[8,6,16,128]{3,2,1,0:T(8,128)} %collective-permute-done.33.refs_4_), channel_id=1, source_target_pairs={{0,1},{1,0},{2,3},{3,2},{4,5},{5,4},{6,7},{7,6},{8,9},{9,8},{10,11... | collective-permute-start | bytes 1179656 | tf_op jit(solution)/shard_map/ppermute | solution.py:484
  226.4 4.3 %collective-permute-start.57 = (f32[16,8,16,128]{3,2,1,0:T(8,128)}, f32[16,8,16,128]{3,2,1,0:T(8,128)S(1)}, u32[]{:S(2)}, u32[]{:S(2)}) collective-permute-start(f32[16,8,16,128]{3,2,1,0:T(8,128)} %get-tuple-element.84), channel_id=1, source_target_pairs={{0,1},{1,0},{2,3},{3,2},{4,5},{5,4},{6,7},{7,6},{8,9},{9,8},{10,11... | collective-permute-start | bytes 3145736 | tf_op jit(solution)/shard_map/ppermute | solution.py:484
  226.9 26.3 %collective-permute-start.58 = (f32[16,8,16,128]{3,2,1,0:T(8,128)}, f32[16,8,16,128]{3,2,1,0:T(8,128)S(1)}, u32[]{:S(2)}, u32[]{:S(2)}) collective-permute-start(f32[16,8,16,128]{3,2,1,0:T(8,128)} %get-tuple-element.85), channel_id=1, source_target_pairs={{0,2},{1,3},{2,0},{3,1},{4,6},{5,7},{6,4},{7,5},{8,10},{9,11},{10,... | collective-permute-start | bytes 3145736 | tf_op jit(solution)/shard_map/ppermute | solution.py:484
  227.7 27.8 %collective-permute-start.53 = (f32[2,128,1024]{2,1,0:T(8,128)}, f32[2,128,1024]{2,1,0:T(8,128)}, u32[]{:S(2)}, u32[]{:S(2)}) collective-permute-start(f32[2,128,1024]{2,1,0:T(8,128)} %collective-permute-done.52.refs_2_), channel_id=1, source_target_pairs={{0,8},{8,16},{16,24},{24,0},{1,9},{9,17},{17,25},{25,1},{2,10},{10... | collective-permute-start | bytes 3145736 | tf_op jit(solution)/shard_map/ppermute | solution.py:499
  227.7 2.3 collective-permute-start.32
  227.8 2.5 collective-permute-start.29
  229.9 23.8 %collective-permute-start.43 = (f32[8,6,16,128]{3,2,1,0:T(8,128)}, f32[8,6,16,128]{3,2,1,0:T(8,128)}, u32[]{:S(2)}, u32[]{:S(2)}) collective-permute-start(f32[8,6,16,128]{3,2,1,0:T(8,128)} %collective-permute-done.42.refs_14_), channel_id=1, source_target_pairs={{0,1},{1,0},{2,3},{3,2},{4,5},{5,4},{6,7},{7,6},{8,9},{9,8},{10,11... | collective-permute-start | bytes 1179656 | tf_op jit(solution)/shard_map/ppermute | solution.py:484
  230.4 23.4 %collective-permute-start.36 = (f32[8,6,16,128]{3,2,1,0:T(8,128)}, f32[8,6,16,128]{3,2,1,0:T(8,128)}, u32[]{:S(2)}, u32[]{:S(2)}) collective-permute-start(f32[8,6,16,128]{3,2,1,0:T(8,128)} %collective-permute-done.35.refs_6_), channel_id=1, source_target_pairs={{0,1},{1,0},{2,3},{3,2},{4,5},{5,4},{6,7},{7,6},{8,9},{9,8},{10,11... | collective-permute-start | bytes 1179656 | tf_op jit(solution)/shard_map/ppermute | solution.py:484
  230.7 102.0 %collective-permute-start.59 = (f32[16,8,16,128]{3,2,1,0:T(8,128)}, f32[16,8,16,128]{3,2,1,0:T(8,128)S(1)}, u32[]{:S(2)}, u32[]{:S(2)}) collective-permute-start(f32[16,8,16,128]{3,2,1,0:T(8,128)} %get-tuple-element.86), channel_id=1, source_target_pairs={{0,3},{1,2},{2,1},{3,0},{4,7},{5,6},{6,5},{7,4},{8,11},{9,10},{10,... | collective-permute-start | bytes 3145736 | tf_op jit(solution)/shard_map/ppermute | solution.py:484
  253.2 79.5 %collective-permute-start.60 = (f32[16,8,16,128]{3,2,1,0:T(8,128)}, f32[16,8,16,128]{3,2,1,0:T(8,128)}, u32[]{:S(2)}, u32[]{:S(2)}) collective-permute-start(f32[16,8,16,128]{3,2,1,0:T(8,128)} %get-tuple-element.87), channel_id=1, source_target_pairs={{0,4},{1,5},{2,6},{3,7},{4,0},{5,1},{6,2},{7,3},{8,12},{9,13},{10,... | collective-permute-start | bytes 3145736 | tf_op jit(solution)/shard_map/ppermute | solution.py:484
  253.8 78.9 %collective-permute-start.61 = (f32[16,8,16,128]{3,2,1,0:T(8,128)}, f32[16,8,16,128]{3,2,1,0:T(8,128)}, u32[]{:S(2)}, u32[]{:S(2)}) collective-permute-start(f32[16,8,16,128]{3,2,1,0:T(8,128)} %get-tuple-element.88), channel_id=1, source_target_pairs={{0,5},{1,4},{2,7},{3,6},{4,1},{5,0},{6,3},{7,2},{8,13},{9,12},{10,... | collective-permute-start | bytes 3145736 | tf_op jit(solution)/shard_map/ppermute | solution.py:484
  253.8 78.9 %collective-permute-start.62 = (f32[16,8,16,128]{3,2,1,0:T(8,128)}, f32[16,8,16,128]{3,2,1,0:T(8,128)}, u32[]{:S(2)}, u32[]{:S(2)}) collective-permute-start(f32[16,8,16,128]{3,2,1,0:T(8,128)} %get-tuple-element.89), channel_id=1, source_target_pairs={{0,6},{1,7},{2,4},{3,5},{4,2},{5,3},{6,0},{7,1},{8,14},{9,15},{10,... | collective-permute-start | bytes 3145736 | tf_op jit(solution)/shard_map/ppermute | solution.py:484
  255.5 87.9 %collective-permute-start.63 = (f32[16,8,16,128]{3,2,1,0:T(8,128)}, f32[16,8,16,128]{3,2,1,0:T(8,128)}, u32[]{:S(2)}, u32[]{:S(2)}) collective-permute-start(f32[16,8,16,128]{3,2,1,0:T(8,128)} %get-tuple-element.90), channel_id=1, source_target_pairs={{0,7},{1,6},{2,5},{3,4},{4,3},{5,2},{6,1},{7,0},{8,15},{9,14},{10,... | collective-permute-start | bytes 3145736 | tf_op jit(solution)/shard_map/ppermute | solution.py:484
  (42 other events, 1175.5 us)

commit v3 on v2

v3 whole, which is shorter than its diff:
```python
import functools

import jax
import jax.numpy as jnp
from jax import lax
from jax.experimental import pallas as pl
from jax.experimental.pallas import tpu as pltpu
from jax.sharding import PartitionSpec as P

BLK = 128
NPIV = 6
PLANE = ("col", "sub")
VMEM_BYTES = 60 * 1024 * 1024

highest = lax.Precision.HIGHEST


def quot(value, number):
    if number & (number - 1) == 0:
        return lax.shift_right_logical(value, jnp.int32(number.bit_length() - 1))
    return lax.div(value, jnp.int32(number))


def rem(value, number):
    if number & (number - 1) == 0:
        return value & (number - 1)
    return lax.rem(value, jnp.int32(number))


def whole(memory):
    return pl.BlockSpec(memory_space=memory)


def cost(micros):
    return pl.CostEstimate(
        flops=micros * 1_000_000_000, bytes_accessed=micros * 3_000_000, transcendentals=0
    )


def params(**more):
    return pltpu.CompilerParams(vmem_limit_bytes=VMEM_BYTES, **more)


class Plan:
    def __init__(self, front_shape, child_shape):
        self.rows = lax.axis_size("row")
        self.cols = lax.axis_size("col")
        self.subs = lax.axis_size("sub")
        self.plane = self.cols * self.subs
        self.part = BLK // self.plane
        self.row_blocks = front_shape[0] // BLK
        self.slots = front_shape[1] // BLK
        self.child_rows = child_shape[1] // BLK
        self.child_cols = child_shape[2] // BLK
        self.order = self.child_rows * self.rows
        self.lead_cols = -(-NPIV // self.cols)
        self.lead_rows = -(-NPIV // self.rows)
        reach = [
            min((self.rows * t + self.rows - 1) // self.cols + 1, self.child_cols)
            for t in range(self.child_rows)
        ]
        first = [(t, u) for t in range(self.child_rows) for u in range(min(reach[t], self.lead_cols))]
        second = [(t, u) for t in range(self.child_rows) for u in range(self.lead_cols, reach[t])]
        self.first = len(first)
        self.second = len(second)
        self.blocks = first + second
        self.rest = self.second + self.row_blocks * self.lead_cols + 1
        self.area = self.row_blocks * self.slots
        self.limit = self.area // 2
        self.first_start = [first.index((t, 0)) for t in range(self.child_rows)]
        self.second_start = [
            sum(1 for b in second if b[0] < t) for t in range(self.child_rows)
        ]

    def dest(self, block):
        high = quot(block, self.cols)
        return rem(block, self.cols), quot(high, self.slots), rem(high, self.slots)

    def offset(self, starts, t):
        out = jnp.int32(starts[0])
        for step in range(1, len(starts)):
            out = jnp.where(t == step, jnp.int32(starts[step]), out)
        return out


def take_rows(ref, lead, base, index, part, lanes):
    if part % 8 == 0:
        return ref[(*lead, pl.ds(pl.multiple_of(base + index * part, part), part), lanes)]
    share = 8 // part
    group = ref[(*lead, pl.ds(pl.multiple_of(base + quot(index, share) * 8, 8), 8), lanes)]
    out = group[:part]
    for step in range(1, share):
        out = jnp.where(rem(index, share) == step, group[step * part : (step + 1) * part], out)
    return out


def put_rows(ref, base, index, lanes, value):
    part = value.shape[0]
    if part % 8 == 0:
        ref[pl.ds(pl.multiple_of(base + index * part, part), part), lanes] = value
        return
    share = 8 // part
    rows = pl.ds(pl.multiple_of(base + quot(index, share) * 8, 8), 8)
    spot = lax.broadcasted_iota(jnp.int32, (8, value.shape[1]), 0)
    mine = quot(spot, part) == rem(index, share)
    ref[rows, lanes] = jnp.where(mine, jnp.concatenate([value] * share, axis=0), ref[rows, lanes])


def block_lanes(number):
    return slice(number * BLK, (number + 1) * BLK)


def cut_child_kernel(plan, tile_ref, out_ref):
    for k in range(plan.plane):
        for b, (t, u) in enumerate(plan.blocks[: plan.first]):
            rows = slice(t * BLK + k * plan.part, t * BLK + (k + 1) * plan.part)
            out_ref[k, b] = tile_ref[0, rows, block_lanes(u)]


def cut_rest_kernel(plan, tile_ref, front_ref, map_ref, out_ref):
    for k in range(plan.plane):
        for b, (t, u) in enumerate(plan.blocks[plan.first :]):
            rows = slice(t * BLK + k * plan.part, t * BLK + (k + 1) * plan.part)
            out_ref[k, b] = tile_ref[0, rows, block_lanes(u)]
        out_ref[k, plan.rest - 1] = map_ref[...]

    @pl.loop(0, plan.row_blocks)
    def _(t):
        for k in range(plan.plane):
            for u in range(plan.lead_cols):
                out_ref[k, plan.second + t * plan.lead_cols + u] = take_rows(
                    front_ref, (), t * BLK, jnp.int32(k), plan.part, block_lanes(u)
                )


def front_panel_kernel(plan, pieces_ref, panel_ref, lead_ref):
    for pivot in range(NPIV):
        owner = pivot % plan.cols * plan.subs

        @pl.loop(0, plan.row_blocks)
        def _(t):
            panel_ref[t, pivot] = pieces_ref[
                owner, plan.second + t * plan.lead_cols + pivot // plan.cols
            ]

    for r in range(plan.rows):
        lead_ref[r] = panel_ref[: plan.lead_rows]


def pack(block, pivot):
    return (block * (block + 1)) // 2 + pivot


def ring_copies(plan, pieces, held, first_block, count, sems, first_sem):
    copies = []
    for number, (h, low, high, piece) in enumerate(pieces):
        copies.append(
            pltpu.make_async_copy(
                piece,
                held.at[h, pl.ds(low, high - low), pl.ds(first_block, count)],
                sems.at[first_sem + number],
            )
        )
    return copies


def panel_kernel(plan, spans, place_ref, maps_ref, *refs):
    rows = plan.rows
    ring = refs[: len(spans)]
    front_ref, panel_ref, corner_ref, across, held, sems = refs[len(spans) :]
    row, col, sub = place_ref[1], place_ref[2], place_ref[3]
    copies = ring_copies(
        plan, [(*span, piece) for span, piece in zip(spans, ring)], held, 0, plan.first, sems, 0
    )
    for copy in copies:
        copy.start()
    panel_ref[...] = front_ref[...]
    corner_ref[...] = jnp.zeros_like(corner_ref)
    across[...] = jnp.zeros_like(across)
    for copy in copies:
        copy.wait()

    def place(block):
        block_col, block_sub, slot = plan.dest(block)
        return block_col * plan.subs + block_sub, slot

    @pl.loop(0, plan.subs)
    def _(ms):
        @pl.loop(0, min(NPIV, plan.order))
        def _(j):
            pivot = maps_ref[ms, j]

            @pl.when(pivot < NPIV)
            def _():
                u = quot(j, plan.cols)
                m = rem(j, plan.cols) * plan.subs + ms

                @pl.loop(j, plan.order)
                def _(i):
                    block = maps_ref[ms, i]
                    h = rem(row - rem(i, rows) + rows, rows)
                    b = plan.offset(plan.first_start, quot(i, rows)) + u

                    @pl.when(rem(block, rows) == row)
                    def _():
                        panel_ref[quot(block, rows), pivot] += held[h, m, b]

                    @pl.when(block < NPIV)
                    def _():
                        base = lax.shift_right_logical(block * (block + 1), jnp.int32(1))
                        corner_ref[base + pivot] += held[h, m, b]

                    @pl.when(rem(pivot, rows) == row)
                    def _():
                        target, slot = place(block)
                        across[target, quot(pivot, rows), slot] += held[h, m, b]

                    @pl.when((block < NPIV) & (block != pivot) & (rem(block, rows) == row))
                    def _():
                        target, slot = place(pivot)
                        across[target, quot(block, rows), slot] += held[h, m, b]


def corner_front_kernel(plan, part_ref, leads_ref, out_ref):
    for block in range(NPIV):
        for pivot in range(block + 1):
            spot = pack(block, pivot)
            out_ref[spot] = (
                part_ref[spot] + leads_ref[block % plan.rows, block // plan.rows, pivot]
            )


def spread_kernel(plan, spans, one_way, place_ref, maps_ref, table_ref, more_ref, *refs):
    rows, plane = plan.rows, plan.plane
    count = len(spans)
    total_count = count + len(one_way)
    ring_first, ring_second = refs[:count], refs[count:total_count]
    outs, rests, held, total, sems, out_sems, rest_sems = refs[total_count:]
    me, row, col, sub = place_ref[0], place_ref[1], place_ref[2], place_ref[3]
    copies = ring_copies(
        plan, [(*span, piece) for span, piece in zip(spans, ring_first)], held, 0, plan.first,
        sems, 0,
    ) + ring_copies(
        plan, [(*span, piece) for span, piece in zip(one_way, ring_second)], held, plan.first,
        plan.second, sems, count,
    )
    for copy in copies:
        copy.start()

    @pl.loop(0, plane)
    def _(m):
        chunk = 8

        @pl.loop(0, plan.limit // chunk)
        def _(step):
            total[m, pl.ds(step * chunk, chunk)] = jnp.zeros((chunk, plan.part, BLK), jnp.float32)

        @pl.when(more_ref[0] > 0)
        def _():
            @pl.loop(plan.limit // chunk, plan.area // chunk)
            def _(step):
                total[m, pl.ds(step * chunk, chunk)] = jnp.zeros(
                    (chunk, plan.part, BLK), jnp.float32
                )

    for copy in copies:
        copy.wait()

    @pl.loop(0, plan.subs)
    def _(ms):
        @pl.loop(0, plan.order)
        def _(i):
            block_row = maps_ref[ms, i]

            @pl.when((rem(block_row, rows) == row) & (block_row >= NPIV))
            def _():
                line = quot(block_row, rows) * plan.slots

                @pl.loop(0, plan.order)
                def _(j):
                    block = maps_ref[ms, j]

                    @pl.when(block >= NPIV)
                    def _():
                        block_col, block_sub, slot = plan.dest(block)
                        high = jnp.maximum(i, j)
                        low = jnp.minimum(i, j)
                        h = rem(row - rem(high, rows) + rows, rows)
                        t = quot(high, rows)
                        u = quot(low, plan.cols)
                        m = rem(low, plan.cols) * plan.subs + ms
                        b = jnp.where(
                            u < plan.lead_cols,
                            plan.offset(plan.first_start, t) + u,
                            plan.first + plan.offset(plan.second_start, t) + u - plan.lead_cols,
                        )
                        dest = block_col * plan.subs + block_sub
                        spot = table_ref[dest, line + slot]
                        total[dest, spot] += held[h, m, b]

    out_copies = [
        pltpu.make_async_copy(total.at[m, pl.ds(0, plan.limit)], outs.at[m], out_sems.at[m])
        for m in range(plane)
    ]
    for copy in out_copies:
        copy.start()

    @pl.when(more_ref[0] > 0)
    def _():
        rest_copies = [
            pltpu.make_async_copy(
                total.at[m, pl.ds(plan.limit, plan.area - plan.limit)], rests.at[m], rest_sems.at[m]
            )
            for m in range(plane)
        ]
        for copy in rest_copies:
            copy.start()
        for copy in rest_copies:
            copy.wait()

    for copy in out_copies:
        copy.wait()


def lead_rows_kernel(plan, place_ref, front_ref, parts_ref, out_ref):
    row, col, sub = place_ref[1], place_ref[2], place_ref[3]
    for q in range(plan.lead_rows):
        block = plan.rows * q + row
        for slot in range(plan.slots):
            column = (sub * plan.slots + slot) * plan.cols + col
            joined = jnp.concatenate(
                [parts_ref[k, q, slot] for k in range(plan.plane)], axis=0
            )
            joined = jnp.where(column > block, joined.T, joined)
            out_ref[q, :, block_lanes(slot)] = (
                front_ref[q * BLK : (q + 1) * BLK, block_lanes(slot)] + joined
            )


def spread_lane(value, lane):
    return jnp.broadcast_to(value[:, lane : lane + 1], value.shape)


def spread_row(value, row):
    return jnp.broadcast_to(value[row : row + 1, :], value.shape)


def factor_block(matrix):
    group = 8
    count = BLK // group
    shape = (group, BLK)
    at_row = lax.broadcasted_iota(jnp.int32, shape, 0)
    at_lane = lax.broadcasted_iota(jnp.int32, shape, 1)
    left = [matrix[group * s : group * (s + 1), :] for s in range(count)]
    right = [jnp.where(at_lane == at_row + group * s, 1.0, 0.0) for s in range(count)]
    for s in range(count):
        cols = {
            t: [spread_lane(left[t], group * s + q) for q in range(group)] for t in range(s, count)
        }
        for o in range(group):
            inverse = 1.0 / spread_row(cols[s][o], o)
            scale = [spread_row(cols[s][q], o) * inverse for q in range(o + 1, group)]
            row_left = spread_row(left[s], o) * inverse
            row_right = spread_row(right[s], o) * inverse
            for t in range(s, count):
                col = cols[t][o]
                if t == s:
                    col = jnp.where(at_row > o, col, 0.0)
                for q in range(o + 1, group):
                    cols[t][q] = cols[t][q] - col * scale[q - o - 1]
                left[t] = left[t] - col * row_left
                right[t] = right[t] - col * row_right
    for s in range(count):
        pivots = jnp.sum(
            jnp.where(at_lane == at_row + group * s, left[s], 0.0), axis=1, keepdims=True
        )
        root = lax.rsqrt(pivots)
        root = root * (1.5 - 0.5 * pivots * root * root)
        left[s] = jnp.where(at_lane >= at_row + group * s, left[s] * root, 0.0)
        right[s] = right[s] * root
    return jnp.concatenate(left, axis=0), jnp.concatenate(right, axis=0)


def corner_load_kernel(plan, steps, place_ref, near_ref, far_ref, factor_ref, work):
    me = place_ref[0]
    for m in range(plan.plane):
        part = (near_ref, far_ref)[m % 2].at[m // 2]
        for block in range(NPIV):
            for pivot in range(block + 1):
                put_rows(
                    work, block * BLK, me ^ m, block_lanes(pivot), part[pack(block, pivot)]
                )
    for block in range(NPIV):
        for pivot in range(block):
            work[block_lanes(pivot), block_lanes(block)] = work[
                block_lanes(block), block_lanes(pivot)
            ].T
    factor_ref[...] = jnp.zeros_like(factor_ref)
    eliminate(steps, factor_ref, work)


def corner_rest_kernel(steps, factor_in, work_in, factor_ref, work):
    factor_ref[...] = factor_in[...]
    work[...] = work_in[...]
    eliminate(steps, factor_ref, work)


def eliminate(steps, factor_ref, work):
    exact = functools.partial(
        lax.dot_general, precision=highest, preferred_element_type=jnp.float32
    )

    @pl.loop(*steps)
    def _(pivot):
        here = pl.ds(pl.multiple_of(pivot * BLK, BLK), BLK)
        upper, inverse = factor_block(work[here, here])
        factor_ref[here, here] = upper.T
        work[here, :] = exact(inverse, work[here, :], (((1,), (0,)), ((), ())))
        work[here, here] = inverse

        @pl.loop(pivot + 1, NPIV)
        def _(block):
            there = pl.ds(pl.multiple_of(block * BLK, BLK), BLK)
            lower = work[here, there].T
            factor_ref[there, here] = lower
            work[there, here] = jnp.zeros((BLK, BLK), jnp.float32)
            work[there, :] -= exact(lower, work[here, :], (((1,), (0,)), ((), ())))

        @pl.loop(pivot + 1, NPIV)
        def _(block):
            there = pl.ds(pl.multiple_of(block * BLK, BLK), BLK)
            work[here, there] = jnp.zeros((BLK, BLK), jnp.float32)


def halves(value):
    high = value.astype(jnp.bfloat16)
    return high, (value - high.astype(jnp.float32)).astype(jnp.bfloat16)


def right_kernel(plan, spans, place_ref, inverse_ref, *refs):
    leads = refs[: len(spans)]
    high_ref, low_ref, stack = refs[len(spans) :]
    row = place_ref[1]
    for (h, low, high), lead in zip(spans, leads):
        for q in range(low // BLK, -(-high // BLK)):
            start, end = max(low, q * BLK), min(high, (q + 1) * BLK)
            block = plan.rows * q + rem(row - h + plan.rows, plan.rows)

            @pl.when(block < NPIV)
            def _():
                spot = pl.multiple_of(block * BLK + (start - q * BLK), 8)
                stack[pl.ds(spot, end - start), :] = lead[start - low : end - low]

    for pivot in range(NPIV):
        depth = (pivot + 1) * BLK
        value = jnp.dot(
            inverse_ref[pivot * BLK : depth, :depth], stack[:depth, :],
            precision=highest, preferred_element_type=jnp.float32,
        )
        high, low = halves(value)
        high_ref[pivot * BLK : depth, :] = high
        low_ref[pivot * BLK : depth, :] = low


def left_kernel(plan, tile_blocks, place_ref, inverse_ref, factor_ref, *refs):
    count = plan.plane
    parts = refs[:2]
    high_ref, low_ref, own_ref, panel, value_ref = refs[2:]
    me, row, col = place_ref[0], place_ref[1], place_ref[2]
    step = pl.program_id(0)
    for t in range(tile_blocks):
        for m in range(count):
            for pivot in range(NPIV):
                put_rows(panel, t * BLK, me ^ m, block_lanes(pivot), parts[m % 2][m // 2, t, pivot])
    for pivot in range(0, NPIV, 2):
        depth = min(pivot + 2, NPIV) * BLK
        value_ref[:, pivot * BLK : depth] = lax.dot_general(
            panel[:, :depth], inverse_ref[pivot * BLK : depth, :depth],
            (((1,), (1,)), ((), ())),
            precision=highest, preferred_element_type=jnp.float32,
        )
    high, low = halves(value_ref[...])
    high_ref[...] = high
    low_ref[...] = low
    for t in range(tile_blocks):
        block = plan.rows * (step * tile_blocks + t) + row
        for u in range(plan.lead_cols):
            pivot = jnp.minimum(plan.cols * u + col, NPIV - 1)
            lanes = pl.ds(pl.multiple_of(pivot * BLK, BLK), BLK)
            here = (slice(t * BLK, (t + 1) * BLK), block_lanes(u))
            own_ref[here] = value_ref[t * BLK : (t + 1) * BLK, lanes]

            @pl.when(block < NPIV)
            def _():
                own_ref[here] = factor_ref[
                    pl.ds(pl.multiple_of(block * BLK, BLK), BLK), lanes
                ]


def schur_kernel(plan, tile_blocks, place_ref, table_ref, more_ref, front_ref, high_ref, low_ref,
                 own_ref, right_high_ref, right_low_ref, parts, rests, out_ref, rest, sems):
    plane = plan.plane
    me, row, col, sub = place_ref[0], place_ref[1], place_ref[2], place_ref[3]
    step = pl.program_id(0)

    @pl.when((step == 0) & (more_ref[0] > 0))
    def _():
        copy = pltpu.make_async_copy(rests, rest, sems)
        copy.start()
        copy.wait()

    update = jnp.dot(high_ref[...], right_high_ref[...], preferred_element_type=jnp.float32)
    update += jnp.dot(high_ref[...], right_low_ref[...], preferred_element_type=jnp.float32)
    update += jnp.dot(low_ref[...], right_high_ref[...], preferred_element_type=jnp.float32)
    out_ref[...] = front_ref[...] - update
    for t in range(tile_blocks):
        line = step * tile_blocks + t
        block = plan.rows * line + row
        for slot in range(plan.slots):
            column = (sub * plan.slots + slot) * plan.cols + col
            here = (slice(t * BLK, (t + 1) * BLK), block_lanes(slot))
            spot = table_ref[me, line * plan.slots + slot]

            @pl.when(spot >= 0)
            def _():
                def add(ref, place):
                    joined = jnp.concatenate([ref[k, place] for k in range(plane)], axis=0)
                    out_ref[here] += jnp.where(column > block, joined.T, joined)

                @pl.when(spot < plan.limit)
                def _():
                    add(parts, spot)

                @pl.when(spot >= plan.limit)
                def _():
                    add(rest, spot - plan.limit)

            @pl.when((block < NPIV) & (column >= NPIV))
            def _():
                out_ref[here] = jnp.zeros((BLK, BLK), jnp.float32)

            if slot < plan.lead_cols:
                @pl.when(column < NPIV)
                def _():
                    out_ref[here] = own_ref[here]


def swap(value, plan, bit):
    return lax.ppermute(value, PLANE, [(k, k ^ bit) for k in range(plan.plane)])


def exchange(pieces, plan):
    return [pieces[0]] + [swap(pieces[m], plan, m) for m in range(1, plan.plane)]


def gather_direct(value, plan):
    return [value] + [swap(value, plan, m) for m in range(2, plan.plane, 2)]


def spread_over(value, axis, count):
    return lax.all_to_all(jnp.broadcast_to(value, (count, *value.shape)), axis, 0, 0)


def shift(value, plan, step):
    pairs = [(r, (r + step) % plan.rows) for r in range(plan.rows)]
    return lax.ppermute(value, "row", pairs)


def ring_gather(value, plan, *hold):
    count = value.shape[0]
    middle = count // 2
    out = [(0, 0, count, value)]
    before = behind = value
    for h in range(1, (plan.rows + 1) // 2):
        before, behind = shift(before, plan, 1), shift(behind, plan, -1)
        out += [(h, 0, count, before), (plan.rows - h, 0, count, behind)]
    if plan.rows % 2 == 0 and plan.rows > 1:
        before, behind = after((before, behind), *hold)
        h = plan.rows // 2
        out.append((h, 0, middle, shift(before[:middle], plan, 1)))
        out.append((h, middle, count, shift(behind[middle:], plan, -1)))
    return out


def after(values, *others):
    return lax.optimization_barrier((values, others))[0]


def cover_table(maps, row, plan):
    blocks = plan.row_blocks * plan.rows
    numbers = jnp.arange(blocks, dtype=jnp.int32)
    present = jnp.any(maps[:, :, None] == numbers, axis=1) & (numbers >= NPIV)
    lines = present.reshape(plan.subs, plan.row_blocks, plan.rows).transpose(0, 2, 1)
    columns = present.reshape(plan.subs, plan.subs, plan.slots, plan.cols).transpose(0, 3, 1, 2)
    columns = columns.reshape(plan.subs, plan.plane, plan.slots)
    cover = jnp.any(
        lines[:, :, None, :, None] & columns[:, None, :, None, :], axis=0
    ).reshape(plan.rows, plan.plane, plan.area)
    more = (jnp.max(jnp.sum(cover.astype(jnp.int32), axis=-1)) > plan.limit).astype(jnp.int32)
    mine = lax.dynamic_index_in_dim(cover, row, 0, keepdims=False)
    order = jnp.arange(plan.area, dtype=jnp.int32)
    before = (order[:, None] < order[None, :]).astype(jnp.float32)
    rank = jnp.dot(mine.astype(jnp.float32), before, precision=highest)
    return jnp.where(mine, rank.astype(jnp.int32), -1), more


def body(front_entries, child_blocks, child_map):
    plan = Plan(front_entries.shape, child_blocks.shape)
    f32 = jnp.float32
    row = lax.axis_index("row").astype(jnp.int32)
    col = lax.axis_index("col").astype(jnp.int32)
    sub = lax.axis_index("sub").astype(jnp.int32)
    place = jnp.stack([col * plan.subs + sub, row, col, sub])
    vmem, smem, hbm = whole(pltpu.VMEM), whole(pltpu.SMEM), whole(pl.ANY)
    part, plane, rows = plan.part, plan.plane, plan.rows

    def shape(*sizes, dtype=f32):
        return jax.ShapeDtypeStruct(sizes, dtype)

    lead_width = plan.lead_cols * BLK
    local_rows = front_entries.shape[0]
    cut_first = pl.pallas_call(
        functools.partial(cut_child_kernel, plan),
        out_shape=shape(plane, plan.first, part, BLK),
        in_specs=[vmem],
        out_specs=vmem,
        compiler_params=params(),
        name="cut_child",
        cost_estimate=cost(2),
    )(child_blocks)
    first = lax.all_to_all(cut_first, PLANE, 0, 0, tiled=True)
    ring_first = ring_gather(first, plan)
    spans = [span for *span, _ in ring_first]
    ring_first = [piece for *_, piece in ring_first]

    map_rows = jnp.broadcast_to(
        jnp.pad(child_map.astype(f32), ((0, 0), (0, BLK - plan.order))), (part, BLK)
    )
    cut_rest = pl.pallas_call(
        functools.partial(cut_rest_kernel, plan),
        grid=(1,),
        out_shape=shape(plane, plan.rest, part, BLK),
        in_specs=[
            pl.BlockSpec(child_blocks.shape, lambda g: (0, 0, 0)),
            pl.BlockSpec((local_rows, lead_width), lambda g: (0, 0)),
            pl.BlockSpec((part, BLK), lambda g: (0, 0)),
        ],
        out_specs=vmem,
        compiler_params=params(),
        name="cut_rest",
        cost_estimate=cost(6),
    )(child_blocks, front_entries, map_rows)
    rest = lax.all_to_all(after(cut_rest, first), PLANE, 0, 0, tiled=True)
    rest = after(rest, *ring_first[1:3])
    maps = rest[: plan.subs, plan.rest - 1, 0, : plan.order].astype(jnp.int32)
    table, more = cover_table(maps, row, plan)
    more_flag = more.reshape(1)

    front_panel, front_lead = pl.pallas_call(
        functools.partial(front_panel_kernel, plan),
        out_shape=[
            shape(plan.row_blocks, NPIV, part, BLK),
            shape(rows, plan.lead_rows, NPIV, part, BLK),
        ],
        in_specs=[vmem],
        out_specs=[vmem] * 2,
        compiler_params=params(),
        name="front_panel",
        cost_estimate=cost(4),
    )(rest)
    leads = lax.all_to_all(front_lead, "row", 0, 0, tiled=True)
    second = after(rest[:, : plan.second], leads, *ring_first[1:])
    ring_second = [piece for *_, piece in ring_gather(second, plan)]

    corner_count = NPIV * (NPIV + 1) // 2
    panel, corner_part, lead_parts = pl.pallas_call(
        functools.partial(panel_kernel, plan, spans),
        out_shape=[
            shape(plan.row_blocks, NPIV, part, BLK),
            shape(corner_count, part, BLK),
            shape(plane, plan.lead_rows, plan.slots, part, BLK),
        ],
        in_specs=[smem, smem] + [hbm] * len(spans) + [vmem],
        out_specs=[vmem] * 3,
        scratch_shapes=[
            pltpu.VMEM((rows, plane, plan.first, part, BLK), f32),
            pltpu.SemaphoreType.DMA((len(spans),)),
        ],
        compiler_params=params(),
        name="panel",
        cost_estimate=cost(6),
    )(place, maps, *ring_first, front_panel)

    lead_got = lax.all_to_all(lead_parts, PLANE, 0, 0, tiled=True)
    lead_rows = pl.pallas_call(
        functools.partial(lead_rows_kernel, plan),
        grid=(1,),
        out_shape=shape(plan.lead_rows, BLK, plan.slots * BLK),
        in_specs=[
            smem,
            pl.BlockSpec((plan.lead_rows * BLK, plan.slots * BLK), lambda g: (0, 0)),
            vmem,
        ],
        out_specs=vmem,
        compiler_params=params(),
        name="lead_rows",
        cost_estimate=cost(3),
    )(place, front_entries, lead_got)
    corner_part = pl.pallas_call(
        functools.partial(corner_front_kernel, plan),
        out_shape=shape(corner_count, part, BLK),
        in_specs=[vmem] * 2,
        out_specs=vmem,
        compiler_params=params(),
        name="corner_front",
        cost_estimate=cost(1),
    )(corner_part, leads)
    corner_near = jnp.stack(gather_direct(corner_part, plan))
    panel = after(panel, corner_near)
    corner_far = swap(corner_near, plan, 1)
    corner_near, corner_far = after((corner_near, corner_far), lead_rows, ring_second)
    square = shape(NPIV * BLK, NPIV * BLK)
    middle = NPIV // 2
    factor, inverse = pl.pallas_call(
        functools.partial(corner_load_kernel, plan, (0, middle)),
        out_shape=[square] * 2,
        in_specs=[smem] + [vmem] * 2,
        out_specs=[vmem] * 2,
        compiler_params=params(),
        name="corner_first",
        cost_estimate=cost(21),
    )(place, corner_near, corner_far)
    line_rows = after(lead_rows.reshape(-1, plan.slots * BLK), ring_second)
    lead_ring = [(0, 0, line_rows.shape[0], line_rows)]
    for h in range(1, rows):
        lead_ring.append((h, 0, line_rows.shape[0], shift(line_rows, plan, h)))
    lead_spans = [span for *span, _ in lead_ring]
    lead_ring = [piece for *_, piece in lead_ring]
    panel_near = [panel]
    bits = [m for m in range(2, plane, 2) if m & (m - 1) == 0]
    for bit in bits:
        panel_near.append(swap(panel, plan, bit))
    inverse = after(inverse, panel_near[1])
    factor, inverse = pl.pallas_call(
        functools.partial(corner_rest_kernel, (middle, NPIV)),
        out_shape=[square] * 2,
        in_specs=[vmem] * 2,
        out_specs=[vmem] * 2,
        compiler_params=params(),
        name="corner_rest",
        cost_estimate=cost(20),
    )(factor, inverse)

    rest_count = plan.area - plan.limit
    ring_second = after(ring_second, inverse)
    spread = pl.pallas_call(
        functools.partial(spread_kernel, plan, spans, spans),
        out_shape=[
            shape(plane, plan.limit, part, BLK),
            shape(plane, rest_count, part, BLK),
        ],
        in_specs=[smem] * 4 + [hbm] * (2 * len(spans)),
        out_specs=[hbm] * 2,
        scratch_shapes=[
            pltpu.VMEM((rows, plane, plan.first + plan.second, part, BLK), f32),
            pltpu.VMEM((plane, plan.area, part, BLK), f32),
            pltpu.SemaphoreType.DMA((2 * len(spans),)),
            pltpu.SemaphoreType.DMA((plane,)),
            pltpu.SemaphoreType.DMA((plane,)),
        ],
        compiler_params=params(),
        name="spread",
        cost_estimate=cost(13),
    )(place, maps, table, more_flag, *ring_first, *ring_second)
    panel_held = {0: panel_near[0], **dict(zip(bits, panel_near[1:]))}
    for m in range(2, plane, 2):
        if m not in panel_held:
            low = m & -m
            panel_held[m] = swap(panel_held[m ^ low], plan, low)
    panel_near = jnp.stack([panel_held[m] for m in range(0, plane, 2)])
    panel_far = swap(after(panel_near, factor), plan, 1)
    right_high, right_low = pl.pallas_call(
        functools.partial(right_kernel, plan, lead_spans),
        out_shape=[shape(NPIV * BLK, plan.slots * BLK, dtype=jnp.bfloat16)] * 2,
        in_specs=[smem, vmem] + [vmem] * len(lead_spans),
        out_specs=[vmem] * 2,
        scratch_shapes=[pltpu.VMEM((NPIV * BLK, plan.slots * BLK), f32)],
        compiler_params=params(),
        name="right_factor",
        cost_estimate=cost(10),
    )(place, inverse, *lead_ring)

    tile = 2
    steps = plan.row_blocks // tile
    full = lambda g: (0, 0)
    by_row = lambda g: (g, 0)
    left_high, left_low, own = pl.pallas_call(
        functools.partial(left_kernel, plan, tile),
        grid=(steps,),
        out_shape=[
            shape(local_rows, NPIV * BLK, dtype=jnp.bfloat16),
            shape(local_rows, NPIV * BLK, dtype=jnp.bfloat16),
            shape(local_rows, lead_width),
        ],
        in_specs=[smem, vmem, vmem]
        + [
            pl.BlockSpec((plane // 2, tile, NPIV, part, BLK), lambda g: (0, g, 0, 0, 0))
        ]
        * 2,
        out_specs=[
            pl.BlockSpec((tile * BLK, NPIV * BLK), by_row),
            pl.BlockSpec((tile * BLK, NPIV * BLK), by_row),
            pl.BlockSpec((tile * BLK, lead_width), by_row),
        ],
        scratch_shapes=[
            pltpu.VMEM((tile * BLK, NPIV * BLK), f32),
            pltpu.VMEM((tile * BLK, NPIV * BLK), f32),
        ],
        compiler_params=params(),
        name="left_factor",
        cost_estimate=cost(18),
    )(place, inverse, factor, panel_near, panel_far)

    def trade(value):
        return lax.all_to_all(value, PLANE, 0, 0, tiled=True)

    spread_got = trade(after(spread[0], panel_near))
    rest_got = lax.cond(more > 0, trade, lambda value: value, spread[1])

    width = plan.slots * BLK
    return pl.pallas_call(
        functools.partial(schur_kernel, plan, tile),
        grid=(steps,),
        out_shape=jax.ShapeDtypeStruct(front_entries.shape, f32),
        in_specs=[smem] * 3
        + [
            pl.BlockSpec((tile * BLK, width), by_row),
            pl.BlockSpec((tile * BLK, NPIV * BLK), by_row),
            pl.BlockSpec((tile * BLK, NPIV * BLK), by_row),
            pl.BlockSpec((tile * BLK, lead_width), by_row),
            pl.BlockSpec((NPIV * BLK, width), full),
            pl.BlockSpec((NPIV * BLK, width), full),
            vmem,
            hbm,
        ],
        out_specs=pl.BlockSpec((tile * BLK, width), by_row),
        scratch_shapes=[
            pltpu.VMEM((plane, rest_count, part, BLK), f32),
            pltpu.SemaphoreType.DMA,
        ],
        compiler_params=params(),
        name="schur",
        cost_estimate=cost(20),
    )(
        place, table, more_flag, front_entries, left_high, left_low, own, right_high, right_low,
        spread_got, rest_got,
    )


def solution(mesh):
    placed = (P("row", ("col", "sub")), P("sub", "row", "col"), P("sub", None))
    return jax.shard_map(
        body, mesh=mesh, in_specs=placed, out_specs=P("row", ("col", "sub")), check_vma=False
    )
```

time: 361 us -> 284 us (0.79)
  waiting for transfers between devices: 169 us -> 85.6 us
  other arithmetic: 1.2 us -> 6.84 us
  starting transfers between devices: 54.4 us -> 50.6 us
    ppermute x42 -> x8, waiting for transfers between devices: 74.8 us -> 12.6 us  [swap(): return lax.ppermute(value, PLANE, [(k, k ^ bit) for k in range(plan.plane)])]
    ppermute x22 -> x11, waiting for transfers between devices: 94.3 us -> 43 us  [shift(): return lax.ppermute(value, 'row', pairs)]
    all_to_all x0 -> x5, waiting for transfers between devices: none -> 30.1 us  [the longest x1 19.3 us: trade(): return lax.all_to_all(value, PLANE, 0, 0, tiled=True)]
    ppermute x42 -> x8, starting transfers between devices: 35.1 us -> 8.56 us  [swap(): return lax.ppermute(value, PLANE, [(k, k ^ bit) for k in range(plan.plane)])]
    all_to_all x0 -> x5, starting transfers between devices: none -> 22.7 us  [the longest x1 5.17 us: body(): first = lax.all_to_all(cut_first, PLANE, 0, 0, tiled=True)]
    pallas_call x9 -> x11, Pallas kernels: 128 us -> 127 us  [the longest x1 24.2 us: body(): pl.pallas_call(functools.partial(corner_load_kernel, plan, (0, middle)),...]
    ppermute x22 -> x11, starting transfers between devices: 19.3 us -> 19.3 us  [shift(): return lax.ppermute(value, 'row', pairs)]
  transfers between devices with their start and end apart: 64 -> 24, of which waited for: 23 -> 11; matrix products, arithmetic and copies ran while one was open for 1% -> 4% of each run, Pallas kernels for 30% -> 38%
where the time goes in v3:
time: 284 us; the launch traced here: 283 us
  Pallas kernels  130 us (46%)
  waiting for transfers between devices  85.6 us (30%)
  starting transfers between devices  50.6 us (18%)
  local copies, waits for them, and re-layouts  7.7 us (3%)
  other arithmetic  6.84 us (2%)
    ppermute x11, waiting for transfers between devices, shift(): return lax.ppermute(value, 'row', pairs)  43 us
    pallas_call x1, Pallas kernels, body(): pl.pallas_call(functools.partial(corner_load_kernel, plan, (0, middle)),...  24.2 us
    pallas_call x1, Pallas kernels, body(): pl.pallas_call(functools.partial(schur_kernel, plan, tile), grid=(steps,)...  21 us
    pallas_call x1, Pallas kernels, body(): pl.pallas_call(functools.partial(corner_rest_kernel, (middle, NPIV)), out...  20.3 us
    ppermute x11, starting transfers between devices, shift(): return lax.ppermute(value, 'row', pairs)  19.3 us
    all_to_all x1, waiting for transfers between devices, trade(): return lax.all_to_all(value, PLANE, 0, 0, tiled=True)  19.3 us
    pallas_call x1, Pallas kernels, body(): pl.pallas_call(functools.partial(left_kernel, plan, tile), grid=(steps,),...  17.3 us
    pallas_call x1, Pallas kernels, body(): pl.pallas_call(functools.partial(spread_kernel, plan, spans, spans), out_...  13.4 us
  transfers between devices with their start and end apart: 24, of which 11 were waited for; matrix products, arithmetic and copies ran while one was open for 4% of the time, Pallas kernels for 38%

profile of v3, /device:TPU:0, one launch (start us, length us, event | category | flops | bytes accessed | tf_op | source)
XLA Modules:
  0.0 282.9 jit_solution(8023030643282810559)
XLA Ops:
  0.0 2.5 cut_child.1
  2.5 5.2 %all-to-all-start.1 = ((f32[8,11,16,128]{3,2,1,0:T(8,128)}), f32[8,11,16,128]{3,2,1,0:T(8,128)S(1)}, u32[]{:S(2)}, u32[]{:S(2)}) async-start(f32[8,11,16,128]{3,2,1,0:T(8,128)} %cut_child.1), calls=%async_computation.1 | async-start | bytes 1441792 | tf_op jit(solution)/shard_map/all_to_all | solution.py:631
  7.7 0.6 broadcast_in_dim.8.map_ref
  8.3 4.7 %cut_rest.1 = f32[8,58,16,128]{3,2,1,0:T(8,128)} custom-call(f32[1,512,1024]{2,1,0:T(8,128)} %tile_ref.3, f32[2048,1024]{1,0:T(8,128)} %front_ref.5, f32[16,128]{1,0:T(8,128)} %broadcast_in_dim.8.map_ref), custom_call_target="tpu_custom_call" | custom-call | flops 6000000000 | bytes 18000000 | tf_op jit(solution)/shard_map/cut_rest/pallas_call | solution.py:639
  13.0 5.6 %all-to-all-done.1.refs_0_ = f32[8,11,16,128]{3,2,1,0:T(8,128)S(1)} async-done(((f32[8,11,16,128]{3,2,1,0:T(8,128)}), f32[8,11,16,128]{3,2,1,0:T(8,128)S(1)}, u32[]{:S(2)}, u32[]{:S(2)}) %all-to-all-start.1) | async-done | bytes 720928 | tf_op jit(solution)/shard_map/all_to_all | solution.py:631
  18.6 4.5 %all-to-all-start.2 = ((f32[8,58,16,128]{3,2,1,0:T(8,128)}), f32[8,58,16,128]{3,2,1,0:T(8,128)}, u32[]{:S(2)}, u32[]{:S(2)}) async-start(f32[8,58,16,128]{3,2,1,0:T(8,128)} %cut_rest.1), calls=%async_computation.2 | async-start | bytes 7602176 | tf_op jit(solution)/shard_map/all_to_all | solution.py:653
  23.2 1.6 collective-permute-start
  24.8 2.2 collective-permute-start.1
  27.0 0.6 pad_add_fusion.place_ref
  27.7 16.3 %collective-permute-done.refs_1_ = f32[8,11,16,128]{3,2,1,0:T(8,128)S(1)} collective-permute-done((f32[8,11,16,128]{3,2,1,0:T(8,128)S(1)}, f32[8,11,16,128]{3,2,1,0:T(8,128)S(1)}, u32[]{:S(2)}, u32[]{:S(2)}) %collective-permute-start) | collective-permute-done | bytes 720928 | tf_op jit(solution)/shard_map/ppermute | solution.py:566
  44.0 14.3 %collective-permute-done.1.refs_2_ = f32[8,11,16,128]{3,2,1,0:T(8,128)S(1)} collective-permute-done((f32[8,11,16,128]{3,2,1,0:T(8,128)S(1)}, f32[8,11,16,128]{3,2,1,0:T(8,128)S(1)}, u32[]{:S(2)}, u32[]{:S(2)}) %collective-permute-start.1) | collective-permute-done | bytes 720928 | tf_op jit(solution)/shard_map/ppermute | solution.py:566
  58.4 1.2 collective-permute-start.2
  59.6 2.8 collective-permute-start.3
  62.3 4.8 %all-to-all-done.2.pieces_ref = f32[8,58,16,128]{3,2,1,0:T(8,128)} async-done(((f32[8,58,16,128]{3,2,1,0:T(8,128)}), f32[8,58,16,128]{3,2,1,0:T(8,128)}, u32[]{:S(2)}, u32[]{:S(2)}) %all-to-all-start.2) | async-done | bytes 3801120 | tf_op jit(solution)/shard_map/all_to_all | solution.py:653
  67.1 3.6 %front_panel.1 = (f32[16,6,16,128]{3,2,1,0:T(8,128)}, f32[4,2,6,16,128]{4,3,2,1,0:T(8,128)}) custom-call(f32[8,58,16,128]{3,2,1,0:T(8,128)} %all-to-all-done.2.pieces_ref), custom_call_target="tpu_custom_call" | custom-call | flops 4000000000 | bytes 12000000 | tf_op jit(solution)/shard_map/front_panel/pallas_call | solution.py:659
  70.8 4.9 %all-to-all-start.3 = ((f32[4,2,6,16,128]{4,3,2,1,0:T(8,128)}), f32[4,2,6,16,128]{4,3,2,1,0:T(8,128)S(1)}, u32[]{:S(2)}, u32[]{:S(2)}) async-start(f32[4,2,6,16,128]{4,3,2,1,0:T(8,128)} %get-tuple-element.51), calls=%async_computation.3 | async-start | bytes 786432 | tf_op jit(solution)/shard_map/all_to_all | solution.py:671
  75.6 0.7 slice_convert_fusion
  76.5 0.1 reduce_or.24
  76.7 1.1 slice.21.refs_5_
  77.8 0.8 copy-done.14
  78.6 8.1 %panel.1 = (f32[16,6,16,128]{3,2,1,0:T(8,128)}, f32[21,16,128]{2,1,0:T(8,128)}, f32[8,2,8,16,128]{4,3,2,1,0:T(8,128)}) custom-call(s32[4]{0:T(128)} %pad_add_fusion.place_ref, s32[4,16]{1,0:T(4,128)} %bitcast.37, f32[8,11,16,128]{3,2,1,0:T(8,128)} %copy-done.7, f32[8,11,16,128]{3,2,1,0:T(8,128)} %copy-done.10, f32[8,11,16,128]{3,2,1,0:T(8,128)} %copy-done.11, ...), custom_call_target="tpu_custom_call" | custom-call | flops 6000000000 | bytes 18000000 | tf_op jit(solution)/shard_map/panel/pallas_call | solution.py:676
  86.7 0.4 all-to-all-done.3.leads_ref
  87.1 3.6 %all-to-all-start.4 = ((f32[8,2,8,16,128]{4,3,2,1,0:T(8,128)}), f32[8,2,8,16,128]{4,3,2,1,0:T(8,128)S(1)}, u32[]{:S(2)}, u32[]{:S(2)}) async-start(f32[8,2,8,16,128]{4,3,2,1,0:T(8,128)} %get-tuple-element.52), calls=%async_computation.4 | async-start | bytes 2097152 | tf_op jit(solution)/shard_map/all_to_all | solution.py:694
  90.7 1.8 corner_front.1
  92.5 2.8 %collective-permute-start.6 = (f32[21,16,128]{2,1,0:T(8,128)}, f32[21,16,128]{2,1,0:T(8,128)S(1)}, u32[]{:S(2)}, u32[]{:S(2)}) collective-permute-start(f32[21,16,128]{2,1,0:T(8,128)} %corner_front.1), channel_id=1, source_target_pairs={{0,6},{1,7},{2,4},{3,5},{4,2},{5,3},{6,0},{7,1},{8,14},{9,15},{10,... | collective-permute-start | bytes 516104 | tf_op jit(solution)/shard_map/ppermute | solution.py:549
  95.4 0.5 collective-permute-start.5
  95.9 0.1 collective-permute-start.4
  96.1 1.6 collective-permute-start.8
  97.7 2.3 collective-permute-start.9
  99.9 10.2 %collective-permute-done.6 = f32[21,16,128]{2,1,0:T(8,128)S(1)} collective-permute-done((f32[21,16,128]{2,1,0:T(8,128)}, f32[21,16,128]{2,1,0:T(8,128)S(1)}, u32[]{:S(2)}, u32[]{:S(2)}) %collective-permute-start.6) | collective-permute-done | bytes 172064 | tf_op jit(solution)/shard_map/ppermute | solution.py:549
  110.2 2.3 collective-permute-done.5
  112.5 1.8 pad_maximum_fusion.1.near_ref
  114.3 0.2 copy.8
  114.6 0.1 and_reduce_fusion
  114.8 0.2 copy.9
  114.9 0.2 reshape.36
  115.1 0.7 convert_reduce_fusion
  115.8 9.1 %collective-permute-done.9.refs_7_ = f32[8,9,16,128]{3,2,1,0:T(8,128)} collective-permute-done((f32[8,9,16,128]{3,2,1,0:T(8,128)S(1)}, f32[8,9,16,128]{3,2,1,0:T(8,128)}, u32[]{:S(2)}, u32[]{:S(2)}) %collective-permute-start.9) | collective-permute-done | bytes 589856 | tf_op jit(solution)/shard_map/ppermute | solution.py:566
  124.9 0.7 slice.22
  125.6 1.1 collective-permute-start.10
  126.7 1.7 slice.23
  128.4 2.7 collective-permute-start.11
  131.2 0.7 fusion.table_ref
  131.9 0.7 reduce_max.9
  133.2 1.7 collective-permute-start.12
  135.0 1.5 collective-permute-start.13
  136.5 1.0 copy-done.2
  137.4 2.9 %lead_rows.1 = f32[2,128,1024]{2,1,0:T(8,128)} custom-call(s32[4]{0:T(128)} %pad_add_fusion.place_ref, f32[2048,1024]{1,0:T(8,128)} %front_ref.5, f32[8,2,8,16,128]{4,3,2,1,0:T(8,128)} %copy-done.2), custom_call_target="tpu_custom_call" | custom-call | flops 3000000000 | bytes 9000000 | tf_op jit(solution)/shard_map/lead_rows/pallas_call | solution.py:695
  140.3 2.1 collective-permute-done.11.refs_9_
  142.4 0.5 collective-permute-start.16
  142.9 1.7 collective-permute-start.17
  144.6 1.6 collective-permute-start.18
  146.2 24.2 %corner_first.1 = (f32[768,768]{1,0:T(8,128)}, f32[768,768]{1,0:T(8,128)}) custom-call(s32[4]{0:T(128)} %pad_add_fusion.place_ref, f32[4,21,16,128]{3,2,1,0:T(8,128)} %pad_maximum_fusion.1.near_ref, f32[4,21,16,128]{3,2,1,0:T(8,128)} %collective-permute-done.7.far_ref), custom_call_target="tpu_custom_call" | custom-call | flops 20999999488 | bytes 63000000 | tf_op jit(solution)/shard_map/corner_first/pallas_call | solution.py:724
  170.5 1.7 collective-permute-start.14
  172.2 20.3 %corner_rest.1 = (f32[768,768]{1,0:T(8,128)}, f32[768,768]{1,0:T(8,128)}) custom-call(f32[768,768]{1,0:T(8,128)} %get-tuple-element.58.factor_in, f32[768,768]{1,0:T(8,128)} %get-tuple-element.62.work_in), custom_call_target="tpu_custom_call" | custom-call | flops 20000000000 | bytes 60000000 | tf_op jit(solution)/shard_map/corner_rest/pallas_call | solution.py:744
  192.5 0.9 copy-done.6
  193.4 2.1 pad_maximum_fusion.refs_0_
  195.5 13.4 %spread.1 = (f32[8,64,16,128]{3,2,1,0:T(8,128)}, f32[8,64,16,128]{3,2,1,0:T(8,128)}) custom-call(s32[4]{0:T(128)} %pad_add_fusion.place_ref, s32[4,16]{1,0:T(4,128)} %bitcast.38, s32[8,128]{1,0:T(8,128)} %fusion.table_ref, s32[1]{0:T(128)} %bitcast.10.more_ref, f32[8,11,16,128]{3,2,1,0:T(8,128)} %copy-done.7, f32[8,11,16,128]{3,2,1,0:T(8,128)} %copy-done.10, ...), custom_call_target="tpu_custom_call" | custom-call | flops 12999999488 | bytes 39000000 | tf_op jit(solution)/shard_map/spread/pallas_call | solution.py:756
  209.0 4.5 %all-to-all-start.5 = ((f32[8,64,16,128]{3,2,1,0:T(8,128)}), f32[8,64,16,128]{3,2,1,0:T(8,128)}, u32[]{:S(2)}, u32[]{:S(2)}) async-start(f32[8,64,16,128]{3,2,1,0:T(8,128)} %get-tuple-element.78), calls=%async_computation.5 | async-start | bytes 8388608 | tf_op jit(solution)/shard_map/all_to_all | solution.py:825
  213.6 1.1 collective-permute-done.17.refs_2_
  214.7 10.5 %right_factor.1 = (bf16[768,1024]{1,0:T(8,128)(2,1)}, bf16[768,1024]{1,0:T(8,128)(2,1)}) custom-call(s32[4]{0:T(128)} %pad_add_fusion.place_ref, f32[768,768]{1,0:T(8,128)} %get-tuple-element.63.inverse_ref, f32[256,1024]{1,0:T(8,128)} %bitcast.42, f32[256,1024]{1,0:T(8,128)} %collective-permute-done.16.refs_1_, ...), custom_call_target="tpu_custom_call" | custom-call | flops 10000000000 | bytes 30000000 | tf_op jit(solution)/shard_map/right_factor/pallas_call | solution.py:782
  225.2 17.3 %left_factor.1 = (bf16[2048,768]{1,0:T(8,128)(2,1)}, bf16[2048,768]{1,0:T(8,128)(2,1)}, f32[2048,384]{1,0:T(8,128)}) custom-call(s32[4]{0:T(128)} %pad_add_fusion.place_ref, f32[768,768]{1,0:T(8,128)} %get-tuple-element.63.inverse_ref, f32[768,768]{1,0:T(8,128)} %get-tuple-element.64.factor_ref, f32[4,16,6,16,128]{4,3,2,1,0:T(8,128)} %copy-done.1, ...), custom_call_target="tpu_custom_call" | custom-call | flops 17999998976 | bytes 54000000 | tf_op jit(solution)/shard_map/left_factor/pallas_call | solution.py:797
  242.4 19.3 %all-to-all-done.5.parts = f32[8,64,16,128]{3,2,1,0:T(8,128)} async-done(((f32[8,64,16,128]{3,2,1,0:T(8,128)}), f32[8,64,16,128]{3,2,1,0:T(8,128)}, u32[]{:S(2)}, u32[]{:S(2)}) %all-to-all-start.5) | async-done | bytes 4194336 | tf_op jit(solution)/shard_map/all_to_all | solution.py:825
  261.7 21.0 %schur.1 = f32[2048,1024]{1,0:T(8,128)} custom-call(s32[4]{0:T(128)} %pad_add_fusion.place_ref, s32[8,128]{1,0:T(8,128)} %fusion.table_ref, s32[1]{0:T(128)} %bitcast.10.more_ref, f32[2048,1024]{1,0:T(8,128)} %front_ref.5, bf16[2048,768]{1,0:T(8,128)(2,1)} %get-tuple-element.66.high_ref, bf16[2048,768]{1,0:T(8,128)(2,1)} %get-tuple-element.67.low_ref, ...), custom_call_target="tpu_custom_call" | custom-call | flops 20000000000 | bytes 60000000 | tf_op jit(solution)/shard_map/schur/pallas_call | solution.py:831
  (54 shorter events, 0.6 us)
Async XLA Ops:
  0.0 7.7 %copy-start.15 = (s32[1,16]{1,0:T(1,128)S(1)}, s32[1,16]{1,0:T(1,128)}, u32[]{:S(2)}) copy-start(s32[1,16]{1,0:T(1,128)} %param.7) | copy-start | bytes 196
  2.5 16.1 %all-to-all-start.1 = ((f32[8,11,16,128]{3,2,1,0:T(8,128)}), f32[8,11,16,128]{3,2,1,0:T(8,128)S(1)}, u32[]{:S(2)}, u32[]{:S(2)}) async-start(f32[8,11,16,128]{3,2,1,0:T(8,128)} %cut_child.1), calls=%async_computation.1 | async-start | bytes 1441792 | tf_op jit(solution)/shard_map/all_to_all | solution.py:631
  18.6 6.2 %copy-start.7 = (f32[8,11,16,128]{3,2,1,0:T(8,128)}, f32[8,11,16,128]{3,2,1,0:T(8,128)S(1)}, u32[]{:S(2)}) copy-start(f32[8,11,16,128]{3,2,1,0:T(8,128)S(1)} %all-to-all-done.1.refs_0_) | copy-start | bytes 2162692
  18.6 48.5 %all-to-all-start.2 = ((f32[8,58,16,128]{3,2,1,0:T(8,128)}), f32[8,58,16,128]{3,2,1,0:T(8,128)}, u32[]{:S(2)}, u32[]{:S(2)}) async-start(f32[8,58,16,128]{3,2,1,0:T(8,128)} %cut_rest.1), calls=%async_computation.2 | async-start | bytes 7602176 | tf_op jit(solution)/shard_map/all_to_all | solution.py:653
  23.2 20.8 %collective-permute-start = (f32[8,11,16,128]{3,2,1,0:T(8,128)S(1)}, f32[8,11,16,128]{3,2,1,0:T(8,128)S(1)}, u32[]{:S(2)}, u32[]{:S(2)}) collective-permute-start(f32[8,11,16,128]{3,2,1,0:T(8,128)S(1)} %all-to-all-done.1.refs_0_), channel_id=1, source_target_pairs={{0,8},{8,16},{16,24},{24,0},{1,9},{9,17},{17,25},{25,1},{2,10},{10... | collective-permute-start | bytes 2162696 | tf_op jit(solution)/shard_map/ppermute | solution.py:566
  24.8 33.5 %collective-permute-start.1 = (f32[8,11,16,128]{3,2,1,0:T(8,128)S(1)}, f32[8,11,16,128]{3,2,1,0:T(8,128)S(1)}, u32[]{:S(2)}, u32[]{:S(2)}) collective-permute-start(f32[8,11,16,128]{3,2,1,0:T(8,128)S(1)} %all-to-all-done.1.refs_0_), channel_id=1, source_target_pairs={{0,24},{8,0},{16,8},{24,16},{1,25},{9,1},{17,9},{25,17},{2,26},{10... | collective-permute-start | bytes 2162696 | tf_op jit(solution)/shard_map/ppermute | solution.py:566
  44.0 26.8 %copy-start.10 = (f32[8,11,16,128]{3,2,1,0:T(8,128)}, f32[8,11,16,128]{3,2,1,0:T(8,128)S(1)}, u32[]{:S(2)}) copy-start(f32[8,11,16,128]{3,2,1,0:T(8,128)S(1)} %collective-permute-done.refs_1_) | copy-start | bytes 2162692
  58.3 12.4 %copy-start.11 = (f32[8,11,16,128]{3,2,1,0:T(8,128)}, f32[8,11,16,128]{3,2,1,0:T(8,128)S(1)}, u32[]{:S(2)}) copy-start(f32[8,11,16,128]{3,2,1,0:T(8,128)S(1)} %collective-permute-done.1.refs_2_) | copy-start | bytes 2162692
  58.4 19.5 %collective-permute-start.2 = (f32[4,11,16,128]{3,2,1,0:T(8,128)S(1)}, f32[4,11,16,128]{3,2,1,0:T(8,128)S(1)}, u32[]{:S(2)}, u32[]{:S(2)}) collective-permute-start(f32[4,11,16,128]{3,2,1,0:T(8,128)S(1)} %slice.19), channel_id=1, source_target_pairs={{0,8},{8,16},{16,24},{24,0},{1,9},{9,17},{17,25},{25,1},{2,10},{10... | collective-permute-start | bytes 1081352 | tf_op jit(solution)/shard_map/ppermute | solution.py:566
  59.6 18.3 %collective-permute-start.3 = (f32[4,11,16,128]{3,2,1,0:T(8,128)S(1)}, f32[4,11,16,128]{3,2,1,0:T(8,128)}, u32[]{:S(2)}, u32[]{:S(2)}) collective-permute-start(f32[4,11,16,128]{3,2,1,0:T(8,128)S(1)} %slice.20), channel_id=1, source_target_pairs={{0,24},{8,0},{16,8},{24,16},{1,25},{9,1},{17,9},{25,17},{2,26},{10... | collective-permute-start | bytes 1081352 | tf_op jit(solution)/shard_map/ppermute | solution.py:566
  70.8 16.4 %all-to-all-start.3 = ((f32[4,2,6,16,128]{4,3,2,1,0:T(8,128)}), f32[4,2,6,16,128]{4,3,2,1,0:T(8,128)S(1)}, u32[]{:S(2)}, u32[]{:S(2)}) async-start(f32[4,2,6,16,128]{4,3,2,1,0:T(8,128)} %get-tuple-element.51), calls=%async_computation.3 | async-start | bytes 786432 | tf_op jit(solution)/shard_map/all_to_all | solution.py:671
  76.4 1.5 copy-start.13
  77.8 19.9 %copy-start.8 = (f32[8,9,16,128]{3,2,1,0:T(8,128)}, f32[8,9,16,128]{3,2,1,0:T(8,128)S(1)}, u32[]{:S(2)}) copy-start(f32[8,9,16,128]{3,2,1,0:T(8,128)S(1)} %slice.21.refs_5_) | copy-start | bytes 1769476
  77.8 0.8 copy-start.14
  87.1 3.6 %copy-start.9 = (f32[4,2,6,16,128]{4,3,2,1,0:T(8,128)}, f32[4,2,6,16,128]{4,3,2,1,0:T(8,128)S(1)}, u32[]{:S(2)}) copy-start(f32[4,2,6,16,128]{4,3,2,1,0:T(8,128)S(1)} %all-to-all-done.3.leads_ref) | copy-start | bytes 1179652
  87.1 49.4 %all-to-all-start.4 = ((f32[8,2,8,16,128]{4,3,2,1,0:T(8,128)}), f32[8,2,8,16,128]{4,3,2,1,0:T(8,128)S(1)}, u32[]{:S(2)}, u32[]{:S(2)}) async-start(f32[8,2,8,16,128]{4,3,2,1,0:T(8,128)} %get-tuple-element.52), calls=%async_computation.4 | async-start | bytes 2097152 | tf_op jit(solution)/shard_map/all_to_all | solution.py:694
  90.7 42.5 %copy-start.3 = (f32[16,6,16,128]{3,2,1,0:T(8,128)S(1)}, f32[16,6,16,128]{3,2,1,0:T(8,128)}, u32[]{:S(2)}) copy-start(f32[16,6,16,128]{3,2,1,0:T(8,128)} %get-tuple-element.61) | copy-start | bytes 2359300
  92.5 17.6 %collective-permute-start.6 = (f32[21,16,128]{2,1,0:T(8,128)}, f32[21,16,128]{2,1,0:T(8,128)S(1)}, u32[]{:S(2)}, u32[]{:S(2)}) collective-permute-start(f32[21,16,128]{2,1,0:T(8,128)} %corner_front.1), channel_id=1, source_target_pairs={{0,6},{1,7},{2,4},{3,5},{4,2},{5,3},{6,0},{7,1},{8,14},{9,15},{10,... | collective-permute-start | bytes 516104 | tf_op jit(solution)/shard_map/ppermute | solution.py:549
  95.4 17.1 %collective-permute-start.5 = (f32[21,16,128]{2,1,0:T(8,128)}, f32[21,16,128]{2,1,0:T(8,128)S(1)}, u32[]{:S(2)}, u32[]{:S(2)}) collective-permute-start(f32[21,16,128]{2,1,0:T(8,128)} %corner_front.1), channel_id=1, source_target_pairs={{0,4},{1,5},{2,6},{3,7},{4,0},{5,1},{6,2},{7,3},{8,12},{9,13},{10,... | collective-permute-start | bytes 516104 | tf_op jit(solution)/shard_map/ppermute | solution.py:549
  95.9 16.6 %collective-permute-start.4 = (f32[21,16,128]{2,1,0:T(8,128)}, f32[21,16,128]{2,1,0:T(8,128)S(1)}, u32[]{:S(2)}, u32[]{:S(2)}) collective-permute-start(f32[21,16,128]{2,1,0:T(8,128)} %corner_front.1), channel_id=1, source_target_pairs={{0,2},{1,3},{2,0},{3,1},{4,6},{5,7},{6,4},{7,5},{8,10},{9,11},{10,... | collective-permute-start | bytes 516104 | tf_op jit(solution)/shard_map/ppermute | solution.py:549
  96.1 19.7 %collective-permute-start.8 = (f32[8,9,16,128]{3,2,1,0:T(8,128)S(1)}, f32[8,9,16,128]{3,2,1,0:T(8,128)S(1)}, u32[]{:S(2)}, u32[]{:S(2)}) collective-permute-start(f32[8,9,16,128]{3,2,1,0:T(8,128)S(1)} %slice.21.refs_5_), channel_id=1, source_target_pairs={{0,8},{8,16},{16,24},{24,0},{1,9},{9,17},{17,25},{25,1},{2,10},{10... | collective-permute-start | bytes 1769480 | tf_op jit(solution)/shard_map/ppermute | solution.py:566
  97.7 27.2 %collective-permute-start.9 = (f32[8,9,16,128]{3,2,1,0:T(8,128)S(1)}, f32[8,9,16,128]{3,2,1,0:T(8,128)}, u32[]{:S(2)}, u32[]{:S(2)}) collective-permute-start(f32[8,9,16,128]{3,2,1,0:T(8,128)S(1)} %slice.21.refs_5_), channel_id=1, source_target_pairs={{0,24},{8,0},{16,8},{24,16},{1,25},{9,1},{17,9},{25,17},{2,26},{10... | collective-permute-start | bytes 1769480 | tf_op jit(solution)/shard_map/ppermute | solution.py:566
  114.3 30.3 %collective-permute-start.7 = (f32[4,21,16,128]{3,2,1,0:T(8,128)}, f32[4,21,16,128]{3,2,1,0:T(8,128)}, u32[]{:S(2)}, u32[]{:S(2)}) collective-permute-start(f32[4,21,16,128]{3,2,1,0:T(8,128)} %pad_maximum_fusion.1.near_ref), channel_id=1, source_target_pairs={{0,1},{1,0},{2,3},{3,2},{4,5},{5,4},{6,7},{7,6},{8,9},{9,8},{10,11... | collective-permute-start | bytes 2064392 | tf_op jit(solution)/shard_map/ppermute | solution.py:549
  115.8 17.5 %copy-start.12 = (f32[8,9,16,128]{3,2,1,0:T(8,128)}, f32[8,9,16,128]{3,2,1,0:T(8,128)S(1)}, u32[]{:S(2)}) copy-start(f32[8,9,16,128]{3,2,1,0:T(8,128)S(1)} %collective-permute-done.8.refs_6_) | copy-start | bytes 1769476
  125.6 14.7 %collective-permute-start.10 = (f32[4,9,16,128]{3,2,1,0:T(8,128)}, f32[4,9,16,128]{3,2,1,0:T(8,128)}, u32[]{:S(2)}, u32[]{:S(2)}) collective-permute-start(f32[4,9,16,128]{3,2,1,0:T(8,128)} %slice.22), channel_id=1, source_target_pairs={{0,8},{8,16},{16,24},{24,0},{1,9},{9,17},{17,25},{25,1},{2,10},{10... | collective-permute-start | bytes 884744 | tf_op jit(solution)/shard_map/ppermute | solution.py:566
  128.4 14.0 %collective-permute-start.11 = (f32[4,9,16,128]{3,2,1,0:T(8,128)}, f32[4,9,16,128]{3,2,1,0:T(8,128)}, u32[]{:S(2)}, u32[]{:S(2)}) collective-permute-start(f32[4,9,16,128]{3,2,1,0:T(8,128)} %slice.23), channel_id=1, source_target_pairs={{0,24},{8,0},{16,8},{24,16},{1,25},{9,1},{17,9},{25,17},{2,26},{10... | collective-permute-start | bytes 884744 | tf_op jit(solution)/shard_map/ppermute | solution.py:566
  133.2 37.2 %collective-permute-start.12 = (f32[16,6,16,128]{3,2,1,0:T(8,128)S(1)}, f32[16,6,16,128]{3,2,1,0:T(8,128)S(1)}, u32[]{:S(2)}, u32[]{:S(2)}) collective-permute-start(f32[16,6,16,128]{3,2,1,0:T(8,128)S(1)} %copy-done.3), channel_id=1, source_target_pairs={{0,2},{1,3},{2,0},{3,1},{4,6},{5,7},{6,4},{7,5},{8,10},{9,11},{10,... | collective-permute-start | bytes 2359304 | tf_op jit(solution)/shard_map/ppermute | solution.py:549
  135.0 35.5 %collective-permute-start.13 = (f32[16,6,16,128]{3,2,1,0:T(8,128)S(1)}, f32[16,6,16,128]{3,2,1,0:T(8,128)S(1)}, u32[]{:S(2)}, u32[]{:S(2)}) collective-permute-start(f32[16,6,16,128]{3,2,1,0:T(8,128)S(1)} %copy-done.3), channel_id=1, source_target_pairs={{0,4},{1,5},{2,6},{3,7},{4,0},{5,1},{6,2},{7,3},{8,12},{9,13},{10,... | collective-permute-start | bytes 2359304 | tf_op jit(solution)/shard_map/ppermute | solution.py:549
  136.5 1.0 copy-start.2
  142.4 71.2 %collective-permute-start.16 = (f32[256,1024]{1,0:T(8,128)}, f32[256,1024]{1,0:T(8,128)}, u32[]{:S(2)}, u32[]{:S(2)}) collective-permute-start(f32[256,1024]{1,0:T(8,128)} %bitcast.39), channel_id=1, source_target_pairs={{0,8},{8,16},{16,24},{24,0},{1,9},{9,17},{17,25},{25,1},{2,10},{10... | collective-permute-start | bytes 3145736 | tf_op jit(solution)/shard_map/ppermute | solution.py:566
  142.9 71.7 %collective-permute-start.17 = (f32[256,1024]{1,0:T(8,128)}, f32[256,1024]{1,0:T(8,128)}, u32[]{:S(2)}, u32[]{:S(2)}) collective-permute-start(f32[256,1024]{1,0:T(8,128)} %bitcast.40), channel_id=1, source_target_pairs={{0,16},{8,24},{16,0},{24,8},{1,17},{9,25},{17,1},{25,9},{2,18},{10... | collective-permute-start | bytes 3145736 | tf_op jit(solution)/shard_map/ppermute | solution.py:566
  144.6 70.0 %collective-permute-start.18 = (f32[256,1024]{1,0:T(8,128)}, f32[256,1024]{1,0:T(8,128)}, u32[]{:S(2)}, u32[]{:S(2)}) collective-permute-start(f32[256,1024]{1,0:T(8,128)} %bitcast.41), channel_id=1, source_target_pairs={{0,24},{8,0},{16,8},{24,16},{1,25},{9,1},{17,9},{25,17},{2,26},{10... | collective-permute-start | bytes 3145736 | tf_op jit(solution)/shard_map/ppermute | solution.py:566
  170.5 22.0 %copy-start.4 = (f32[16,6,16,128]{3,2,1,0:T(8,128)}, f32[16,6,16,128]{3,2,1,0:T(8,128)S(1)}, u32[]{:S(2)}) copy-start(f32[16,6,16,128]{3,2,1,0:T(8,128)S(1)} %collective-permute-done.12) | copy-start | bytes 2359300
  170.5 22.0 %copy-start.5 = (f32[16,6,16,128]{3,2,1,0:T(8,128)}, f32[16,6,16,128]{3,2,1,0:T(8,128)S(1)}, u32[]{:S(2)}) copy-start(f32[16,6,16,128]{3,2,1,0:T(8,128)S(1)} %collective-permute-done.13) | copy-start | bytes 2359300
  170.5 22.0 %collective-permute-start.14 = (f32[16,6,16,128]{3,2,1,0:T(8,128)S(1)}, f32[16,6,16,128]{3,2,1,0:T(8,128)S(1)}, u32[]{:S(2)}, u32[]{:S(2)}) collective-permute-start(f32[16,6,16,128]{3,2,1,0:T(8,128)S(1)} %collective-permute-done.13), channel_id=1, source_target_pairs={{0,2},{1,3},{2,0},{3,1},{4,6},{5,7},{6,4},{7,5},{8,10},{9,11},{10,... | collective-permute-start | bytes 2359304 | tf_op jit(solution)/shard_map/ppermute | solution.py:549
  192.5 0.9 copy-start.6
  195.4 13.5 %copy-start.1 = (f32[4,16,6,16,128]{4,3,2,1,0:T(8,128)}, f32[4,16,6,16,128]{4,3,2,1,0:T(8,128)S(1)}, u32[]{:S(2)}) copy-start(f32[4,16,6,16,128]{4,3,2,1,0:T(8,128)S(1)} %pad_maximum_fusion.refs_0_) | copy-start | bytes 9437188
  195.5 29.7 %collective-permute-start.15 = (f32[4,16,6,16,128]{4,3,2,1,0:T(8,128)S(1)}, f32[4,16,6,16,128]{4,3,2,1,0:T(8,128)}, u32[]{:S(2)}, u32[]{:S(2)}) collective-permute-start(f32[4,16,6,16,128]{4,3,2,1,0:T(8,128)S(1)} %pad_maximum_fusion.refs_0_), channel_id=1, source_target_pairs={{0,1},{1,0},{2,3},{3,2},{4,5},{5,4},{6,7},{7,6},{8,9},{9,8},{10,11... | collective-permute-start | bytes 9437192 | tf_op jit(solution)/shard_map/ppermute | solution.py:549
  209.0 52.7 %all-to-all-start.5 = ((f32[8,64,16,128]{3,2,1,0:T(8,128)}), f32[8,64,16,128]{3,2,1,0:T(8,128)}, u32[]{:S(2)}, u32[]{:S(2)}) async-start(f32[8,64,16,128]{3,2,1,0:T(8,128)} %get-tuple-element.78), calls=%async_computation.5 | async-start | bytes 8388608 | tf_op jit(solution)/shard_map/all_to_all | solution.py:825
